TPU v7x, 128 devices: a whole 4x4x4 slice. The times are simulated.
128 devices in a mesh: grp: 4 (over y_lo, core), dev: 32 (over x, z, y_hi).
Axes of the slice: x: 4, y: 4 (y_hi: 2, y_lo: 2; y = y_hi * 2 + y_lo), z: 4, core: 2. Of those that a mesh axis runs over, the one named last changes fastest.
Arguments:
- entity: float32 [4, 65536, 256], P('grp', 'dev')
- entity_acc: float32 [4, 65536], P('grp', 'dev'), may hold values from 0.001 to 0.1
- relation: float32 [40, 256, 256], replicated, may hold values from -0.375 to 0.375
- relation_acc: float32 [40, 256], replicated, may hold values from 1 to 10000
- partner: int32 [4, 32], replicated, may hold values from 0 to 3
- src_row: int32 [4, 65536], P('grp', 'dev'), may hold values from 0 to 2047
- dst_owner: int32 [4, 65536, 1], P('grp', 'dev'), may hold values from 0 to 31; in each aligned block of 2048 rows (0 to 2047, 2048 to 4095, ..., all dimensions but the last counted through in order) at most 128 rows name the same one
- dst_row: int32 [4, 65536], P('grp', 'dev'), may hold values from 0 to 2047
- rel_ids: int32 [4, 64], P('grp', 'dev'), may hold values from 0 to 39
- neg_src: int32 [4, 64, 1024], P('grp', 'dev'), may hold values from 0 to 2047
- neg_dst: int32 [4, 64, 1024], P('grp', 'dev'), may hold values from 0 to 2047
- edge_count: int32 [4, 32], P('grp', 'dev'), may hold values from 1024 to 2048
Outputs:
- entity_new: float32 [4, 65536, 256], P('grp', 'dev')
- entity_acc_new: float32 [4, 65536], P('grp', 'dev')
- relation_new: float32 [40, 256, 256], replicated
- relation_acc_new: float32 [40, 256], replicated
Inputs may be any that keep to these rules, and one draw needn't show every extreme that they name: `dst_owner`: among the edges of one device at most 128 name the same shard.
All inputs are finite; a program needn't handle non-finite values.
Results may differ from a plain program's by a relative error of at most 0.0085.
The roundings to bfloat16 on the way count: a program that leaves them out, or rounds other values in their place, can miss the bound.
Values may be sent and summed in bfloat16 or wider, within the bound.
No kernel may reach another device: no remote copies, remote signals or barrier semaphores. Data moves between devices by JAX's collectives and lax.ppermute only.
A program may use at most 192 MiB of HBM per device.

v0:
```python
import jax
import jax.numpy as jnp
from jax import lax
from jax.sharding import PartitionSpec as P

step_rate = 0.1


def block_grads(src_rows, dst_rows, neg_src_rows, neg_dst_rows, operator, live):

    def loss_fn(src_rows, dst_rows, neg_src_rows, neg_dst_rows, operator):
        op_half = operator.astype(jnp.bfloat16)
        lhs_rows = jnp.dot(src_rows, op_half, preferred_element_type=jnp.float32).astype(
            jnp.bfloat16
        )
        rhs_rows = jnp.dot(dst_rows, op_half.T, preferred_element_type=jnp.float32).astype(
            jnp.bfloat16
        )
        positive = jnp.sum(lhs_rows.astype(jnp.float32) * dst_rows.astype(jnp.float32), axis=1)
        dst_scores = jnp.dot(lhs_rows, neg_dst_rows.T, preferred_element_type=jnp.float32)
        src_scores = jnp.dot(rhs_rows, neg_src_rows.T, preferred_element_type=jnp.float32)

        def softmax_loss(scores):
            highest = lax.stop_gradient(jnp.maximum(jnp.max(scores, axis=1), positive))
            totals = jnp.exp(positive - highest) + jnp.sum(
                jnp.exp(scores - highest[:, None]), axis=1
            )
            return highest + jnp.log(totals) - positive

        return jnp.sum(live * (softmax_loss(dst_scores) + softmax_loss(src_scores)))

    return jax.grad(loss_fn, argnums=(0, 1, 2, 3, 4))(
        src_rows, dst_rows, neg_src_rows, neg_dst_rows, operator
    )


def on_device(
    entity,
    entity_acc,
    relation,
    relation_acc,
    partner,
    src_row,
    dst_owner,
    dst_row,
    rel_ids,
    neg_src,
    neg_dst,
    edge_count,
):
    group_id = lax.axis_index("grp")
    place_id = lax.axis_index("dev")
    groups = lax.axis_size("grp")
    peers = lax.axis_size("dev")
    ent_rows = entity.shape[1]
    width = entity.shape[2]
    edges = src_row.shape[1]
    blocks = rel_ids.shape[1]
    block_len = edges // blocks
    capacity = max(4, 2 * edges // peers)
    own_rows = entity[0].astype(jnp.bfloat16)
    group_row = lax.dynamic_index_in_dim(partner, group_id, 0, keepdims=False)
    visit_id = lax.dynamic_index_in_dim(group_row, place_id, 0, keepdims=False)
    every_part = lax.all_gather(own_rows[None], "grp", axis=0, tiled=True)
    visiting = lax.dynamic_index_in_dim(every_part, visit_id, 0, keepdims=False)
    owners = dst_owner[0, :, 0]
    hits = (owners[:, None] == jnp.arange(peers, dtype=jnp.int32)[None, :]).astype(jnp.int32)
    order = jnp.sum(jnp.cumsum(hits, axis=0) * hits, axis=1) - 1
    slot = owners * capacity + order
    wanted = (
        jnp.zeros((peers * capacity,), jnp.int32).at[slot].set(dst_row[0]).reshape(peers, capacity)
    )
    asked = lax.all_to_all(wanted, "dev", split_axis=0, concat_axis=0, tiled=True)
    found = every_part[group_row[:, None], asked]
    fetched = lax.all_to_all(found, "dev", split_axis=0, concat_axis=0, tiled=True)
    dst_all = fetched.reshape(peers * capacity, width)[slot]
    own_grad = jnp.zeros((ent_rows, width), jnp.float32)
    visit_grad = jnp.zeros((ent_rows, width), jnp.float32)
    rel_grad = jnp.zeros(relation.shape, jnp.float32)
    dst_parts = []
    count = edge_count[0, 0]
    for block_index in range(blocks):
        start = block_index * block_len
        src_ids = src_row[0, start : start + block_len]
        neg_src_ids = neg_src[0, block_index]
        neg_dst_ids = neg_dst[0, block_index]
        rel_index = rel_ids[0, block_index]
        live = (start + jnp.arange(block_len, dtype=jnp.int32) < count).astype(jnp.float32)
        grads = block_grads(
            own_rows[src_ids],
            dst_all[start : start + block_len],
            own_rows[neg_src_ids],
            visiting[neg_dst_ids],
            relation[rel_index],
            live,
        )
        own_grad = own_grad.at[src_ids].add(grads[0].astype(jnp.float32))
        own_grad = own_grad.at[neg_src_ids].add(grads[2].astype(jnp.float32))
        visit_grad = visit_grad.at[neg_dst_ids].add(grads[3].astype(jnp.float32))
        dst_parts.append(grads[1].astype(jnp.float32))
        rel_grad = rel_grad.at[rel_index].add(grads[4])
    dst_grad = jnp.concatenate(dst_parts, axis=0)
    outgoing = (
        jnp.zeros((peers * capacity, width), jnp.float32)
        .at[slot]
        .set(dst_grad)
        .reshape(peers, capacity, width)
    )
    returned = lax.all_to_all(outgoing, "dev", split_axis=0, concat_axis=0, tiled=True)
    part_grads = jnp.zeros((groups, ent_rows, width), jnp.float32).at[visit_id].set(visit_grad)
    part_grads = part_grads.at[group_row[:, None], asked].add(returned)
    home_grad = lax.psum_scatter(part_grads, "grp", scatter_dimension=0, tiled=True)[0]
    total_grad = own_grad + home_grad
    acc_new = entity_acc[0] + jnp.mean(total_grad * total_grad, axis=1)
    entity_new = entity[0] - step_rate * total_grad / jnp.sqrt(acc_new)[:, None]
    rel_total = lax.psum(rel_grad, ("grp", "dev"))
    relation_acc_new = relation_acc + jnp.mean(rel_total * rel_total, axis=2)
    relation_new = relation - step_rate * rel_total / jnp.sqrt(relation_acc_new)[:, :, None]
    return (entity_new[None], acc_new[None], relation_new, relation_acc_new)


def solution(mesh):
    return jax.shard_map(
        on_device,
        mesh=mesh,
        in_specs=(
            P("grp", "dev", None),
            P("grp", "dev"),
            P(),
            P(),
            P(),
            P("grp", "dev"),
            P("grp", "dev", None),
            P("grp", "dev"),
            P("grp", "dev"),
            P("grp", "dev", None),
            P("grp", "dev", None),
            P("grp", "dev"),
        ),
        out_specs=(P("grp", "dev", None), P("grp", "dev"), P(), P()),
        check_vma=False,
    )
```

profile of v0, /device:TPU:1, one launch (start us, length us, event | category | flops | bytes accessed | tf_op | source)
XLA Modules:
  0.0 670.5 jit_solution(6625187518274476153)
XLA Ops:
  10.7 9.1 %reduce-window.6 = s32[32,16,128]{2,1,0:T(8,128)S(1)} reduce-window(s32[32,16,128]{2,1,0:T(8,128)S(1)} %fusion.114, s32[]{:T(128)} %constant.120.clone.1), window={size=1x1x128 pad=0_0x0_0x127_0}, to_apply=%region_1.2 | reduce-window | flops 8323072 | bytes 524292 | tf_op jit(solution)/shard_map/reduce-window
  20.7 8.8 %scatter_custom_fusion = s32[4096]{0:T(1024)} fusion(s32[2048]{0:T(1024)S(1)} %bitcast.159, s32[2048]{0:T(1024)} %bitcast.167, s32[]{:T(128)} %constant.120.clone.1), kind=kCustom, calls=%fused_computation.161 | custom fusion | bytes 16896 | tf_op jit(solution)/shard_map/scatter | solution.py:71
  29.4 11.3 %all-to-all-start = ((s32[32,1,128]{2,1,0:T(1,128)}), s32[32,1,128]{2,1,0:T(1,128)S(1)}, u32[]{:S(2)}, u32[]{:S(2)}) async-start(s32[32,1,128]{2,1,0:T(1,128)} %bitcast.20), calls=%async_computation | async-start | bytes 32768 | tf_op jit(solution)/shard_map/all_to_all | solution.py:73
  40.9 8.4 %all-to-all-done = s32[32,1,128]{2,1,0:T(1,128)S(1)} async-done(((s32[32,1,128]{2,1,0:T(1,128)}), s32[32,1,128]{2,1,0:T(1,128)S(1)}, u32[]{:S(2)}, u32[]{:S(2)}) %all-to-all-start) | async-done | bytes 16416 | tf_op jit(solution)/shard_map/all_to_all | solution.py:73
  49.4 11.8 %all-gather.2.cloned.1.call-done = bf16[4,2048,256]{2,1,0:T(8,128)(2,1)} async-done(((bf16[1,2048,256]{2,1,0:T(8,128)(2,1)}), bf16[4,2048,256]{2,1,0:T(8,128)(2,1)}) %all-gather.2.cloned.1.call-update) | async-done | bytes 4194320 | tf_op jit(solution)/shard_map/all_gather | solution.py:64
  61.2 143.9 %gather_fusion.1 = bf16[4096,256]{1,0:T(8,128)(2,1)} fusion(bf16[4,2048,256]{2,1,0:T(8,128)(2,1)} %all-gather.2.cloned.1.call-done, s32[4096]{0:T(1024)S(1)} %get-tuple-element.53), kind=kCustom, calls=%fused_computation.1 | custom fusion | bytes 4227072 | tf_op jit(solution)/shard_map/gather | solution.py:74
  205.1 35.4 %all-to-all-start.1 = ((bf16[32,128,256]{2,1,0:T(8,128)(2,1)}), bf16[32,128,256]{2,1,0:T(8,128)(2,1)S(1)}, u32[]{:S(2)}, u32[]{:S(2)}) async-start(bf16[32,128,256]{2,1,0:T(8,128)(2,1)} %bitcast.142), calls=%async_computation.1 | async-start | bytes 4194304 | tf_op jit(solution)/shard_map/all_to_all | solution.py:75
  261.0 5.0 gather_fusion
  287.2 9.5 %gather_fusion.2 = bf16[2048,256]{1,0:T(8,128)(2,1)} fusion(bf16[4096,256]{1,0:T(8,128)(2,1)S(1)} %bitcast.140, s32[2048]{0:T(1024)S(1)} %broadcast_clamp_fusion), kind=kCustom, calls=%fused_computation.2 | custom fusion | bytes 2105344 | tf_op jit(solution)/shard_map/gather | solution.py:76
  314.9 5.3 broadcast_in_dim.38
  327.3 13.2 %scatter_custom_fusion.3 = f32[4096,256]{1,0:T(8,128)} fusion(s32[2048]{0:T(1024)S(1)} %bitcast.161, f32[]{:T(128)} %constant.119.clone.1, bf16[1024,256]{1,0:T(8,128)(2,1)S(1)} %fusion.79, bf16[]{:T(256)} %constant.173, bf16[1024,256]{1,0:T(8,128)(2,1)S(1)} %fusion.78), kind=kCustom, calls=%fused_computation.48 | custom fusion | flops 2097152 | bytes 5242886 | tf_op jit(solution)/shard_map/scatter | solution.py:106
  340.5 9.5 %all-to-all-start.2 = ((f32[32,128,256]{2,1,0:T(8,128)}), f32[32,128,256]{2,1,0:T(8,128)}, u32[]{:S(2)}, u32[]{:S(2)}) async-start(f32[32,128,256]{2,1,0:T(8,128)} %bitcast.141), calls=%async_computation.2 | async-start | bytes 8388608 | tf_op jit(solution)/shard_map/all_to_all | solution.py:109
  355.0 7.0 %scatter_custom_fusion.1 = f32[2048,256]{1,0:T(8,128)S(1)} fusion(s32[1024]{0:T(1024)S(1)} %bitcast.166, f32[1024,256]{1,0:T(8,128)} %fusion.75, f32[]{:T(128)} %constant.119.clone.1), kind=kCustom, calls=%fused_computation.124 | custom fusion | flops 262144 | bytes 2097664 | tf_op jit(solution)/shard_map/scatter-add | solution.py:99
  366.1 7.3 %scatter_fusion = f32[2048,256]{1,0:T(8,128)S(1)} fusion(f32[2048,256]{1,0:T(8,128)S(1)} %scatter_custom_fusion.1, s32[1024]{0:T(1024)S(1)} %bitcast.158, f32[1024,256]{1,0:T(8,128)} %fusion.72), kind=kCustom, calls=%fused_computation.10 | custom fusion | flops 262144 | bytes 3149824 | tf_op jit(solution)/shard_map/scatter-add | solution.py:99
  379.5 33.9 %all-to-all-done.2 = f32[32,128,256]{2,1,0:T(8,128)} async-done(((f32[32,128,256]{2,1,0:T(8,128)}), f32[32,128,256]{2,1,0:T(8,128)}, u32[]{:S(2)}, u32[]{:S(2)}) %all-to-all-start.2) | async-done | bytes 4194336 | tf_op jit(solution)/shard_map/all_to_all | solution.py:109
  413.4 33.1 %scatter_fusion.5 = f32[8192,256]{1,0:T(8,128)} fusion(f32[8192,256]{1,0:T(8,128)} %bitcast.33, s32[4096]{0:T(1024)S(1)} %select_bitcast_fusion, f32[4096,256]{1,0:T(8,128)} %bitcast.40), kind=kCustom, calls=%fused_computation.16 | custom fusion | flops 1048576 | bytes 12599296
  455.3 86.1 %all-reduce.2.cloned.1.call-done = f32[40,256,256]{2,1,0:T(8,128)} async-done(((f32[40,256,256]{2,1,0:T(8,128)}), f32[40,256,256]{2,1,0:T(8,128)}) %all-reduce.2.cloned.1.call-update) | async-done | bytes 10485776 | tf_op jit(solution)/shard_map/psum | solution.py:116
  541.3 5.6 multiply_reduce_fusion
  548.3 9.4 %divide_subtract_fusion = f32[40,256,256]{2,1,0:T(8,128)} fusion(f32[40,256,256]{2,1,0:T(8,128)} %param.20, f32[40,256,256]{2,1,0:T(8,128)S(1)} %copy-done.5, f32[40,256]{1,0:T(8,128)S(1)} %get-tuple-element.44), kind=kLoop, calls=%fused_computation.17 | loop fusion | flops 7864320 | bytes 31498240 | tf_op jit(solution)/shard_map/sub | solution.py:118
  557.7 63.9 %reduce-scatter.2.cloned.1.call-done = f32[1,2048,256]{2,1,0:T(8,128)} async-done(((f32[4,2048,256]{2,1,0:T(8,128)}), f32[1,2048,256]{2,1,0:T(8,128)}) %reduce-scatter.2.cloned.1.call-update) | async-done | bytes 2097168 | tf_op jit(solution)/shard_map/reduce_scatter | solution.py:112
  621.6 9.0 %scatter_fusion.1 = f32[2048,256]{1,0:T(8,128)} fusion(f32[2048,256]{1,0:T(8,128)} %bitcast.139, s32[1024]{0:T(1024)S(1)} %bitcast.154, f32[1024,256]{1,0:T(8,128)S(1)} %fusion.64), kind=kCustom, calls=%fused_computation.12 | custom fusion | flops 262144 | bytes 3149824 | tf_op jit(solution)/shard_map/scatter-add | solution.py:97
  630.6 8.9 %scatter_fusion.2 = f32[2048,256]{1,0:T(8,128)} fusion(f32[2048,256]{1,0:T(8,128)} %scatter_fusion.1, s32[1024]{0:T(1024)S(1)} %bitcast.156, f32[1024,256]{1,0:T(8,128)S(1)} %copy-done.10), kind=kCustom, calls=%fused_computation.13 | custom fusion | flops 262144 | bytes 3149824 | tf_op jit(solution)/shard_map/scatter-add | solution.py:98
  639.5 9.2 %scatter_fusion.3 = f32[2048,256]{1,0:T(8,128)} fusion(f32[2048,256]{1,0:T(8,128)} %scatter_fusion.2, s32[1024]{0:T(1024)S(1)} %bitcast.150, f32[1024,256]{1,0:T(8,128)S(1)} %fusion.65), kind=kCustom, calls=%fused_computation.14 | custom fusion | flops 262144 | bytes 3149824 | tf_op jit(solution)/shard_map/scatter-add | solution.py:97
  648.7 9.0 %scatter_fusion.4 = f32[2048,256]{1,0:T(8,128)} fusion(f32[2048,256]{1,0:T(8,128)} %scatter_fusion.3, s32[1024]{0:T(1024)S(1)} %bitcast.152, f32[1024,256]{1,0:T(8,128)S(1)} %copy-done.9), kind=kCustom, calls=%fused_computation.15 | custom fusion | flops 262144 | bytes 3149824 | tf_op jit(solution)/shard_map/scatter-add | solution.py:98
  (153 shorter events, 95.8 us)
Async XLA Ops:
  7.2 33.6 %copy-start.27 = (s32[1,2048]{1,0:T(1,128)S(1)}, s32[1,2048]{1,0:T(1,128)}, u32[]{:S(2)}) copy-start(s32[1,2048]{1,0:T(1,128)} %param.23) | copy-start | bytes 24580
  7.2 33.7 %copy-start.28 = (s32[1,2,1024]{2,1,0:T(2,128)S(1)}, s32[1,2,1024]{2,1,0:T(2,128)}, u32[]{:S(2)}) copy-start(s32[1,2,1024]{2,1,0:T(2,128)} %param.27) | copy-start | bytes 24580
  7.2 33.7 %copy-start.33 = (s32[4,32]{1,0:T(4,128)S(1)}, s32[4,32]{1,0:T(4,128)}, u32[]{:S(2)}) copy-start(s32[4,32]{1,0:T(4,128)} %param.22) | copy-start | bytes 1540
  7.2 54.0 %all-gather.2.cloned.1.call-start = ((), (), s32[]{:S(2)}) async-start(), calls=%async_computation.4 | async-start | bytes 5242880 | tf_op jit(solution)/shard_map/all_gather | solution.py:64
  29.4 19.9 %all-to-all-start = ((s32[32,1,128]{2,1,0:T(1,128)}), s32[32,1,128]{2,1,0:T(1,128)S(1)}, u32[]{:S(2)}, u32[]{:S(2)}) async-start(s32[32,1,128]{2,1,0:T(1,128)} %bitcast.20), calls=%async_computation | async-start | bytes 32768 | tf_op jit(solution)/shard_map/all_to_all | solution.py:73
  205.1 35.4 %copy-start.30 = (s32[1,2]{1,0:T(1,128)S(1)}, s32[1,2]{1,0:T(1,128)}, u32[]{:S(2)}) copy-start(s32[1,2]{1,0:T(1,128)} %param.26) | copy-start | bytes 28
  205.1 82.1 %all-to-all-start.1 = ((bf16[32,128,256]{2,1,0:T(8,128)(2,1)}), bf16[32,128,256]{2,1,0:T(8,128)(2,1)S(1)}, u32[]{:S(2)}, u32[]{:S(2)}) async-start(bf16[32,128,256]{2,1,0:T(8,128)(2,1)} %bitcast.142), calls=%async_computation.1 | async-start | bytes 4194304 | tf_op jit(solution)/shard_map/all_to_all | solution.py:75
  240.4 300.9 %all-reduce.2.cloned.1.call-start = ((), (), s32[]{:S(2)}) async-start(), calls=%async_computation.6 | async-start | bytes 20971520 | tf_op jit(solution)/shard_map/psum | solution.py:116
  256.0 11.9 %copy-start.35 = (s32[3]{0:T(128)S(1)}, s32[3]{0:T(128)}, u32[]{:S(2)}) copy-start(s32[3]{0:T(128)} %constant.140.clone.1) | copy-start | bytes 40
  256.1 13.7 %copy-start.29 = (s32[1,2,1024]{2,1,0:T(2,128)S(1)}, s32[1,2,1024]{2,1,0:T(2,128)}, u32[]{:S(2)}) copy-start(s32[1,2,1024]{2,1,0:T(2,128)} %param.28) | copy-start | bytes 24580
  287.2 12.3 %copy-start.6 = (bf16[1024,256]{1,0:T(8,128)(2,1)S(1)}, bf16[1024,256]{1,0:T(8,128)(2,1)}, u32[]{:S(2)}) copy-start(bf16[1024,256]{1,0:T(8,128)(2,1)} %convolution_convert_fusion.7) | copy-start | bytes 1572868
  301.4 24.6 %copy-start.8 = (bf16[1024,256]{1,0:T(8,128)(2,1)}, bf16[1024,256]{1,0:T(8,128)(2,1)S(1)}, u32[]{:S(2)}) copy-start(bf16[1024,256]{1,0:T(8,128)(2,1)S(1)} %get-tuple-element.74) | copy-start | bytes 1572868
  304.0 10.0 %copy-start = (f32[1024,1024]{0,1:T(8,128)}, f32[1024,1024]{0,1:T(8,128)S(1)}, u32[]{:S(2)}) copy-start(f32[1024,1024]{0,1:T(8,128)S(1)} %get-tuple-element.76) | copy-start | bytes 12582916
  312.4 9.5 %copy-start.20 = (bf16[1024,256]{1,0:T(8,128)(2,1)}, bf16[1024,256]{1,0:T(8,128)(2,1)S(1)}, u32[]{:S(2)}) copy-start(bf16[1024,256]{1,0:T(8,128)(2,1)S(1)} %fusion.58) | copy-start | bytes 1572868
  340.5 9.6 %copy-start.34 = (s32[3]{0:T(128)S(1)}, s32[3]{0:T(128)}, u32[]{:S(2)}) copy-start(s32[3]{0:T(128)} %constant.129.clone.1) | copy-start | bytes 40
  340.5 10.3 %copy-start.32 = (s32[2]{0:T(128)S(1)}, s32[2]{0:T(128)}, u32[]{:S(2)}) copy-start(s32[2]{0:T(128)} %constant.150) | copy-start | bytes 28
  340.5 10.4 %copy-start.31 = (s32[2]{0:T(128)S(1)}, s32[2]{0:T(128)}, u32[]{:S(2)}) copy-start(s32[2]{0:T(128)} %constant.153) | copy-start | bytes 28
  340.5 72.9 %all-to-all-start.2 = ((f32[32,128,256]{2,1,0:T(8,128)}), f32[32,128,256]{2,1,0:T(8,128)}, u32[]{:S(2)}, u32[]{:S(2)}) async-start(f32[32,128,256]{2,1,0:T(8,128)} %bitcast.141), calls=%async_computation.2 | async-start | bytes 8388608 | tf_op jit(solution)/shard_map/all_to_all | solution.py:109
  350.0 271.7 %reduce-scatter.2.cloned.1.call-start = ((), (), s32[]{:S(2)}) async-start(), calls=%async_computation.5 | async-start | bytes 10485760 | tf_op jit(solution)/shard_map/reduce_scatter | solution.py:112
  455.3 91.6 %copy-start.25 = (f32[40,256]{1,0:T(8,128)S(1)}, f32[40,256]{1,0:T(8,128)}, u32[]{:S(2)}) copy-start(f32[40,256]{1,0:T(8,128)} %param.21) | copy-start | bytes 122884
  621.6 9.0 %copy-start.10 = (f32[1024,256]{1,0:T(8,128)S(1)}, f32[1024,256]{1,0:T(8,128)}, u32[]{:S(2)}) copy-start(f32[1024,256]{1,0:T(8,128)} %fusion.69) | copy-start | bytes 3145732
  639.5 9.2 %copy-start.9 = (f32[1024,256]{1,0:T(8,128)S(1)}, f32[1024,256]{1,0:T(8,128)}, u32[]{:S(2)}) copy-start(f32[1024,256]{1,0:T(8,128)} %fusion.66) | copy-start | bytes 3145732
  648.7 11.0 %copy-start.26 = (f32[1,2048]{1,0:T(1,128)S(1)}, f32[1,2048]{1,0:T(1,128)}, u32[]{:S(2)}) copy-start(f32[1,2048]{1,0:T(1,128)} %param.19) | copy-start | bytes 24580
  648.7 11.6 %copy-start.7 = (f32[1,2048,256]{2,1,0:T(8,128)S(1)}, f32[1,2048,256]{2,1,0:T(8,128)}, u32[]{:S(2)}) copy-start(f32[1,2048,256]{2,1,0:T(8,128)} %param.18) | copy-start | bytes 6291460
  (18 other events, 57.9 us)
Sparse Core Ops, SparseCore 0:
  10.8 50.3 all-gather.1
  324.7 216.5 all-reduce.1
  543.9 77.6 reduce-scatter.1
where the time goes:
time: 676 us; the launch traced here: 670 us
  local copies, waits for them, and re-layouts  212 us (31%)
  waiting for transfers between devices  204 us (30%)
  other arithmetic  137 us (20%)
  starting transfers between devices  56.3 us (8%)
  matrix products  38.9 us (6%)
  between operations  21.3 us (3%)
    gather x1, local copies, waits for them, and re-layouts, on_device(): found = every_part[group_row[:, None], asked]  144 us
    psum x1, waiting for transfers between devices, on_device(): rel_total = lax.psum(rel_grad, ('grp', 'dev'))  86.1 us
    reduce_scatter x1, waiting for transfers between devices, on_device(): lax.psum_scatter(part_grads, 'grp', scatter_dimension=0, tiled=True)[0]  63.9 us
    all_to_all x1, starting transfers between devices, on_device(): lax.all_to_all(found, 'dev', split_axis=0, concat_axis=0, tiled=True)  35.4 us
    all_to_all x1, waiting for transfers between devices, on_device(): lax.all_to_all(outgoing, 'dev', split_axis=0, concat_axis=0, tiled=True)  33.9 us
    unnamed x4, other arithmetic  33.3 us
    scatter-add x2, other arithmetic, on_device(): own_grad = own_grad.at[src_ids].add(grads[0].astype(jnp.float32))  18.2 us
    scatter-add x2, other arithmetic, on_device(): own_grad = own_grad.at[neg_src_ids].add(grads[2].astype(jnp.float32))  17.9 us
  transfers between devices with their start and end apart: 6, of which 5 were waited for; matrix products, arithmetic and copies ran while one was open for 24% of the time, Pallas kernels for 0%

commit v1 on v0

v1 whole, which is shorter than its diff:
```python
import functools

import jax
import jax.numpy as jnp
from jax import lax
from jax.experimental import pallas as pl
from jax.experimental.pallas import tpu as pltpu
from jax.sharding import PartitionSpec as P

step_rate = 0.1
VMEM_BYTES = 50 * 1024 * 1024
half = jnp.bfloat16
full = jnp.float32
VMEM = pl.BlockSpec(memory_space=pltpu.VMEM)
SMEM = pl.BlockSpec(memory_space=pltpu.SMEM)


def dot(a, b, ca, cb):
    return lax.dot_general(a, b, (((ca,), (cb,)), ((), ())), preferred_element_type=full)


def turned(row):
    pieces = [
        jnp.broadcast_to(row[:, at : at + 128], (128, 128)).T for at in range(0, row.shape[1], 128)
    ]
    return pieces[0] if len(pieces) == 1 else jnp.concatenate(pieces, axis=0)


def pick(row, width):
    spread = turned(row.astype(full))
    lane = lax.broadcasted_iota(jnp.int32, (1, 128), 1).astype(full)
    pieces = [
        jnp.where(spread == lane + float(at), 1.0, 0.0).astype(half) for at in range(0, width, 128)
    ]
    return jnp.concatenate(pieces, axis=1)


def place(row, first, height):
    line = lax.broadcasted_iota(jnp.int32, (height, 1), 0) + first
    return jnp.where(row == line, 1.0, 0.0).astype(half)


def call(body, outs, scratch=(), specs=None, cost=None, **kw):
    return pl.pallas_call(
        body,
        out_shape=outs,
        in_specs=specs,
        out_specs=jax.tree.map(lambda _: VMEM, outs),
        scratch_shapes=list(scratch),
        compiler_params=pltpu.CompilerParams(vmem_limit_bytes=VMEM_BYTES),
        cost_estimate=cost,
        **kw,
    )


def cost(flops, moved):
    return pl.CostEstimate(flops=int(flops), bytes_accessed=int(moved), transcendentals=0)


def slots_body(owner_ref, row_ref, slot_ref, wanted_ref):
    peers, room = wanted_ref.shape
    edges = owner_ref.shape[1]
    step = 256
    before = lax.broadcasted_iota(jnp.int32, (step, step), 0)
    after = lax.broadcasted_iota(jnp.int32, (step, step), 1)
    upper = jnp.where(before <= after, 1.0, 0.0).astype(half)
    peer = lax.broadcasted_iota(jnp.int32, (peers, step), 0)
    carry = jnp.zeros((peers, 1), full)
    high = jnp.zeros((peers, room), full)
    low = jnp.zeros((peers, room), full)
    for at in range(0, edges, step):
        owner = owner_ref[:, at : at + step]
        hit = jnp.where(peer == owner, 1.0, 0.0)
        count = dot(hit.astype(half), upper, 1, 0) + carry
        carry = count[:, step - 1 :]
        order = (jnp.sum(count * hit, axis=0, keepdims=True) - 1.0).astype(jnp.int32)
        slot_ref[:, at : at + step] = owner * room + order
        spot = place(order, 0, room)
        row = row_ref[:, at : at + step]
        top = lax.shift_right_logical(row, 4)
        high += dot((hit * top.astype(full)).astype(half), spot, 1, 1)
        low += dot((hit * (row - top * 16).astype(full)).astype(half), spot, 1, 1)
    wanted_ref[...] = (high * 16.0 + low).astype(jnp.int32)


def list_peers(partner_ref, group_ref, list_ref, count_ref):
    peers = partner_ref.shape[1]
    me = group_ref[0]
    for part in range(4):
        count_ref[part] = 0

    def add(peer, carry):
        part = partner_ref[me, peer] ^ me
        at = count_ref[part]
        list_ref[part, at] = peer
        count_ref[part] = at + 1
        return carry

    lax.fori_loop(0, peers, add, 0)


def answer_body(partner_ref, group_ref, asked_ref, *refs):
    tables, (found_ref, list_ref, count_ref) = refs[:4], refs[4:]
    rows, width = tables[0].shape
    room = asked_ref.shape[1]
    list_peers(partner_ref, group_ref, list_ref, count_ref)
    for part in range(4):
        count = count_ref[part]

        def pair(t, carry, part=part, count=count):
            one = list_ref[part, 2 * t]
            two = list_ref[part, jnp.minimum(2 * t + 1, count - 1)]
            ask = jnp.concatenate([asked_ref[pl.ds(one, 1), :], asked_ref[pl.ds(two, 1), :]], axis=1)
            got = dot(pick(ask, rows), tables[part][...], 1, 0).astype(half)
            found_ref[pl.ds(one, 1)] = got[:room].reshape(1, room, width)
            found_ref[pl.ds(two, 1)] = got[room:].reshape(1, room, width)
            return carry

        lax.fori_loop(0, (count + 1) // 2, pair, 0)


def rows_body(visit_ref, src_ref, neg_src_ref, neg_dst_ref, *refs):
    tables, (src_out, neg_src_out, neg_dst_out, visit) = refs[:4], refs[4:]
    rows = tables[0].shape[0]
    for part in range(4):

        @pl.when(visit_ref[0] == part)
        def _(part=part):
            visit[...] = tables[part][...]

    step = 256
    blocks, negs = neg_src_ref.shape
    for at in range(0, src_ref.shape[1], step):
        src_out[at : at + step] = dot(
            pick(src_ref[:, at : at + step], rows), tables[0][...], 1, 0
        ).astype(half)
    for block in range(blocks):
        for at in range(0, negs, step):
            to = block * negs + at
            neg_src_out[to : to + step] = dot(
                pick(neg_src_ref[block : block + 1, at : at + step], rows), tables[0][...], 1, 0
            ).astype(half)
            neg_dst_out[to : to + step] = dot(
                pick(neg_dst_ref[block : block + 1, at : at + step], rows), visit[...], 1, 0
            ).astype(half)


def model_body(
    rel_ref,
    count_ref,
    slot_ref,
    fetched_ref,
    src_ref,
    neg_src_ref,
    neg_dst_ref,
    relation_ref,
    outgoing_ref,
    d_src_ref,
    d_neg_src_ref,
    d_neg_dst_ref,
    d_dst,
    operator,
    op_half,
    neg_dst_sum,
    neg_src_sum,
    op_sum,
    op_turned_sum,
    op_sem,
):
    slots, width = fetched_ref.shape
    edges = src_ref.shape[0]
    blocks = rel_ref.shape[1]
    block_len = edges // blocks
    negs = neg_src_ref.shape[0] // blocks
    peers, room, _ = outgoing_ref.shape
    extra = width // peers
    places = slots // peers
    step = 256
    copies = []
    for block in range(blocks):
        copies.append(
            pltpu.make_async_copy(
                relation_ref.at[rel_ref[0, block]], operator.at[block], op_sem.at[block]
            )
        )
        copies[-1].start()
    for block in range(blocks):
        copies[block].wait()
        op_half[...] = operator[block].astype(half)
        neg_dst_sum[...] = jnp.zeros_like(neg_dst_sum)
        neg_src_sum[...] = jnp.zeros_like(neg_src_sum)
        op_sum[...] = jnp.zeros_like(op_sum)
        op_turned_sum[...] = jnp.zeros_like(op_turned_sum)

        def chunk(t, carry, block=block):
            at = pl.multiple_of(block * block_len + t * step, step)
            here = pl.ds(at, step)
            op = op_half[...]
            dst = dot(pick(slot_ref[:, here], slots), fetched_ref[...], 1, 0).astype(half)
            src = src_ref[here, :]
            negs_at = pl.ds(block * negs, negs)
            neg_dst = neg_dst_ref[negs_at, :]
            neg_src = neg_src_ref[negs_at, :]
            line = lax.broadcasted_iota(jnp.int32, (step, 1), 0) + at
            live = jnp.where(line < count_ref[0, 0], 1.0, 0.0)
            lhs = dot(src, op, 1, 0).astype(half)
            rhs = dot(dst, op, 1, 1).astype(half)
            positive = jnp.sum(lhs.astype(full) * dst.astype(full), axis=1, keepdims=True)

            def softmax(scores):
                highest = jnp.maximum(jnp.max(scores, axis=1, keepdims=True), positive)
                terms = jnp.exp(scores - highest)
                own = jnp.exp(positive - highest)
                scale = live / (own + jnp.sum(terms, axis=1, keepdims=True))
                return (terms * scale).astype(half), own * scale - live

            dst_terms, dst_own = softmax(dot(lhs, neg_dst, 1, 1))
            src_terms, src_own = softmax(dot(rhs, neg_src, 1, 1))
            d_positive = dst_own + src_own
            d_lhs = dot(dst_terms, neg_dst, 1, 0).astype(half)
            d_lhs = d_lhs + (d_positive * dst.astype(full)).astype(half)
            d_rhs = dot(src_terms, neg_src, 1, 0).astype(half)
            neg_dst_sum[...] += dot(lhs, dst_terms, 0, 0)
            neg_src_sum[...] += dot(rhs, src_terms, 0, 0)
            d_src_ref[here, :] = dot(d_lhs, op, 1, 1).astype(half)
            op_sum[...] += dot(src, d_lhs, 0, 0)
            op_turned_sum[...] += dot(d_rhs, dst, 0, 0)
            d_dst[here, :] = dot(d_rhs, op, 1, 0).astype(half) + (
                d_positive * lhs.astype(full)
            ).astype(half)
            return carry

        lax.fori_loop(0, block_len // step, chunk, 0)
        d_neg_dst_ref[block * negs : (block + 1) * negs, :] = neg_dst_sum[...].T.astype(half)
        d_neg_src_ref[block * negs : (block + 1) * negs, :] = neg_src_sum[...].T.astype(half)
        d_op = op_sum[...].astype(half) + op_turned_sum[...].astype(half)
        outgoing_ref[:, places + block * extra : places + (block + 1) * extra, :] = d_op.reshape(
            peers, extra, width
        )

    def send(t, carry):
        spot = place(slot_ref[...], t * 2 * places, 2 * places)
        out = dot(spot, d_dst[...], 1, 0).astype(half)
        outgoing_ref[pl.ds(2 * t, 2), :places, :] = out.reshape(2, places, width)
        return carry

    lax.fori_loop(0, peers // 2, send, 0)


def sums_body(src_ref, neg_src_ref, neg_dst_ref, d_src, d_neg_src, d_neg_dst, own_ref, visit_ref):
    rows = own_ref.shape[0]
    blocks, negs = neg_src_ref.shape
    step = 256

    def part(t, carry):
        first = pl.multiple_of(t * step, step)
        own = dot(place(src_ref[...], first, step), d_src[...], 1, 0)
        visit = jnp.zeros_like(own)
        for block in range(blocks):
            at = slice(block * negs, (block + 1) * negs)
            one = slice(block, block + 1)
            own += dot(place(neg_src_ref[one, :], first, step), d_neg_src[at, :], 1, 0)
            visit += dot(place(neg_dst_ref[one, :], first, step), d_neg_dst[at, :], 1, 0)
        own_ref[pl.ds(first, step), :] = own
        visit_ref[pl.ds(first, step), :] = visit
        return carry

    lax.fori_loop(0, rows // step, part, 0)


def home_body(partner_ref, group_ref, visit_to_ref, asked_ref, returned_ref, visit_ref, *refs):
    outs, (total, list_ref, count_ref) = refs[:4], refs[4:]
    rows, width = visit_ref.shape
    places = asked_ref.shape[1]
    list_peers(partner_ref, group_ref, list_ref, count_ref)
    total[...] = jnp.zeros_like(total)
    total[pl.ds(visit_to_ref[0], 1)] = visit_ref[...].reshape(1, rows, width)
    for part in range(4):
        count = count_ref[part]

        def pair(t, carry, part=part, count=count):
            one = list_ref[part, 2 * t]
            two = list_ref[part, jnp.minimum(2 * t + 1, count - 1)]
            ask_two = jnp.where(2 * t + 1 < count, asked_ref[pl.ds(two, 1), :], -1)
            ask = jnp.concatenate([asked_ref[pl.ds(one, 1), :], ask_two], axis=1)
            back = jnp.concatenate(
                [
                    returned_ref[pl.ds(one, 1), :places, :].reshape(places, width),
                    returned_ref[pl.ds(two, 1), :places, :].reshape(places, width),
                ],
                axis=0,
            )
            for first in range(0, rows, 512):
                total[part, first : first + 512] += dot(place(ask, first, 512), back, 1, 0)
            return carry

        lax.fori_loop(0, (count + 1) // 2, pair, 0)
        outs[part][...] = total[part].astype(half)


def operators_body(ids_ref, part_ref, out_ref, total):
    peers, _, width = part_ref.shape
    blocks = ids_ref.shape[1]
    rows = total.shape[1]
    total[...] = jnp.zeros_like(total)

    def add(peer, carry):
        piece = part_ref[pl.ds(peer, 1)].reshape(blocks * rows, width).astype(full)
        for block in range(blocks):
            at = ids_ref[peer, block]
            total[pl.ds(at, 1)] += piece[block * rows : (block + 1) * rows].reshape(1, rows, width)
        return carry

    lax.fori_loop(0, peers, add, 0)
    out_ref[...] = total[...].astype(half)


def on_device(
    entity,
    entity_acc,
    relation,
    relation_acc,
    partner,
    src_row,
    dst_owner,
    dst_row,
    rel_ids,
    neg_src,
    neg_dst,
    edge_count,
):
    me = lax.axis_index("grp")
    place_id = lax.axis_index("dev")
    peers = lax.axis_size("dev")
    rows, width = entity.shape[1:]
    edges = src_row.shape[1]
    blocks = rel_ids.shape[1]
    negs = neg_src.shape[2]
    relations = relation.shape[0]
    room = 2 * edges // peers
    extra = width // peers
    sds = jax.ShapeDtypeStruct

    def neighbour(x, flip):
        return lax.ppermute(x, "grp", [(g, g ^ flip) for g in range(4)])

    group = me.reshape(1)
    visit_to = (partner[me, place_id] ^ me).reshape(1)
    owners = dst_owner.reshape(1, edges)
    neg_src = neg_src.reshape(blocks, negs)
    neg_dst = neg_dst.reshape(blocks, negs)

    own = entity[0].astype(half)
    cross = neighbour(own, 2)
    sibling = neighbour(own, 1)
    group_ids = lax.all_gather(rel_ids[0], "dev", axis=0)
    slot, wanted = call(
        slots_body, (sds((1, edges), jnp.int32), sds((peers, room), jnp.int32)), specs=[VMEM] * 2
    )(owners, dst_row)
    asked = lax.all_to_all(wanted, "dev", split_axis=0, concat_axis=0, tiled=True)
    cross_sibling = neighbour(cross, 1)
    tables = (own, sibling, cross, cross_sibling)

    lists = [pltpu.SMEM((4, peers), jnp.int32), pltpu.SMEM((4,), jnp.int32)]
    found = call(
        answer_body,
        sds((peers, room, width), half),
        lists,
        [SMEM] * 2 + [VMEM] * 5,
    )(partner, group, asked, *tables)
    fetched = lax.all_to_all(found, "dev", split_axis=0, concat_axis=0, tiled=True)

    src_rows, neg_src_rows, neg_dst_rows = call(
        rows_body,
        (sds((edges, width), half), sds((blocks * negs, width), half), sds((blocks * negs, width), half)),
        [pltpu.VMEM((rows, width), half)],
        [SMEM] + [VMEM] * 7,
        cost(2 * 3 * edges * rows * width, 6 * rows * width * 2),
    )(visit_to, src_row, neg_src, neg_dst, *tables)

    outgoing, d_src, d_neg_src, d_neg_dst = call(
        model_body,
        (
            sds((peers, room + blocks * extra, width), half),
            sds((edges, width), half),
            sds((blocks * negs, width), half),
            sds((blocks * negs, width), half),
        ),
        [
            pltpu.VMEM((edges, width), half),
            pltpu.VMEM((blocks, width, width), full),
            pltpu.VMEM((width, width), half),
            pltpu.VMEM((width, negs), full),
            pltpu.VMEM((width, negs), full),
            pltpu.VMEM((width, width), full),
            pltpu.VMEM((width, width), full),
            pltpu.SemaphoreType.DMA((blocks,)),
        ],
        [SMEM] * 2 + [VMEM] * 5 + [pl.BlockSpec(memory_space=pl.ANY)],
    )(
        rel_ids,
        edge_count,
        slot,
        fetched.reshape(peers * room, width),
        src_rows,
        neg_src_rows,
        neg_dst_rows,
        relation,
    )
    returned = lax.all_to_all(outgoing, "dev", split_axis=0, concat_axis=0, tiled=True)

    own_grad, visit_grad = call(
        sums_body,
        (sds((rows, width), full), sds((rows, width), full)),
        (),
        [VMEM] * 6,
        cost(2 * 3 * edges * rows * width, 7 * rows * width * 2),
    )(src_row, neg_src, neg_dst, d_src, d_neg_src, d_neg_dst)

    rel_part = call(
        operators_body,
        sds((relations, extra, width), half),
        [pltpu.VMEM((relations, extra, width), full)],
        [SMEM, VMEM],
    )(group_ids, returned[:, room:, :])
    core = me & 1
    halves = rel_part.reshape(2, relations // 2, extra, width)
    mine = lax.dynamic_index_in_dim(halves, core, 0, keepdims=False)
    other = lax.dynamic_index_in_dim(halves, 1 - core, 0, keepdims=False)
    chip = (mine.astype(full) + neighbour(other, 1).astype(full)).astype(half)
    pair = (chip.astype(full) + neighbour(chip, 2).astype(full)).astype(half)
    gathered = lax.all_gather(pair, "dev", axis=0)

    home, home_sibling, home_cross, home_cross_sibling = call(
        home_body,
        tuple(sds((rows, width), half) for _ in range(4)),
        [pltpu.VMEM((4, rows, width), full)] + lists,
        [SMEM] * 3 + [VMEM] * 3,
    )(partner, group, visit_to, asked, returned, visit_grad)
    chip_cross = (home_cross.astype(full) + neighbour(home_cross_sibling, 1).astype(full)).astype(half)
    from_cross = neighbour(chip_cross, 2)
    from_sibling = neighbour(home_sibling, 1)
    total_grad = (
        own_grad + home.astype(full) + from_sibling.astype(full) + from_cross.astype(full)
    )
    acc_new = entity_acc[0] + jnp.mean(total_grad * total_grad, axis=1)
    entity_new = entity[0] - step_rate * total_grad / jnp.sqrt(acc_new)[:, None]

    other_half = neighbour(gathered, 1)
    both = jnp.where(core == 0, jnp.stack([gathered, other_half]), jnp.stack([other_half, gathered]))
    rel_total = both.transpose(0, 2, 1, 3, 4).reshape(relations, width, width).astype(full)
    relation_acc_new = relation_acc + jnp.mean(rel_total * rel_total, axis=2)
    relation_new = relation - step_rate * rel_total / jnp.sqrt(relation_acc_new)[:, :, None]
    return (entity_new[None], acc_new[None], relation_new, relation_acc_new)


def solution(mesh):
    return jax.shard_map(
        on_device,
        mesh=mesh,
        in_specs=(
            P("grp", "dev", None),
            P("grp", "dev"),
            P(),
            P(),
            P(),
            P("grp", "dev"),
            P("grp", "dev", None),
            P("grp", "dev"),
            P("grp", "dev"),
            P("grp", "dev", None),
            P("grp", "dev", None),
            P("grp", "dev"),
        ),
        out_specs=(P("grp", "dev", None), P("grp", "dev"), P(), P()),
        check_vma=False,
    )
```

time: 676 us -> 408 us (0.60)
  local copies, waits for them, and re-layouts: 212 us -> 11.6 us
  other arithmetic: 137 us -> 34.3 us
  blocking collectives: 0 us -> 97.5 us
  waiting for transfers between devices: 204 us -> 114 us
  Pallas kernels: 0 us -> 83.2 us
  matrix products: 38.9 us -> 0 us
    gather x8 -> x0, local copies, waits for them, and re-layouts: 183 us -> none  [the longest x1 144 us: on_device(): found = every_part[group_row[:, None], asked]]
    all_gather x0 -> x1, blocking collectives: none -> 97.5 us  [on_device(): group_ids = lax.all_gather(rel_ids[0], 'dev', axis=0)]
    psum x1 -> x0, waiting for transfers between devices: 86.1 us -> none  [on_device(): rel_total = lax.psum(rel_grad, ('grp', 'dev'))]
    pallas_call x0 -> x7, Pallas kernels: none -> 83.2 us  [the longest x1 36.6 us: on_device(): call(model_body, (sds((peers, room + blocks * extra, width), half), sds((...]
    reduce_scatter x1 -> x0, waiting for transfers between devices: 63.9 us -> none  [on_device(): lax.psum_scatter(part_grads, 'grp', scatter_dimension=0, tiled=True)[0]]
    scatter-add x6 -> x0, other arithmetic: 50.4 us -> none  [the longest x2 18.2 us: on_device(): own_grad = own_grad.at[src_ids].add(grads[0].astype(jnp.float32))]
    ppermute x0 -> x9, waiting for transfers between devices: none -> 49.6 us  [neighbour(): return lax.ppermute(x, 'grp', [(g, g ^ flip) for g in range(4)])]
    dot_general x24 -> x0, matrix products: 38.9 us -> none  [the longest x6 14.5 us: loss_fn(): jnp.dot(lhs_rows, neg_dst_rows.T, preferred_element_type=jnp.float32)]
  transfers between devices with their start and end apart: 6 -> 13, of which waited for: 5 -> 7; matrix products, arithmetic and copies ran while one was open for 24% -> 3% of each run, Pallas kernels for 0% -> 8%
where the time goes in v1:
time: 408 us; the launch traced here: 407 us
  waiting for transfers between devices  114 us (28%)
  blocking collectives  97.5 us (24%)
  Pallas kernels  83.2 us (20%)
  starting transfers between devices  50.6 us (12%)
  other arithmetic  34.3 us (8%)
  between operations  15.6 us (4%)
  local copies, waits for them, and re-layouts  11.6 us (3%)
    all_gather x1, blocking collectives, on_device(): group_ids = lax.all_gather(rel_ids[0], 'dev', axis=0)  97.5 us
    ppermute x9, waiting for transfers between devices, neighbour(): return lax.ppermute(x, 'grp', [(g, g ^ flip) for g in range(4)])  49.6 us
    all_gather x1, waiting for transfers between devices, on_device(): gathered = lax.all_gather(pair, 'dev', axis=0)  42.1 us
    pallas_call x1, Pallas kernels, on_device(): call(model_body, (sds((peers, room + blocks * extra, width), half), sds((...  36.6 us
    ppermute x9, starting transfers between devices, neighbour(): return lax.ppermute(x, 'grp', [(g, g ^ flip) for g in range(4)])  26.2 us
    all_to_all x1, waiting for transfers between devices, on_device(): lax.all_to_all(found, 'dev', split_axis=0, concat_axis=0, tiled=True)  13.9 us
    pallas_call x1, Pallas kernels, on_device(): call(home_body, tuple((sds((rows, width), half) for _ in range(4))), [plt...  12.6 us
    pallas_call x1, Pallas kernels, on_device(): call(answer_body, sds((peers, room, width), half), lists, [SMEM] * 2 + [V...  11.8 us
  transfers between devices with their start and end apart: 13, of which 7 were waited for; matrix products, arithmetic and copies ran while one was open for 3% of the time, Pallas kernels for 8%

profile of v1, /device:TPU:1, one launch (start us, length us, event | category | flops | bytes accessed | tf_op | source)
XLA Modules:
  0.0 407.0 jit_solution(5198314530304697911)
XLA Ops:
  12.1 21.5 %collective-permute-done.1.refs_2_ = bf16[2048,256]{1,0:T(8,128)(2,1)S(1)} collective-permute-done((bf16[2048,256]{1,0:T(8,128)(2,1)S(1)}, bf16[2048,256]{1,0:T(8,128)(2,1)S(1)}, u32[]{:S(2)}, u32[]{:S(2)}) %collective-permute-start.1) | collective-permute-done | bytes 1048608 | tf_op jit(solution)/shard_map/ppermute | solution.py:345
  35.2 2.3 shard_map.147
  37.5 10.7 %all-to-all-start = ((s32[32,1,128]{2,1,0:T(1,128)}), s32[32,1,128]{2,1,0:T(1,128)S(1)}, u32[]{:S(2)}, u32[]{:S(2)}) async-start(s32[32,1,128]{2,1,0:T(1,128)} %bitcast.6), calls=%async_computation | async-start | bytes 32768 | tf_op jit(solution)/shard_map/all_to_all | solution.py:360
  48.2 8.5 %all-to-all-done = s32[32,1,128]{2,1,0:T(1,128)S(1)} async-done(((s32[32,1,128]{2,1,0:T(1,128)}), s32[32,1,128]{2,1,0:T(1,128)S(1)}, u32[]{:S(2)}, u32[]{:S(2)}) %all-to-all-start) | async-done | bytes 16416 | tf_op jit(solution)/shard_map/all_to_all | solution.py:360
  56.7 11.8 %shard_map.148 = bf16[32,128,256]{2,1,0:T(8,128)(2,1)} custom-call(s32[4,32]{1,0:T(4,128)S(1)} %copy-done.6, s32[1]{0:T(128)} %bitcast.4.group_ref, s32[32,128]{1,0:T(8,128)S(1)} %bitcast.40, bf16[2048,256]{1,0:T(8,128)(2,1)S(1)} %bitcast_convert_fusion.refs_0_, bf16[2048,256]{1,0:T(8,128)(2,1)S(1)} %collective-permute-done.refs_1_, ...), custom_call_target="tpu_custom_call" | custom-call | tf_op jit(solution)/shard_map/pallas_call | solution.py:365
  68.6 4.9 %all-to-all-start.1 = ((bf16[32,128,256]{2,1,0:T(8,128)(2,1)}), bf16[32,128,256]{2,1,0:T(8,128)(2,1)}, u32[]{:S(2)}, u32[]{:S(2)}) async-start(bf16[32,128,256]{2,1,0:T(8,128)(2,1)} %shard_map.148), calls=%async_computation.1 | async-start | bytes 4194304 | tf_op jit(solution)/shard_map/all_to_all | solution.py:371
  75.4 9.0 %shard_map.149 = (bf16[2048,256]{1,0:T(8,128)(2,1)S(1)}, bf16[2048,256]{1,0:T(8,128)(2,1)S(1)}, bf16[2048,256]{1,0:T(8,128)(2,1)S(1)}) custom-call(s32[1]{0:T(128)} %bitcast.10.visit_ref.visit_to_ref, s32[1,2048]{1,0:T(1,128)S(1)} %copy-done.12, s32[2,1024]{1,0:T(2,128)S(1)} %bitcast.45, s32[2,1024]{1,0:T(2,128)S(1)} %bitcast.47, bf16[2048,256]{1,0:T(8,128)(2,1)} %copy-done, ...), custom_call_target="tpu_custom_call" | custom-call | flops 6442450944 | bytes 6291456 | tf_op jit(solution)/shard_map/pallas_call | solution.py:373
  87.4 13.9 %all-to-all-done.1 = bf16[32,128,256]{2,1,0:T(8,128)(2,1)} async-done(((bf16[32,128,256]{2,1,0:T(8,128)(2,1)}), bf16[32,128,256]{2,1,0:T(8,128)(2,1)}, u32[]{:S(2)}, u32[]{:S(2)}) %all-to-all-start.1) | async-done | bytes 2097184 | tf_op jit(solution)/shard_map/all_to_all | solution.py:371
  101.3 36.6 %shard_map.150 = (bf16[32,144,256]{2,1,0:T(8,128)(2,1)}, bf16[2048,256]{1,0:T(8,128)(2,1)S(1)}, bf16[2048,256]{1,0:T(8,128)(2,1)S(1)}, bf16[2048,256]{1,0:T(8,128)(2,1)S(1)}) custom-call(s32[1,2]{1,0:T(1,128)S(1)} %copy-done.9, s32[1,1]{1,0:T(1,128)S(6)} %copy.43.count_ref, s32[1,2048]{1,0:T(1,128)S(1)} %get-tuple-element.19.slot_ref, ...), custom_call_target="tpu_custom_call" | custom-call | tf_op jit(solution)/shard_map/pallas_call | solution.py:381
  138.9 8.8 %all-to-all-start.2 = ((bf16[32,144,256]{2,1,0:T(8,128)(2,1)}), bf16[32,144,256]{2,1,0:T(8,128)(2,1)}, u32[]{:S(2)}, u32[]{:S(2)}) async-start(bf16[32,144,256]{2,1,0:T(8,128)(2,1)} %get-tuple-element.28), calls=%async_computation.2 | async-start | bytes 4718592 | tf_op jit(solution)/shard_map/all_to_all | solution.py:410
  147.8 97.5 %all-gather.1 = s32[32,1,2]{2,1,0:T(1,128)S(1)} all-gather(s32[1,1,2]{2,1,0:T(1,128)S(1)} %bitcast.44), channel_id=1, replica_groups=mesh['grp'=4,'dev'=32] {'dev'}, dimensions={0}, use_global_device_ids=true | all-gather | bytes 264 | tf_op jit(solution)/shard_map/all_gather | solution.py:356
  247.5 16.1 %collective-permute-start.6 = (bf16[20,8,256]{2,1,0:T(8,128)(2,1)S(1)}, bf16[20,8,256]{2,1,0:T(8,128)(2,1)S(1)}, u32[]{:S(2)}, u32[]{:S(2)}) collective-permute-start(bf16[20,8,256]{2,1,0:T(8,128)(2,1)S(1)} %dynamic-slice_bitcast_fusion), channel_id=1, source_target_pairs={{0,32},{32,0},{64,96},{96,64},{1,33},{33,1},{65,97},{97,65},{2,34}... | collective-permute-start | bytes 245768 | tf_op jit(solution)/shard_map/ppermute | solution.py:345
  266.4 2.5 collective-permute-done.7
  270.9 9.9 %shard_map.151 = (f32[2048,256]{1,0:T(8,128)}, f32[2048,256]{1,0:T(8,128)}) custom-call(s32[1,2048]{1,0:T(1,128)S(1)} %copy-done.12, s32[2,1024]{1,0:T(2,128)S(1)} %bitcast.46, s32[2,1024]{1,0:T(2,128)S(1)} %bitcast.48, bf16[2048,256]{1,0:T(8,128)(2,1)S(1)} %get-tuple-element.24.d_src, bf16[2048,256]{1,0:T(8,128)(2,1)S(1)} %get-tuple-element.25.d_neg_src, ...), custom_call_target="tpu_custom_call" | custom-call | flops 6442450944 | bytes 7340032 | tf_op jit(solution)/shard_map/pallas_call | solution.py:412
  280.7 12.6 %shard_map.152 = (bf16[2048,256]{1,0:T(8,128)(2,1)S(1)}, bf16[2048,256]{1,0:T(8,128)(2,1)S(1)}, bf16[2048,256]{1,0:T(8,128)(2,1)S(1)}, bf16[2048,256]{1,0:T(8,128)(2,1)}) custom-call(s32[4,32]{1,0:T(4,128)S(1)} %copy-done.6, s32[1]{0:T(128)} %bitcast.4.group_ref, s32[1]{0:T(128)} %bitcast.10.visit_ref.visit_to_ref, s32[32,128]{1,0:T(8,128)S(1)} %bitcast.41, ...), custom_call_target="tpu_custom_call" | custom-call | tf_op jit(solution)/shard_map/pallas_call | solution.py:434
  294.1 42.1 %all-gather.4.cloned.1.call-done = bf16[640,8,256]{2,1,0:T(8,128)(2,1)} async-done(((bf16[20,8,256]{2,1,0:T(8,128)(2,1)}), bf16[640,8,256]{2,1,0:T(8,128)(2,1)}) %all-gather.4.cloned.1.call-update) | async-done | bytes 2621456 | tf_op jit(solution)/shard_map/all_gather | solution.py:432
  336.3 3.5 copy.32
  339.8 2.2 collective-permute-start.8
  342.0 2.5 add_convert_fusion
  344.9 24.6 %collective-permute-done.5 = bf16[2048,256]{1,0:T(8,128)(2,1)S(1)} collective-permute-done((bf16[2048,256]{1,0:T(8,128)(2,1)}, bf16[2048,256]{1,0:T(8,128)(2,1)S(1)}, u32[]{:S(2)}, u32[]{:S(2)}) %collective-permute-start.5) | collective-permute-done | bytes 1048608 | tf_op jit(solution)/shard_map/ppermute | solution.py:345
  369.5 2.8 multiply_reduce_fusion
  372.9 3.5 fusion.1
  376.4 10.8 %fusion = (f32[2,32,20,8]{3,1,2,0:T(8,128)S(1)}, f32[2,32,20,8,256]{4,3,1,2,0:T(8,128)}) fusion(bf16[1,32,20,8,256]{4,3,1,2,0:T(8,128)(2,1)} %bitcast.21, pred[]{:T(512)S(6)} %eq.3, bf16[1,32,20,8,256]{4,3,2,1,0:T(8,128)(2,1)S(1)} %bitcast.51), kind=kLoop, calls=%fused_computation.2 | loop fusion | flops 34068480 | bytes 15769601 | tf_op jit(solution)/shard_map/reduce_sum | solution.py:452
  388.5 11.7 %divide_subtract_fusion = f32[40,256,256]{2,1,0:T(8,128)} fusion(f32[40,256,256]{2,1,0:T(8,128)} %relation_ref.1, f32[40,256,256]{2,1,0:T(8,128)} %bitcast.49, f32[40,256]{1,0:T(8,128)S(1)} %copy.37), kind=kLoop, calls=%fused_computation.3 | loop fusion | flops 5242880 | bytes 31498240 | tf_op jit(solution)/shard_map/sub | solution.py:453
  (72 shorter events, 21.2 us)
Async XLA Ops:
  7.2 28.1 %copy-start.8 = (s32[1,2048]{1,0:T(1,128)S(1)}, s32[1,2048]{1,0:T(1,128)}, u32[]{:S(2)}) copy-start(s32[1,2048]{1,0:T(1,128)} %row_ref.1) | copy-start | bytes 24580
  7.2 28.1 %copy-start.7 = (s32[1,2048,1]{1,2,0:T(1,128)S(1)}, s32[1,2048,1]{1,2,0:T(1,128)}, u32[]{:S(2)}) copy-start(s32[1,2048,1]{1,2,0:T(1,128)} %param.18) | copy-start | bytes 24580
  7.2 49.6 %copy-start.6 = (s32[4,32]{1,0:T(4,128)S(1)}, s32[4,32]{1,0:T(4,128)}, u32[]{:S(2)}) copy-start(s32[4,32]{1,0:T(4,128)} %partner_ref.3) | copy-start | bytes 1540
  8.9 59.6 %copy-start = (bf16[2048,256]{1,0:T(8,128)(2,1)}, bf16[2048,256]{1,0:T(8,128)(2,1)S(1)}, u32[]{:S(2)}) copy-start(bf16[2048,256]{1,0:T(8,128)(2,1)S(1)} %bitcast_convert_fusion.refs_0_) | copy-start | bytes 3145732
  8.9 24.7 %collective-permute-start.1 = (bf16[2048,256]{1,0:T(8,128)(2,1)S(1)}, bf16[2048,256]{1,0:T(8,128)(2,1)S(1)}, u32[]{:S(2)}, u32[]{:S(2)}) collective-permute-start(bf16[2048,256]{1,0:T(8,128)(2,1)S(1)} %bitcast_convert_fusion.refs_0_), channel_id=1, source_target_pairs={{0,64},{32,96},{64,0},{96,32},{1,65},{33,97},{65,1},{97,33},{2,66}... | collective-permute-start | bytes 3145736 | tf_op jit(solution)/shard_map/ppermute | solution.py:345
  11.1 45.6 %collective-permute-start = (bf16[2048,256]{1,0:T(8,128)(2,1)S(1)}, bf16[2048,256]{1,0:T(8,128)(2,1)S(1)}, u32[]{:S(2)}, u32[]{:S(2)}) collective-permute-start(bf16[2048,256]{1,0:T(8,128)(2,1)S(1)} %bitcast_convert_fusion.refs_0_), channel_id=1, source_target_pairs={{0,32},{32,0},{64,96},{96,64},{1,33},{33,1},{65,97},{97,65},{2,34}... | collective-permute-start | bytes 3145736 | tf_op jit(solution)/shard_map/ppermute | solution.py:345
  33.6 34.9 %copy-start.4 = (bf16[2048,256]{1,0:T(8,128)(2,1)}, bf16[2048,256]{1,0:T(8,128)(2,1)S(1)}, u32[]{:S(2)}) copy-start(bf16[2048,256]{1,0:T(8,128)(2,1)S(1)} %collective-permute-done.1.refs_2_) | copy-start | bytes 3145732
  33.6 23.1 %collective-permute-start.2 = (bf16[2048,256]{1,0:T(8,128)(2,1)S(1)}, bf16[2048,256]{1,0:T(8,128)(2,1)}, u32[]{:S(2)}, u32[]{:S(2)}) collective-permute-start(bf16[2048,256]{1,0:T(8,128)(2,1)S(1)} %collective-permute-done.1.refs_2_), channel_id=1, source_target_pairs={{0,32},{32,0},{64,96},{96,64},{1,33},{33,1},{65,97},{97,65},{2,34}... | collective-permute-start | bytes 3145736 | tf_op jit(solution)/shard_map/ppermute | solution.py:345
  37.5 19.2 %all-to-all-start = ((s32[32,1,128]{2,1,0:T(1,128)}), s32[32,1,128]{2,1,0:T(1,128)S(1)}, u32[]{:S(2)}, u32[]{:S(2)}) async-start(s32[32,1,128]{2,1,0:T(1,128)} %bitcast.6), calls=%async_computation | async-start | bytes 32768 | tf_op jit(solution)/shard_map/all_to_all | solution.py:360
  56.7 11.8 %copy-start.5 = (bf16[2048,256]{1,0:T(8,128)(2,1)}, bf16[2048,256]{1,0:T(8,128)(2,1)S(1)}, u32[]{:S(2)}) copy-start(bf16[2048,256]{1,0:T(8,128)(2,1)S(1)} %collective-permute-done.refs_1_) | copy-start | bytes 3145732
  68.6 6.8 %copy-start.12 = (s32[1,2048]{1,0:T(1,128)S(1)}, s32[1,2048]{1,0:T(1,128)}, u32[]{:S(2)}) copy-start(s32[1,2048]{1,0:T(1,128)} %src_ref.3) | copy-start | bytes 24580
  68.6 6.8 %copy-start.13 = (s32[1,2,1024]{2,1,0:T(2,128)S(1)}, s32[1,2,1024]{2,1,0:T(2,128)}, u32[]{:S(2)}) copy-start(s32[1,2,1024]{2,1,0:T(2,128)} %param.21) | copy-start | bytes 24580
  68.6 6.8 %copy-start.14 = (s32[1,2,1024]{2,1,0:T(2,128)S(1)}, s32[1,2,1024]{2,1,0:T(2,128)}, u32[]{:S(2)}) copy-start(s32[1,2,1024]{2,1,0:T(2,128)} %param.22) | copy-start | bytes 24580
  68.6 32.7 %all-to-all-start.1 = ((bf16[32,128,256]{2,1,0:T(8,128)(2,1)}), bf16[32,128,256]{2,1,0:T(8,128)(2,1)}, u32[]{:S(2)}, u32[]{:S(2)}) async-start(bf16[32,128,256]{2,1,0:T(8,128)(2,1)} %shard_map.148), calls=%async_computation.1 | async-start | bytes 4194304 | tf_op jit(solution)/shard_map/all_to_all | solution.py:371
  75.4 25.9 %copy-start.9 = (s32[1,2]{1,0:T(1,128)S(1)}, s32[1,2]{1,0:T(1,128)}, u32[]{:S(2)}) copy-start(s32[1,2]{1,0:T(1,128)} %rel_ref.1) | copy-start | bytes 28
  138.9 106.4 %all-to-all-start.2 = ((bf16[32,144,256]{2,1,0:T(8,128)(2,1)}), bf16[32,144,256]{2,1,0:T(8,128)(2,1)}, u32[]{:S(2)}, u32[]{:S(2)}) async-start(bf16[32,144,256]{2,1,0:T(8,128)(2,1)} %get-tuple-element.28), calls=%async_computation.2 | async-start | bytes 4718592 | tf_op jit(solution)/shard_map/all_to_all | solution.py:410
  147.7 188.6 %all-gather.4.cloned.1.call-start = ((), (), s32[]{:S(2)}) async-start(), calls=%async_computation.3 | async-start | bytes 2703360 | tf_op jit(solution)/shard_map/all_gather | solution.py:432
  247.5 17.0 %collective-permute-start.6 = (bf16[20,8,256]{2,1,0:T(8,128)(2,1)S(1)}, bf16[20,8,256]{2,1,0:T(8,128)(2,1)S(1)}, u32[]{:S(2)}, u32[]{:S(2)}) collective-permute-start(bf16[20,8,256]{2,1,0:T(8,128)(2,1)S(1)} %dynamic-slice_bitcast_fusion), channel_id=1, source_target_pairs={{0,32},{32,0},{64,96},{96,64},{1,33},{33,1},{65,97},{97,65},{2,34}... | collective-permute-start | bytes 245768 | tf_op jit(solution)/shard_map/ppermute | solution.py:345
  264.5 4.4 %collective-permute-start.7 = (bf16[20,8,256]{2,1,0:T(8,128)(2,1)S(1)}, bf16[20,8,256]{2,1,0:T(8,128)(2,1)S(1)}, u32[]{:S(2)}, u32[]{:S(2)}) collective-permute-start(bf16[20,8,256]{2,1,0:T(8,128)(2,1)S(1)} %fusion.2), channel_id=1, source_target_pairs={{0,64},{32,96},{64,0},{96,32},{1,65},{33,97},{65,1},{97,33},{2,66}... | collective-permute-start | bytes 245768 | tf_op jit(solution)/shard_map/ppermute | solution.py:345
  293.3 48.7 %collective-permute-start.4 = (bf16[2048,256]{1,0:T(8,128)(2,1)}, bf16[2048,256]{1,0:T(8,128)(2,1)}, u32[]{:S(2)}, u32[]{:S(2)}) collective-permute-start(bf16[2048,256]{1,0:T(8,128)(2,1)} %get-tuple-element.33), channel_id=1, source_target_pairs={{0,32},{32,0},{64,96},{96,64},{1,33},{33,1},{65,97},{97,65},{2,34}... | collective-permute-start | bytes 3145736 | tf_op jit(solution)/shard_map/ppermute | solution.py:345
  294.1 50.7 %collective-permute-start.3 = (bf16[2048,256]{1,0:T(8,128)(2,1)S(1)}, bf16[2048,256]{1,0:T(8,128)(2,1)}, u32[]{:S(2)}, u32[]{:S(2)}) collective-permute-start(bf16[2048,256]{1,0:T(8,128)(2,1)S(1)} %get-tuple-element.31), channel_id=1, source_target_pairs={{0,32},{32,0},{64,96},{96,64},{1,33},{33,1},{65,97},{97,65},{2,34}... | collective-permute-start | bytes 3145736 | tf_op jit(solution)/shard_map/ppermute | solution.py:345
  339.8 5.0 %copy-start.18 = (f32[40,256]{1,0:T(8,128)S(1)}, f32[40,256]{1,0:T(8,128)}, u32[]{:S(2)}) copy-start(f32[40,256]{1,0:T(8,128)} %param.15) | copy-start | bytes 122884
  339.8 36.6 %collective-permute-start.8 = (bf16[32,20,8,256]{3,2,0,1:T(8,128)(2,1)}, bf16[32,20,8,256]{3,2,0,1:T(8,128)(2,1)}, u32[]{:S(2)}, u32[]{:S(2)}) collective-permute-start(bf16[32,20,8,256]{3,2,0,1:T(8,128)(2,1)} %copy.32), channel_id=1, source_target_pairs={{0,32},{32,0},{64,96},{96,64},{1,33},{33,1},{65,97},{97,65},{2,34}... | collective-permute-start | bytes 7864328 | tf_op jit(solution)/shard_map/ppermute | solution.py:345
  344.5 25.0 %collective-permute-start.5 = (bf16[2048,256]{1,0:T(8,128)(2,1)}, bf16[2048,256]{1,0:T(8,128)(2,1)S(1)}, u32[]{:S(2)}, u32[]{:S(2)}) collective-permute-start(bf16[2048,256]{1,0:T(8,128)(2,1)} %add_convert_fusion), channel_id=1, source_target_pairs={{0,64},{32,96},{64,0},{96,32},{1,65},{33,97},{65,1},{97,33},{2,66}... | collective-permute-start | bytes 3145736 | tf_op jit(solution)/shard_map/ppermute | solution.py:345
  (9 other events, 18.3 us)
Sparse Core Ops, SparseCore 0:
  269.8 66.4 all-gather.3

commit v2 on v1

--- a/solution.py
+++ b/solution.py
@@ -57,8 +57,8 @@
     return pl.CostEstimate(flops=int(flops), bytes_accessed=int(moved), transcendentals=0)
 
 
-def slots_body(owner_ref, row_ref, slot_ref, wanted_ref):
-    peers, room = wanted_ref.shape
+def slots_body(rel_ref, owner_ref, row_ref, slot_ref, wanted_ref):
+    peers, _, room = wanted_ref.shape
     edges = owner_ref.shape[1]
     step = 256
     before = lax.broadcasted_iota(jnp.int32, (step, step), 0)
@@ -80,7 +80,12 @@
         top = lax.shift_right_logical(row, 4)
         high += dot((hit * top.astype(full)).astype(half), spot, 1, 1)
         low += dot((hit * (row - top * 16).astype(full)).astype(half), spot, 1, 1)
-    wanted_ref[...] = (high * 16.0 + low).astype(jnp.int32)
+    wanted_ref[:, 0, :] = (high * 16.0 + low).astype(jnp.int32)
+    lane = lax.broadcasted_iota(jnp.int32, (peers, room), 1)
+    ids = jnp.zeros((peers, room), jnp.int32)
+    for block in range(rel_ref.shape[1]):
+        ids = jnp.where(lane == block, rel_ref[0, block], ids)
+    wanted_ref[:, 1, :] = ids
 
 
 def list_peers(partner_ref, group_ref, list_ref, count_ref):
@@ -102,7 +107,7 @@
 def answer_body(partner_ref, group_ref, asked_ref, *refs):
     tables, (found_ref, list_ref, count_ref) = refs[:4], refs[4:]
     rows, width = tables[0].shape
-    room = asked_ref.shape[1]
+    room = asked_ref.shape[2]
     list_peers(partner_ref, group_ref, list_ref, count_ref)
     for part in range(4):
         count = count_ref[part]
@@ -110,7 +115,9 @@
         def pair(t, carry, part=part, count=count):
             one = list_ref[part, 2 * t]
             two = list_ref[part, jnp.minimum(2 * t + 1, count - 1)]
-            ask = jnp.concatenate([asked_ref[pl.ds(one, 1), :], asked_ref[pl.ds(two, 1), :]], axis=1)
+            ask = jnp.concatenate(
+                [asked_ref[pl.ds(one, 1), 0, :], asked_ref[pl.ds(two, 1), 0, :]], axis=1
+            )
             got = dot(pick(ask, rows), tables[part][...], 1, 0).astype(half)
             found_ref[pl.ds(one, 1)] = got[:room].reshape(1, room, width)
             found_ref[pl.ds(two, 1)] = got[room:].reshape(1, room, width)
@@ -268,21 +275,22 @@
     lax.fori_loop(0, rows // step, part, 0)
 
 
-def home_body(partner_ref, group_ref, visit_to_ref, asked_ref, returned_ref, visit_ref, *refs):
-    outs, (total, list_ref, count_ref) = refs[:4], refs[4:]
+def home_body(
+    parts, partner_ref, group_ref, visit_to_ref, asked_ref, returned_ref, visit_ref, *refs
+):
+    outs, (total, list_ref, count_ref) = refs[: len(parts)], refs[len(parts) :]
     rows, width = visit_ref.shape
-    places = asked_ref.shape[1]
+    places = asked_ref.shape[2]
     list_peers(partner_ref, group_ref, list_ref, count_ref)
-    total[...] = jnp.zeros_like(total)
-    total[pl.ds(visit_to_ref[0], 1)] = visit_ref[...].reshape(1, rows, width)
-    for part in range(4):
+    for part, out_ref in zip(parts, outs):
         count = count_ref[part]
+        total[...] = jnp.where(visit_to_ref[0] == part, visit_ref[...], 0.0)
 
         def pair(t, carry, part=part, count=count):
             one = list_ref[part, 2 * t]
             two = list_ref[part, jnp.minimum(2 * t + 1, count - 1)]
-            ask_two = jnp.where(2 * t + 1 < count, asked_ref[pl.ds(two, 1), :], -1)
-            ask = jnp.concatenate([asked_ref[pl.ds(one, 1), :], ask_two], axis=1)
+            ask_two = jnp.where(2 * t + 1 < count, asked_ref[pl.ds(two, 1), 0, :], -1)
+            ask = jnp.concatenate([asked_ref[pl.ds(one, 1), 0, :], ask_two], axis=1)
             back = jnp.concatenate(
                 [
                     returned_ref[pl.ds(one, 1), :places, :].reshape(places, width),
@@ -291,28 +299,109 @@
                 axis=0,
             )
             for first in range(0, rows, 512):
-                total[part, first : first + 512] += dot(place(ask, first, 512), back, 1, 0)
+                total[first : first + 512] += dot(place(ask, first, 512), back, 1, 0)
             return carry
 
         lax.fori_loop(0, (count + 1) // 2, pair, 0)
-        outs[part][...] = total[part].astype(half)
-
-
-def operators_body(ids_ref, part_ref, out_ref, total):
+        out_ref[...] = total[...].astype(half)
+
+
+def operators_body(ids_ref, part_ref, out_ref):
     peers, _, width = part_ref.shape
     blocks = ids_ref.shape[1]
-    rows = total.shape[1]
-    total[...] = jnp.zeros_like(total)
+    rows = out_ref.shape[1]
+    out_ref[...] = jnp.zeros_like(out_ref)
 
     def add(peer, carry):
         piece = part_ref[pl.ds(peer, 1)].reshape(blocks * rows, width).astype(full)
         for block in range(blocks):
             at = ids_ref[peer, block]
-            total[pl.ds(at, 1)] += piece[block * rows : (block + 1) * rows].reshape(1, rows, width)
+            out_ref[pl.ds(at, 1)] += piece[block * rows : (block + 1) * rows].reshape(1, rows, width)
         return carry
 
     lax.fori_loop(0, peers, add, 0)
-    out_ref[...] = total[...].astype(half)
+
+
+def laid(column):
+    return jnp.broadcast_to(column, (column.shape[0], 128)).T[:1, :]
+
+
+def relation_body(core_ref, mine_ref, other_ref, relation_ref, acc_ref, new_ref, acc_new_ref):
+    step, rows, width = relation_ref.shape
+    at = pl.program_id(0)
+    own_half = at // (pl.num_programs(0) // 2) == core_ref[0]
+    for k in range(step):
+        line = at * step + k
+        mine = mine_ref[:, k].astype(full).reshape(rows, width)
+        other = other_ref[:, k].astype(full).reshape(rows, width)
+        grad = jnp.where(own_half, mine, other)
+        square = jnp.mean(grad * grad, axis=1, keepdims=True)
+        acc = acc_ref[pl.ds(line, 1), :]
+        acc_new_ref[pl.ds(line, 1), :] = acc + laid(square)
+        rate = step_rate / jnp.sqrt(turned(acc)[:, :1] + square)
+        new_ref[k] = relation_ref[k] - grad * rate
+
+
+def entity_body(grad_ref, home_ref, sibling_ref, cross_ref, entity_ref, acc_ref, new_ref, acc_new_ref):
+    grad = (
+        grad_ref[...]
+        + home_ref[...].astype(full)
+        + sibling_ref[...].astype(full)
+        + cross_ref[...].astype(full)
+    )
+    square = jnp.mean(grad * grad, axis=1, keepdims=True)
+    acc = acc_ref[...]
+    acc_new_ref[...] = acc + laid(square)
+    new_ref[0] = entity_ref[0] - grad * (step_rate / jnp.sqrt(turned(acc)[:, :1] + square))
+
+
+def relation_update(core, mine, other, relation, relation_acc):
+    peers, count, extra, width = mine.shape
+    relations, rows = relation_acc.shape
+    step = 4 if count % 4 == 0 else 1
+    steps = count // step
+
+    def near(flip):
+        def at(i, core):
+            return (0, jnp.clip(i - steps * (core[0] ^ flip), 0, steps - 1), 0, 0)
+
+        return pl.BlockSpec((peers, step, extra, width), at)
+
+    whole = pl.BlockSpec((relations, rows), lambda i, core: (0, 0))
+    block = pl.BlockSpec((step, rows, width), lambda i, core: (i, 0, 0))
+    return pl.pallas_call(
+        relation_body,
+        grid_spec=pltpu.PrefetchScalarGridSpec(
+            num_scalar_prefetch=1,
+            grid=(2 * steps,),
+            in_specs=[near(0), near(1), block, whole],
+            out_specs=[block, whole],
+        ),
+        out_shape=[
+            jax.ShapeDtypeStruct(relation.shape, full),
+            jax.ShapeDtypeStruct(relation_acc.shape, full),
+        ],
+        compiler_params=pltpu.CompilerParams(vmem_limit_bytes=VMEM_BYTES),
+    )(core, mine, other, relation, relation_acc)
+
+
+def entity_update(grad, home, sibling, cross, entity, entity_acc):
+    rows, width = grad.shape
+    step = 256
+    part = pl.BlockSpec((step, width), lambda i: (i, 0))
+    block = pl.BlockSpec((1, step, width), lambda i: (0, i, 0))
+    line = pl.BlockSpec((1, step), lambda i: (0, i))
+    return pl.pallas_call(
+        entity_body,
+        grid=(rows // step,),
+        in_specs=[part] * 4 + [block, line],
+        out_specs=[block, line],
+        out_shape=[
+            jax.ShapeDtypeStruct(entity.shape, full),
+            jax.ShapeDtypeStruct(entity_acc.shape, full),
+        ],
+        compiler_params=pltpu.CompilerParams(vmem_limit_bytes=VMEM_BYTES),
+    )(grad, home, sibling, cross, entity, entity_acc)
 
 
 def on_device(
@@ -353,11 +442,13 @@
     own = entity[0].astype(half)
     cross = neighbour(own, 2)
     sibling = neighbour(own, 1)
-    group_ids = lax.all_gather(rel_ids[0], "dev", axis=0)
     slot, wanted = call(
-        slots_body, (sds((1, edges), jnp.int32), sds((peers, room), jnp.int32)), specs=[VMEM] * 2
-    )(owners, dst_row)
+        slots_body,
+        (sds((1, edges), jnp.int32), sds((peers, 2, room), jnp.int32)),
+        specs=[SMEM] + [VMEM] * 2,
+    )(rel_ids, owners, dst_row)
     asked = lax.all_to_all(wanted, "dev", split_axis=0, concat_axis=0, tiled=True)
+    cross, asked = lax.optimization_barrier((cross, asked))
     cross_sibling = neighbour(cross, 1)
     tables = (own, sibling, cross, cross_sibling)
 
@@ -417,41 +508,40 @@
         cost(2 * 3 * edges * rows * width, 7 * rows * width * 2),
     )(src_row, neg_src, neg_dst, d_src, d_neg_src, d_neg_dst)
 
-    rel_part = call(
-        operators_body,
-        sds((relations, extra, width), half),
-        [pltpu.VMEM((relations, extra, width), full)],
-        [SMEM, VMEM],
-    )(group_ids, returned[:, room:, :])
+    rel_part = call(operators_body, sds((relations, extra, width), full), (), [SMEM, VMEM])(
+        asked[:, 1, :blocks], returned[:, room:, :]
+    )
     core = me & 1
     halves = rel_part.reshape(2, relations // 2, extra, width)
     mine = lax.dynamic_index_in_dim(halves, core, 0, keepdims=False)
     other = lax.dynamic_index_in_dim(halves, 1 - core, 0, keepdims=False)
-    chip = (mine.astype(full) + neighbour(other, 1).astype(full)).astype(half)
-    pair = (chip.astype(full) + neighbour(chip, 2).astype(full)).astype(half)
-    gathered = lax.all_gather(pair, "dev", axis=0)
-
-    home, home_sibling, home_cross, home_cross_sibling = call(
-        home_body,
-        tuple(sds((rows, width), half) for _ in range(4)),
-        [pltpu.VMEM((4, rows, width), full)] + lists,
-        [SMEM] * 3 + [VMEM] * 3,
-    )(partner, group, visit_to, asked, returned, visit_grad)
+    chip = mine + neighbour(other, 1)
+    pair = (chip + neighbour(chip, 2)).astype(half)
+    gathered = lax.all_to_all(
+        jnp.broadcast_to(pair[None], (peers,) + pair.shape), "dev", split_axis=0, concat_axis=0, tiled=True
+    )
+    other_half = neighbour(gathered, 1)
+
+    def home(parts):
+        return call(
+            functools.partial(home_body, parts),
+            tuple(sds((rows, width), half) for _ in parts),
+            [pltpu.VMEM((rows, width), full)] + lists,
+            [SMEM] * 3 + [VMEM] * 3,
+        )(partner, group, visit_to, asked, returned, visit_grad)
+
+    home_cross_sibling, home_cross = home((3, 2))
     chip_cross = (home_cross.astype(full) + neighbour(home_cross_sibling, 1).astype(full)).astype(half)
     from_cross = neighbour(chip_cross, 2)
+    home_sibling, home_own = home((1, 0))
     from_sibling = neighbour(home_sibling, 1)
-    total_grad = (
-        own_grad + home.astype(full) + from_sibling.astype(full) + from_cross.astype(full)
-    )
-    acc_new = entity_acc[0] + jnp.mean(total_grad * total_grad, axis=1)
-    entity_new = entity[0] - step_rate * total_grad / jnp.sqrt(acc_new)[:, None]
-
-    other_half = neighbour(gathered, 1)
-    both = jnp.where(core == 0, jnp.stack([gathered, other_half]), jnp.stack([other_half, gathered]))
-    rel_total = both.transpose(0, 2, 1, 3, 4).reshape(relations, width, width).astype(full)
-    relation_acc_new = relation_acc + jnp.mean(rel_total * rel_total, axis=2)
-    relation_new = relation - step_rate * rel_total / jnp.sqrt(relation_acc_new)[:, :, None]
-    return (entity_new[None], acc_new[None], relation_new, relation_acc_new)
+    entity_new, acc_new = entity_update(
+        own_grad, home_own, from_sibling, from_cross, entity, entity_acc
+    )
+    relation_new, relation_acc_new = relation_update(
+        core.reshape(1), gathered, other_half, relation, relation_acc
+    )
+    return (entity_new, acc_new, relation_new, relation_acc_new)
 
 
 def solution(mesh):

time: 408 us -> 278 us (0.68)
  blocking collectives: 97.5 us -> 0 us
  other arithmetic: 34.3 us -> 3.25 us
  Pallas kernels: 83.2 us -> 107 us
  between operations: 15.6 us -> 2.19 us
  waiting for transfers between devices: 114 us -> 105 us
  starting transfers between devices: 50.6 us -> 43.2 us
  local copies, waits for them, and re-layouts: 11.6 us -> 15.8 us
    all_gather x1 -> x0, blocking collectives: 97.5 us -> none  [on_device(): group_ids = lax.all_gather(rel_ids[0], 'dev', axis=0)]
    all_gather x1 -> x0, waiting for transfers between devices: 42.1 us -> none  [on_device(): gathered = lax.all_gather(pair, 'dev', axis=0)]
    all_to_all x1, waiting for transfers between devices: 0.01 us -> 32.3 us  [on_device(): lax.all_to_all(outgoing, 'dev', split_axis=0, concat_axis=0, tiled=True)]
    pallas_call x3 -> x6, Pallas kernels: 16 us -> 40.6 us  [the longest x2 15.2 us: home(): call(functools.partial(home_body, parts), tuple((sds((rows, width), half)...]
    ppermute x9, waiting for transfers between devices: 49.6 us -> 30.9 us  [neighbour(): return lax.ppermute(x, 'grp', [(g, g ^ flip) for g in range(4)])]
    reduce_sum x2 -> x0, other arithmetic: 13.6 us -> none  [the longest x1 10.8 us: on_device(): relation_acc_new = relation_acc + jnp.mean(rel_total * rel_total, axis=2)]
    ppermute x9, starting transfers between devices: 26.2 us -> 13.4 us  [neighbour(): return lax.ppermute(x, 'grp', [(g, g ^ flip) for g in range(4)])]
    all_to_all x0 -> x1, waiting for transfers between devices: none -> 11.8 us  [on_device(): lax.all_to_all(jnp.broadcast_to(pair[None], (peers,) + pair.shape), 'dev'...]
  transfers between devices with their start and end apart: 13 -> 13, of which waited for: 7 -> 8; matrix products, arithmetic and copies ran while one was open for 3% -> 1% of each run, Pallas kernels for 8% -> 16%
where the time goes in v2:
time: 278 us; the launch traced here: 277 us
  Pallas kernels  107 us (38%)
  waiting for transfers between devices  105 us (38%)
  starting transfers between devices  43.2 us (16%)
  local copies, waits for them, and re-layouts  15.8 us (6%)
  other arithmetic  3.25 us (1%)
    pallas_call x1, Pallas kernels, on_device(): call(model_body, (sds((peers, room + blocks * extra, width), half), sds((...  36.5 us
    all_to_all x1, waiting for transfers between devices, on_device(): lax.all_to_all(outgoing, 'dev', split_axis=0, concat_axis=0, tiled=True)  32.3 us
    ppermute x9, waiting for transfers between devices, neighbour(): return lax.ppermute(x, 'grp', [(g, g ^ flip) for g in range(4)])  30.9 us
    all_to_all x1, waiting for transfers between devices, on_device(): lax.all_to_all(found, 'dev', split_axis=0, concat_axis=0, tiled=True)  15.9 us
    pallas_call x2, Pallas kernels, home(): call(functools.partial(home_body, parts), tuple((sds((rows, width), half)...  15.2 us
    all_to_all x1, waiting for transfers between devices, on_device(): lax.all_to_all(wanted, 'dev', split_axis=0, concat_axis=0, tiled=True)  14.3 us
    pallas_call x1, Pallas kernels, relation_update(): pl.pallas_call(relation_body, grid_spec=pltpu.PrefetchScalarGridSpec(num_...  14.2 us
    ppermute x9, starting transfers between devices, neighbour(): return lax.ppermute(x, 'grp', [(g, g ^ flip) for g in range(4)])  13.4 us
  transfers between devices with their start and end apart: 13, of which 8 were waited for; matrix products, arithmetic and copies ran while one was open for 1% of the time, Pallas kernels for 16%

profile of v2, /device:TPU:1, one launch (start us, length us, event | category | flops | bytes accessed | tf_op | source)
XLA Modules:
  0.0 277.1 jit_solution(17996248624999163292)
XLA Ops:
  2.4 2.2 collective-permute-start
  4.6 2.8 %shard_map.147 = (s32[1,2048]{1,0:T(1,128)S(1)}, s32[32,2,128]{2,1,0:T(2,128)}) custom-call(s32[1,2]{1,0:T(1,128)S(1)} %copy-done.13, s32[1,2048]{1,0:T(1,128)S(1)} %bitcast.19, s32[1,2048]{1,0:T(1,128)S(1)} %copy-done.11), custom_call_target="tpu_custom_call" | custom-call | tf_op jit(solution)/shard_map/pallas_call | solution.py:445
  7.5 10.2 %all-to-all-start = ((s32[32,2,128]{2,1,0:T(2,128)}), s32[32,2,128]{2,1,0:T(2,128)S(1)}, u32[]{:S(2)}, u32[]{:S(2)}) async-start(s32[32,2,128]{2,1,0:T(2,128)} %get-tuple-element.26), calls=%async_computation | async-start | bytes 65536 | tf_op jit(solution)/shard_map/all_to_all | solution.py:450
  19.0 14.3 %all-to-all-done.asked_ref = s32[32,2,128]{2,1,0:T(2,128)S(1)} async-done(((s32[32,2,128]{2,1,0:T(2,128)}), s32[32,2,128]{2,1,0:T(2,128)S(1)}, u32[]{:S(2)}, u32[]{:S(2)}) %all-to-all-start) | async-done | bytes 32800 | tf_op jit(solution)/shard_map/all_to_all | solution.py:450
  33.3 1.9 collective-permute-start.2
  35.2 2.4 collective-permute-done.2.refs_3_
  37.6 11.4 %shard_map.148 = bf16[32,128,256]{2,1,0:T(8,128)(2,1)} custom-call(s32[4,32]{1,0:T(4,128)S(1)} %copy-done.9, s32[1]{0:T(128)} %bitcast.3.group_ref, s32[32,2,128]{2,1,0:T(2,128)S(1)} %all-to-all-done.asked_ref, bf16[2048,256]{1,0:T(8,128)(2,1)S(1)} %convert_bitcast_fusion.refs_0_, bf16[2048,256]{1,0:T(8,128)(2,1)S(1)} %collective-permute-done.1.refs_1_, ...), custom_call_target="tpu_custom_call" | custom-call | tf_op jit(solution)/shard_map/pallas_call | solution.py:456
  49.0 5.5 %all-to-all-start.1 = ((bf16[32,128,256]{2,1,0:T(8,128)(2,1)}), bf16[32,128,256]{2,1,0:T(8,128)(2,1)S(1)}, u32[]{:S(2)}, u32[]{:S(2)}) async-start(bf16[32,128,256]{2,1,0:T(8,128)(2,1)} %shard_map.148), calls=%async_computation.1 | async-start | bytes 4194304 | tf_op jit(solution)/shard_map/all_to_all | solution.py:462
  56.5 9.0 %shard_map.149 = (bf16[2048,256]{1,0:T(8,128)(2,1)S(1)}, bf16[2048,256]{1,0:T(8,128)(2,1)S(1)}, bf16[2048,256]{1,0:T(8,128)(2,1)S(1)}) custom-call(s32[1]{0:T(128)} %bitcast.7.visit_ref.visit_to_ref, s32[1,2048]{1,0:T(1,128)S(1)} %copy-done.20, s32[2,1024]{1,0:T(2,128)S(1)} %bitcast.20, s32[2,1024]{1,0:T(2,128)S(1)} %bitcast.22, bf16[2048,256]{1,0:T(8,128)(2,1)} %copy-done, ...), custom_call_target="tpu_custom_call" | custom-call | flops 6442450944 | bytes 6291456 | tf_op jit(solution)/shard_map/pallas_call | solution.py:464
  68.4 15.9 %all-to-all-done.1 = bf16[32,128,256]{2,1,0:T(8,128)(2,1)S(1)} async-done(((bf16[32,128,256]{2,1,0:T(8,128)(2,1)}), bf16[32,128,256]{2,1,0:T(8,128)(2,1)S(1)}, u32[]{:S(2)}, u32[]{:S(2)}) %all-to-all-start.1) | async-done | bytes 2097184 | tf_op jit(solution)/shard_map/all_to_all | solution.py:462
  85.7 36.5 %shard_map.150 = (bf16[32,144,256]{2,1,0:T(8,128)(2,1)}, bf16[2048,256]{1,0:T(8,128)(2,1)S(1)}, bf16[2048,256]{1,0:T(8,128)(2,1)S(1)}, bf16[2048,256]{1,0:T(8,128)(2,1)S(1)}) custom-call(s32[1,2]{1,0:T(1,128)S(1)} %copy-done.13, s32[1,1]{1,0:T(1,128)S(6)} %copy.19.count_ref, s32[1,2048]{1,0:T(1,128)S(1)} %get-tuple-element.25.slot_ref, ...), custom_call_target="tpu_custom_call" | custom-call | tf_op jit(solution)/shard_map/pallas_call | solution.py:472
  125.1 6.7 %all-to-all-start.2 = ((bf16[32,144,256]{2,1,0:T(8,128)(2,1)}), bf16[32,144,256]{2,1,0:T(8,128)(2,1)S(1)}, u32[]{:S(2)}, u32[]{:S(2)}) async-start(bf16[32,144,256]{2,1,0:T(8,128)(2,1)} %get-tuple-element.36), calls=%async_computation.2 | async-start | bytes 4718592 | tf_op jit(solution)/shard_map/all_to_all | solution.py:501
  131.9 32.3 %all-to-all-done.2.returned_ref = bf16[32,144,256]{2,1,0:T(8,128)(2,1)S(1)} async-done(((bf16[32,144,256]{2,1,0:T(8,128)(2,1)}), bf16[32,144,256]{2,1,0:T(8,128)(2,1)S(1)}, u32[]{:S(2)}, u32[]{:S(2)}) %all-to-all-start.2) | async-done | bytes 2359328 | tf_op jit(solution)/shard_map/all_to_all | solution.py:501
  169.2 4.0 %collective-permute-done.7 = f32[20,8,256]{2,1,0:T(8,128)S(1)} collective-permute-done((f32[20,8,256]{2,1,0:T(8,128)S(1)}, f32[20,8,256]{2,1,0:T(8,128)S(1)}, u32[]{:S(2)}, u32[]{:S(2)}) %collective-permute-start.7) | collective-permute-done | bytes 163872 | tf_op jit(solution)/shard_map/ppermute | solution.py:434
  173.3 1.8 broadcast_in_dim.2
  175.1 7.3 %all-to-all-start.3 = ((bf16[32,20,8,256]{3,2,1,0:T(8,128)(2,1)}), bf16[32,20,8,256]{3,2,1,0:T(8,128)(2,1)S(1)}, u32[]{:S(2)}, u32[]{:S(2)}) async-start(bf16[32,20,8,256]{3,2,1,0:T(8,128)(2,1)} %broadcast_in_dim.2), calls=%async_computation.3 | async-start | bytes 5242880 | tf_op jit(solution)/shard_map/all_to_all | solution.py:520
  186.0 9.9 %shard_map.151 = (f32[2048,256]{1,0:T(8,128)}, f32[2048,256]{1,0:T(8,128)}) custom-call(s32[1,2048]{1,0:T(1,128)S(1)} %copy-done.20, s32[2,1024]{1,0:T(2,128)S(1)} %bitcast.21, s32[2,1024]{1,0:T(2,128)S(1)} %bitcast.23, bf16[2048,256]{1,0:T(8,128)(2,1)S(1)} %copy-done.15, bf16[2048,256]{1,0:T(8,128)(2,1)S(1)} %copy-done.17, bf16[2048,256]{1,0:T(8,128)(2,1)S(1)} %copy-done.19), custom_call_target="tpu_custom_call" | custom-call | flops 6442450944 | bytes 7340032 | tf_op jit(solution)/shard_map/pallas_call | solution.py:503
  195.9 6.9 %shard_map.153 = (bf16[2048,256]{1,0:T(8,128)(2,1)}, bf16[2048,256]{1,0:T(8,128)(2,1)S(1)}) custom-call(s32[4,32]{1,0:T(4,128)S(1)} %copy-done.9, s32[1]{0:T(128)} %bitcast.3.group_ref, s32[1]{0:T(128)} %bitcast.7.visit_ref.visit_to_ref, s32[32,2,128]{2,1,0:T(2,128)S(1)} %all-to-all-done.asked_ref, bf16[32,144,256]{2,1,0:T(8,128)(2,1)} %copy-done.23, ...), custom_call_target="tpu_custom_call" | custom-call | tf_op jit(solution)/shard_map/pallas_call | solution.py:526
  205.1 11.8 %all-to-all-done.3.mine_ref = bf16[32,20,8,256]{3,2,1,0:T(8,128)(2,1)S(1)} async-done(((bf16[32,20,8,256]{3,2,1,0:T(8,128)(2,1)}), bf16[32,20,8,256]{3,2,1,0:T(8,128)(2,1)S(1)}, u32[]{:S(2)}, u32[]{:S(2)}) %all-to-all-start.3) | async-done | bytes 2621472 | tf_op jit(solution)/shard_map/all_to_all | solution.py:520
  218.6 8.3 %shard_map.152 = (bf16[2048,256]{1,0:T(8,128)(2,1)S(1)}, bf16[2048,256]{1,0:T(8,128)(2,1)S(1)}) custom-call(s32[4,32]{1,0:T(4,128)S(1)} %copy-done.9, s32[1]{0:T(128)} %bitcast.3.group_ref, s32[1]{0:T(128)} %bitcast.7.visit_ref.visit_to_ref, s32[32,2,128]{2,1,0:T(2,128)S(1)} %all-to-all-done.asked_ref, bf16[32,144,256]{2,1,0:T(8,128)(2,1)} %copy-done.23, ...), custom_call_target="tpu_custom_call" | custom-call | tf_op jit(solution)/shard_map/pallas_call | solution.py:526
  228.6 2.1 collective-permute-start.5
  230.8 23.5 %collective-permute-done.5.cross_ref = bf16[2048,256]{1,0:T(8,128)(2,1)S(1)} collective-permute-done((bf16[2048,256]{1,0:T(8,128)(2,1)S(1)}, bf16[2048,256]{1,0:T(8,128)(2,1)S(1)}, u32[]{:S(2)}, u32[]{:S(2)}) %collective-permute-start.5) | collective-permute-done | bytes 1048608 | tf_op jit(solution)/shard_map/ppermute | solution.py:434
  254.2 7.2 %shard_map.154 = (f32[1,2048,256]{2,1,0:T(8,128)}, f32[1,2048]{1,0:T(1,128)}) custom-call(f32[2048,256]{1,0:T(8,128)} %get-tuple-element.35.grad_ref, bf16[2048,256]{1,0:T(8,128)(2,1)S(1)} %get-tuple-element.38.home_ref, bf16[2048,256]{1,0:T(8,128)(2,1)S(1)} %collective-permute-done.3.sibling_ref, bf16[2048,256]{1,0:T(8,128)(2,1)S(1)} %collective-permute-done.5.cross_ref, ...), custom_call_target="tpu_custom_call" | custom-call | tf_op jit(solution)/shard_map/pallas_call | solution.py:394
  263.0 14.2 %shard_map.156 = (f32[40,256,256]{2,1,0:T(8,128)}, f32[40,256]{1,0:T(8,128)}) custom-call(s32[1]{0:T(128)} %bitcast.8.core_ref, bf16[32,20,8,256]{3,2,1,0:T(8,128)(2,1)S(1)} %all-to-all-done.3.mine_ref, bf16[32,20,8,256]{3,2,1,0:T(8,128)(2,1)} %copy-done.25, f32[40,256,256]{2,1,0:T(8,128)} %relation_ref.3, f32[40,256]{1,0:T(8,128)S(1)} %copy-done.8), custom_call_target="tpu_custom_call" | custom-call | tf_op jit(solution)/shard_map/pallas_call | solution.py:372
  (73 shorter events, 26.7 us)
Async XLA Ops:
  0.7 36.9 %copy-start.9 = (s32[4,32]{1,0:T(4,128)S(1)}, s32[4,32]{1,0:T(4,128)}, u32[]{:S(2)}) copy-start(s32[4,32]{1,0:T(4,128)} %partner_ref.5) | copy-start | bytes 1540
  2.4 46.6 %copy-start = (bf16[2048,256]{1,0:T(8,128)(2,1)}, bf16[2048,256]{1,0:T(8,128)(2,1)S(1)}, u32[]{:S(2)}) copy-start(bf16[2048,256]{1,0:T(8,128)(2,1)S(1)} %convert_bitcast_fusion.refs_0_) | copy-start | bytes 3145732
  2.4 30.9 %collective-permute-start = (bf16[2048,256]{1,0:T(8,128)(2,1)S(1)}, bf16[2048,256]{1,0:T(8,128)(2,1)S(1)}, u32[]{:S(2)}, u32[]{:S(2)}) collective-permute-start(bf16[2048,256]{1,0:T(8,128)(2,1)S(1)} %convert_bitcast_fusion.refs_0_), channel_id=1, source_target_pairs={{0,64},{32,96},{64,0},{96,32},{1,65},{33,97},{65,1},{97,33},{2,66}... | collective-permute-start | bytes 3145736 | tf_op jit(solution)/shard_map/ppermute | solution.py:434
  7.5 25.8 %all-to-all-start = ((s32[32,2,128]{2,1,0:T(2,128)}), s32[32,2,128]{2,1,0:T(2,128)S(1)}, u32[]{:S(2)}, u32[]{:S(2)}) async-start(s32[32,2,128]{2,1,0:T(2,128)} %get-tuple-element.26), calls=%async_computation | async-start | bytes 65536 | tf_op jit(solution)/shard_map/all_to_all | solution.py:450
  17.7 17.5 %collective-permute-start.1 = (bf16[2048,256]{1,0:T(8,128)(2,1)S(1)}, bf16[2048,256]{1,0:T(8,128)(2,1)S(1)}, u32[]{:S(2)}, u32[]{:S(2)}) collective-permute-start(bf16[2048,256]{1,0:T(8,128)(2,1)S(1)} %convert_bitcast_fusion.refs_0_), channel_id=1, source_target_pairs={{0,32},{32,0},{64,96},{96,64},{1,33},{33,1},{65,97},{97,65},{2,34}... | collective-permute-start | bytes 3145736 | tf_op jit(solution)/shard_map/ppermute | solution.py:434
  33.3 15.7 %copy-start.6 = (bf16[2048,256]{1,0:T(8,128)(2,1)}, bf16[2048,256]{1,0:T(8,128)(2,1)S(1)}, u32[]{:S(2)}) copy-start(bf16[2048,256]{1,0:T(8,128)(2,1)S(1)} %collective-permute-done.refs_2_) | copy-start | bytes 3145732
  33.3 4.3 %collective-permute-start.2 = (bf16[2048,256]{1,0:T(8,128)(2,1)S(1)}, bf16[2048,256]{1,0:T(8,128)(2,1)}, u32[]{:S(2)}, u32[]{:S(2)}) collective-permute-start(bf16[2048,256]{1,0:T(8,128)(2,1)S(1)} %collective-permute-done.refs_2_), channel_id=1, source_target_pairs={{0,32},{32,0},{64,96},{96,64},{1,33},{33,1},{65,97},{97,65},{2,34}... | collective-permute-start | bytes 3145736 | tf_op jit(solution)/shard_map/ppermute | solution.py:434
  35.2 13.8 %copy-start.7 = (bf16[2048,256]{1,0:T(8,128)(2,1)}, bf16[2048,256]{1,0:T(8,128)(2,1)S(1)}, u32[]{:S(2)}) copy-start(bf16[2048,256]{1,0:T(8,128)(2,1)S(1)} %collective-permute-done.1.refs_1_) | copy-start | bytes 3145732
  49.0 7.5 %copy-start.20 = (s32[1,2048]{1,0:T(1,128)S(1)}, s32[1,2048]{1,0:T(1,128)}, u32[]{:S(2)}) copy-start(s32[1,2048]{1,0:T(1,128)} %src_ref.3) | copy-start | bytes 24580
  49.0 7.5 %copy-start.21 = (s32[1,2,1024]{2,1,0:T(2,128)S(1)}, s32[1,2,1024]{2,1,0:T(2,128)}, u32[]{:S(2)}) copy-start(s32[1,2,1024]{2,1,0:T(2,128)} %param.21) | copy-start | bytes 24580
  49.0 7.5 %copy-start.22 = (s32[1,2,1024]{2,1,0:T(2,128)S(1)}, s32[1,2,1024]{2,1,0:T(2,128)}, u32[]{:S(2)}) copy-start(s32[1,2,1024]{2,1,0:T(2,128)} %param.22) | copy-start | bytes 24580
  49.0 35.3 %all-to-all-start.1 = ((bf16[32,128,256]{2,1,0:T(8,128)(2,1)}), bf16[32,128,256]{2,1,0:T(8,128)(2,1)S(1)}, u32[]{:S(2)}, u32[]{:S(2)}) async-start(bf16[32,128,256]{2,1,0:T(8,128)(2,1)} %shard_map.148), calls=%async_computation.1 | async-start | bytes 4194304 | tf_op jit(solution)/shard_map/all_to_all | solution.py:462
  125.1 39.1 %all-to-all-start.2 = ((bf16[32,144,256]{2,1,0:T(8,128)(2,1)}), bf16[32,144,256]{2,1,0:T(8,128)(2,1)S(1)}, u32[]{:S(2)}, u32[]{:S(2)}) async-start(bf16[32,144,256]{2,1,0:T(8,128)(2,1)} %get-tuple-element.36), calls=%async_computation.2 | async-start | bytes 4718592 | tf_op jit(solution)/shard_map/all_to_all | solution.py:501
  164.2 10.8 %copy-start.23 = (bf16[32,144,256]{2,1,0:T(8,128)(2,1)}, bf16[32,144,256]{2,1,0:T(8,128)(2,1)S(1)}, u32[]{:S(2)}) copy-start(bf16[32,144,256]{2,1,0:T(8,128)(2,1)S(1)} %all-to-all-done.2.returned_ref) | copy-start | bytes 7077892
  165.4 2.3 collective-permute-start.6
  167.8 5.5 %collective-permute-start.7 = (f32[20,8,256]{2,1,0:T(8,128)S(1)}, f32[20,8,256]{2,1,0:T(8,128)S(1)}, u32[]{:S(2)}, u32[]{:S(2)}) collective-permute-start(f32[20,8,256]{2,1,0:T(8,128)S(1)} %bitcast_add_fusion), channel_id=1, source_target_pairs={{0,64},{32,96},{64,0},{96,32},{1,65},{33,97},{65,1},{97,33},{2,66}... | collective-permute-start | bytes 491528 | tf_op jit(solution)/shard_map/ppermute | solution.py:434
  175.1 41.8 %all-to-all-start.3 = ((bf16[32,20,8,256]{3,2,1,0:T(8,128)(2,1)}), bf16[32,20,8,256]{3,2,1,0:T(8,128)(2,1)S(1)}, u32[]{:S(2)}, u32[]{:S(2)}) async-start(bf16[32,20,8,256]{3,2,1,0:T(8,128)(2,1)} %broadcast_in_dim.2), calls=%async_computation.3 | async-start | bytes 5242880 | tf_op jit(solution)/shard_map/all_to_all | solution.py:520
  203.8 23.3 %collective-permute-start.4 = (bf16[2048,256]{1,0:T(8,128)(2,1)}, bf16[2048,256]{1,0:T(8,128)(2,1)}, u32[]{:S(2)}, u32[]{:S(2)}) collective-permute-start(bf16[2048,256]{1,0:T(8,128)(2,1)} %get-tuple-element.41), channel_id=1, source_target_pairs={{0,32},{32,0},{64,96},{96,64},{1,33},{33,1},{65,97},{97,65},{2,34}... | collective-permute-start | bytes 3145736 | tf_op jit(solution)/shard_map/ppermute | solution.py:434
  216.9 10.2 %copy-start.2 = (bf16[2048,256]{1,0:T(8,128)(2,1)S(1)}, bf16[2048,256]{1,0:T(8,128)(2,1)}, u32[]{:S(2)}) copy-start(bf16[2048,256]{1,0:T(8,128)(2,1)} %copy-done.1) | copy-start | bytes 3145732
  216.9 44.6 %collective-permute-start.8 = (bf16[32,20,8,256]{3,2,1,0:T(8,128)(2,1)S(1)}, bf16[32,20,8,256]{3,2,1,0:T(8,128)(2,1)S(1)}, u32[]{:S(2)}, u32[]{:S(2)}) collective-permute-start(bf16[32,20,8,256]{3,2,1,0:T(8,128)(2,1)S(1)} %all-to-all-done.3.mine_ref), channel_id=1, source_target_pairs={{0,32},{32,0},{64,96},{96,64},{1,33},{33,1},{65,97},{97,65},{2,34}... | collective-permute-start | bytes 7864328 | tf_op jit(solution)/shard_map/ppermute | solution.py:434
  226.9 27.3 %copy-start.12 = (f32[1,2048]{1,0:T(1,128)S(1)}, f32[1,2048]{1,0:T(1,128)}, u32[]{:S(2)}) copy-start(f32[1,2048]{1,0:T(1,128)} %acc_ref.2) | copy-start | bytes 24580
  226.9 3.8 %collective-permute-start.3 = (bf16[2048,256]{1,0:T(8,128)(2,1)S(1)}, bf16[2048,256]{1,0:T(8,128)(2,1)S(1)}, u32[]{:S(2)}, u32[]{:S(2)}) collective-permute-start(bf16[2048,256]{1,0:T(8,128)(2,1)S(1)} %get-tuple-element.39), channel_id=1, source_target_pairs={{0,32},{32,0},{64,96},{96,64},{1,33},{33,1},{65,97},{97,65},{2,34}... | collective-permute-start | bytes 3145736 | tf_op jit(solution)/shard_map/ppermute | solution.py:434
  228.6 25.6 %collective-permute-start.5 = (bf16[2048,256]{1,0:T(8,128)(2,1)S(1)}, bf16[2048,256]{1,0:T(8,128)(2,1)S(1)}, u32[]{:S(2)}, u32[]{:S(2)}) collective-permute-start(bf16[2048,256]{1,0:T(8,128)(2,1)S(1)} %add_convert_fusion), channel_id=1, source_target_pairs={{0,64},{32,96},{64,0},{96,32},{1,65},{33,97},{65,1},{97,33},{2,66}... | collective-permute-start | bytes 3145736 | tf_op jit(solution)/shard_map/ppermute | solution.py:434
  254.2 8.7 %copy-start.8 = (f32[40,256]{1,0:T(8,128)S(1)}, f32[40,256]{1,0:T(8,128)}, u32[]{:S(2)}) copy-start(f32[40,256]{1,0:T(8,128)} %acc_ref.3) | copy-start | bytes 122884
  (15 other events, 25.3 us)

commit v3 on v2

--- a/solution.py
+++ b/solution.py
@@ -8,7 +8,7 @@
 from jax.sharding import PartitionSpec as P
 
 step_rate = 0.1
-VMEM_BYTES = 50 * 1024 * 1024
+MEBI = 1024 * 1024
 half = jnp.bfloat16
 full = jnp.float32
 VMEM = pl.BlockSpec(memory_space=pltpu.VMEM)
@@ -40,14 +40,14 @@
     return jnp.where(row == line, 1.0, 0.0).astype(half)
 
 
-def call(body, outs, scratch=(), specs=None, cost=None, **kw):
+def call(body, outs, scratch=(), specs=None, cost=None, mebi=16, **kw):
     return pl.pallas_call(
         body,
         out_shape=outs,
         in_specs=specs,
         out_specs=jax.tree.map(lambda _: VMEM, outs),
         scratch_shapes=list(scratch),
-        compiler_params=pltpu.CompilerParams(vmem_limit_bytes=VMEM_BYTES),
+        compiler_params=pltpu.CompilerParams(vmem_limit_bytes=mebi * MEBI),
         cost_estimate=cost,
         **kw,
     )
@@ -326,20 +326,37 @@
     return jnp.broadcast_to(column, (column.shape[0], 128)).T[:1, :]
 
 
-def relation_body(core_ref, mine_ref, other_ref, relation_ref, acc_ref, new_ref, acc_new_ref):
+def relation_body(
+    core_ref, mine_ref, other_ref, relation_ref, acc_ref, new_ref, acc_new_ref, acc_turned, acc_found
+):
     step, rows, width = relation_ref.shape
+    relations = acc_ref.shape[0]
     at = pl.program_id(0)
     own_half = at // (pl.num_programs(0) // 2) == core_ref[0]
+    lane = lax.broadcasted_iota(jnp.int32, (rows, 128), 1)
+
+    @pl.when(at == 0)
+    def _():
+        short = jnp.zeros((128 - relations, rows), full)
+        acc_turned[...] = jnp.concatenate([acc_ref[...], short], axis=0).T
+        acc_found[...] = jnp.zeros_like(acc_found)
+
     for k in range(step):
-        line = at * step + k
+        here = lane == at * step + k
         mine = mine_ref[:, k].astype(full).reshape(rows, width)
         other = other_ref[:, k].astype(full).reshape(rows, width)
         grad = jnp.where(own_half, mine, other)
-        square = jnp.mean(grad * grad, axis=1, keepdims=True)
-        acc = acc_ref[pl.ds(line, 1), :]
-        acc_new_ref[pl.ds(line, 1), :] = acc + laid(square)
-        rate = step_rate / jnp.sqrt(turned(acc)[:, :1] + square)
-        new_ref[k] = relation_ref[k] - grad * rate
+        square = grad * grad
+        parts = sum(square[:, first : first + 128] for first in range(0, width, 128))
+        acc = jnp.sum(
+            parts * (1.0 / width) + jnp.where(here, acc_turned[...], 0.0), axis=1, keepdims=True
+        )
+        acc_found[...] = jnp.where(here, acc, acc_found[...])
+        new_ref[k] = relation_ref[k] - grad * (step_rate / jnp.sqrt(acc))
+
+    @pl.when(at == pl.num_programs(0) - 1)
+    def _():
+        acc_new_ref[...] = acc_found[...].T[:relations]
 
 
 def entity_body(grad_ref, home_ref, sibling_ref, cross_ref, entity_ref, acc_ref, new_ref, acc_new_ref):
@@ -376,12 +393,13 @@
             grid=(2 * steps,),
             in_specs=[near(0), near(1), block, whole],
             out_specs=[block, whole],
+            scratch_shapes=[pltpu.VMEM((rows, 128), full), pltpu.VMEM((rows, 128), full)],
         ),
         out_shape=[
             jax.ShapeDtypeStruct(relation.shape, full),
             jax.ShapeDtypeStruct(relation_acc.shape, full),
         ],
-        compiler_params=pltpu.CompilerParams(vmem_limit_bytes=VMEM_BYTES),
+        compiler_params=pltpu.CompilerParams(vmem_limit_bytes=16 * MEBI),
     )(core, mine, other, relation, relation_acc)
 
 
@@ -400,7 +418,7 @@
             jax.ShapeDtypeStruct(entity.shape, full),
             jax.ShapeDtypeStruct(entity_acc.shape, full),
         ],
-        compiler_params=pltpu.CompilerParams(vmem_limit_bytes=VMEM_BYTES),
+        compiler_params=pltpu.CompilerParams(vmem_limit_bytes=16 * MEBI),
     )(grad, home, sibling, cross, entity, entity_acc)
 
 
@@ -488,6 +506,7 @@
             pltpu.SemaphoreType.DMA((blocks,)),
         ],
         [SMEM] * 2 + [VMEM] * 5 + [pl.BlockSpec(memory_space=pl.ANY)],
+        mebi=28,
     )(
         rel_ids,
         edge_count,
@@ -508,6 +527,7 @@
         cost(2 * 3 * edges * rows * width, 7 * rows * width * 2),
     )(src_row, neg_src, neg_dst, d_src, d_neg_src, d_neg_dst)
 
+    returned, own_grad, visit_grad = lax.optimization_barrier((returned, own_grad, visit_grad))
     rel_part = call(operators_body, sds((relations, extra, width), full), (), [SMEM, VMEM])(
         asked[:, 1, :blocks], returned[:, room:, :]
     )
@@ -520,8 +540,6 @@
     gathered = lax.all_to_all(
         jnp.broadcast_to(pair[None], (peers,) + pair.shape), "dev", split_axis=0, concat_axis=0, tiled=True
     )
-    other_half = neighbour(gathered, 1)
-
     def home(parts):
         return call(
             functools.partial(home_body, parts),
@@ -535,6 +553,10 @@
     from_cross = neighbour(chip_cross, 2)
     home_sibling, home_own = home((1, 0))
     from_sibling = neighbour(home_sibling, 1)
+    gathered, from_cross, home_own, from_sibling = lax.optimization_barrier(
+        (gathered, from_cross, home_own, from_sibling)
+    )
+    other_half = neighbour(gathered, 1)
     entity_new, acc_new = entity_update(
         own_grad, home_own, from_sibling, from_cross, entity, entity_acc
     )

time: 278 us -> 271 us (0.975); the launches traced: 277 us -> 267 us
  local copies, waits for them, and re-layouts: 15.8 us -> 39.8 us
  Pallas kernels: 107 us -> 88.9 us
  waiting for transfers between devices: 105 us -> 91.5 us
    unnamed x52 -> x78, local copies, waits for them, and re-layouts: 13.4 us -> 37.4 us
    all_to_all x1, waiting for transfers between devices: 32.3 us -> 18.1 us  [on_device(): lax.all_to_all(outgoing, 'dev', split_axis=0, concat_axis=0, tiled=True)]
    ppermute x9, waiting for transfers between devices: 30.9 us -> 44.7 us  [neighbour(): return lax.ppermute(x, 'grp', [(g, g ^ flip) for g in range(4)])]
    all_to_all x1, waiting for transfers between devices: 11.8 us -> 0.01 us  [on_device(): lax.all_to_all(jnp.broadcast_to(pair[None], (peers,) + pair.shape), 'dev'...]
    pallas_call x1, Pallas kernels: 14.2 us -> 10 us  [relation_update(): pl.pallas_call(relation_body, grid_spec=pltpu.PrefetchScalarGridSpec(num_...]
    pallas_call x1, Pallas kernels: 36.5 us -> 32.7 us  [on_device(): call(model_body, (sds((peers, room + blocks * extra, width), half), sds((...]
    pallas_call x2, Pallas kernels: 15.2 us -> 11.7 us  [home(): call(functools.partial(home_body, parts), tuple((sds((rows, width), half)...]
  transfers between devices with their start and end apart: 13 -> 13, of which waited for: 8 -> 7; matrix products, arithmetic and copies ran while one was open for 1% -> 1% of each run, Pallas kernels for 16% -> 13%
where the time goes in v3:
time: 271 us; the launch traced here: 267 us
  waiting for transfers between devices  91.5 us (34%)
  Pallas kernels  88.9 us (33%)
  starting transfers between devices  41.5 us (15%)
  local copies, waits for them, and re-layouts  39.8 us (15%)
  other arithmetic  3.25 us (1%)
    ppermute x9, waiting for transfers between devices, neighbour(): return lax.ppermute(x, 'grp', [(g, g ^ flip) for g in range(4)])  44.7 us
    unnamed x78, local copies, waits for them, and re-layouts  37.4 us
    pallas_call x1, Pallas kernels, on_device(): call(model_body, (sds((peers, room + blocks * extra, width), half), sds((...  32.7 us
    all_to_all x1, waiting for transfers between devices, on_device(): lax.all_to_all(outgoing, 'dev', split_axis=0, concat_axis=0, tiled=True)  18.1 us
    all_to_all x1, waiting for transfers between devices, on_device(): lax.all_to_all(found, 'dev', split_axis=0, concat_axis=0, tiled=True)  14.4 us
    all_to_all x1, waiting for transfers between devices, on_device(): lax.all_to_all(wanted, 'dev', split_axis=0, concat_axis=0, tiled=True)  14.3 us
    ppermute x9, starting transfers between devices, neighbour(): return lax.ppermute(x, 'grp', [(g, g ^ flip) for g in range(4)])  11.8 us
    pallas_call x2, Pallas kernels, home(): call(functools.partial(home_body, parts), tuple((sds((rows, width), half)...  11.7 us
  transfers between devices with their start and end apart: 13, of which 7 were waited for; matrix products, arithmetic and copies ran while one was open for 1% of the time, Pallas kernels for 13%

profile of v3, /device:TPU:1, one launch (start us, length us, event | category | flops | bytes accessed | tf_op | source)
XLA Modules:
  0.0 267.2 jit_solution(4016065112929856657)
XLA Ops:
  2.4 2.2 collective-permute-start
  4.6 2.8 %shard_map.147 = (s32[1,2048]{1,0:T(1,128)S(1)}, s32[32,2,128]{2,1,0:T(2,128)}) custom-call(s32[1,2]{1,0:T(1,128)S(1)} %copy-done.29, s32[1,2048]{1,0:T(1,128)S(1)} %bitcast.20, s32[1,2048]{1,0:T(1,128)S(1)} %copy-done.27), custom_call_target="tpu_custom_call" | custom-call | tf_op jit(solution)/shard_map/pallas_call | solution.py:463
  7.4 10.2 %all-to-all-start = ((s32[32,2,128]{2,1,0:T(2,128)}), s32[32,2,128]{2,1,0:T(2,128)S(1)}, u32[]{:S(2)}, u32[]{:S(2)}) async-start(s32[32,2,128]{2,1,0:T(2,128)} %get-tuple-element.33), calls=%async_computation | async-start | bytes 65536 | tf_op jit(solution)/shard_map/all_to_all | solution.py:468
  19.0 14.3 %all-to-all-done.asked_ref = s32[32,2,128]{2,1,0:T(2,128)S(1)} async-done(((s32[32,2,128]{2,1,0:T(2,128)}), s32[32,2,128]{2,1,0:T(2,128)S(1)}, u32[]{:S(2)}, u32[]{:S(2)}) %all-to-all-start) | async-done | bytes 32800 | tf_op jit(solution)/shard_map/all_to_all | solution.py:468
  33.3 1.9 collective-permute-start.2
  35.1 2.4 collective-permute-done.2.refs_3_
  37.6 10.1 %shard_map.148 = bf16[32,128,256]{2,1,0:T(8,128)(2,1)S(1)} custom-call(s32[4,32]{1,0:T(4,128)S(1)} %copy-done.25, s32[1]{0:T(128)} %bitcast.1.group_ref, s32[32,2,128]{2,1,0:T(2,128)S(1)} %all-to-all-done.asked_ref, bf16[2048,256]{1,0:T(8,128)(2,1)S(1)} %convert_bitcast_fusion.refs_0_, bf16[2048,256]{1,0:T(8,128)(2,1)S(1)} %collective-permute-done.1.refs_1_, ...), custom_call_target="tpu_custom_call" | custom-call | tf_op jit(solution)/shard_map/pallas_call | solution.py:474
  49.0 5.5 %all-to-all-start.1 = ((bf16[32,128,256]{2,1,0:T(8,128)(2,1)}), bf16[32,128,256]{2,1,0:T(8,128)(2,1)S(1)}, u32[]{:S(2)}, u32[]{:S(2)}) async-start(bf16[32,128,256]{2,1,0:T(8,128)(2,1)} %copy-done.5), calls=%async_computation.1 | async-start | bytes 4194304 | tf_op jit(solution)/shard_map/all_to_all | solution.py:480
  58.9 8.0 %shard_map.149 = (bf16[2048,256]{1,0:T(8,128)(2,1)S(1)}, bf16[2048,256]{1,0:T(8,128)(2,1)S(1)}, bf16[2048,256]{1,0:T(8,128)(2,1)S(1)}) custom-call(s32[1]{0:T(128)} %bitcast.5.visit_ref.visit_to_ref, s32[1,2048]{1,0:T(1,128)S(1)} %copy-done.36, s32[2,1024]{1,0:T(2,128)S(1)} %bitcast.21, s32[2,1024]{1,0:T(2,128)S(1)} %bitcast.23, ...), custom_call_target="tpu_custom_call" | custom-call | flops 6442450944 | bytes 6291456 | tf_op jit(solution)/shard_map/pallas_call | solution.py:482
  70.0 14.4 %all-to-all-done.1 = bf16[32,128,256]{2,1,0:T(8,128)(2,1)S(1)} async-done(((bf16[32,128,256]{2,1,0:T(8,128)(2,1)}), bf16[32,128,256]{2,1,0:T(8,128)(2,1)S(1)}, u32[]{:S(2)}, u32[]{:S(2)}) %all-to-all-start.1) | async-done | bytes 2097184 | tf_op jit(solution)/shard_map/all_to_all | solution.py:480
  84.3 4.0 %copy-done = f32[40,256,256]{2,1,0:T(8,128)S(1)} copy-done((f32[40,256,256]{2,1,0:T(8,128)S(1)}, f32[40,256,256]{2,1,0:T(8,128)}, u32[]{:S(2)}) %copy-start) | copy-done | bytes 10485784
  92.0 32.7 %shard_map.150 = (bf16[32,144,256]{2,1,0:T(8,128)(2,1)S(1)}, bf16[2048,256]{1,0:T(8,128)(2,1)S(1)}, bf16[2048,256]{1,0:T(8,128)(2,1)S(1)}, bf16[2048,256]{1,0:T(8,128)(2,1)S(1)}) custom-call(s32[1,2]{1,0:T(1,128)S(1)} %copy-done.29, s32[1,1]{1,0:T(1,128)S(6)} %copy.19.count_ref, s32[1,2048]{1,0:T(1,128)S(1)} %get-tuple-element.32.slot_ref, ...), custom_call_target="tpu_custom_call" | custom-call | tf_op jit(solution)/shard_map/pallas_call | solution.py:490
  129.1 6.7 %all-to-all-start.2 = ((bf16[32,144,256]{2,1,0:T(8,128)(2,1)}), bf16[32,144,256]{2,1,0:T(8,128)(2,1)S(1)}, u32[]{:S(2)}, u32[]{:S(2)}) async-start(bf16[32,144,256]{2,1,0:T(8,128)(2,1)} %copy-done.7), calls=%async_computation.2 | async-start | bytes 4718592 | tf_op jit(solution)/shard_map/all_to_all | solution.py:520
  139.5 7.8 %shard_map.151 = (f32[2048,256]{1,0:T(8,128)S(1)}, f32[2048,256]{1,0:T(8,128)S(1)}) custom-call(s32[1,2048]{1,0:T(1,128)S(1)} %copy-done.36, s32[2,1024]{1,0:T(2,128)S(1)} %bitcast.22, s32[2,1024]{1,0:T(2,128)S(1)} %bitcast.24, bf16[2048,256]{1,0:T(8,128)(2,1)S(1)} %copy-done.31, bf16[2048,256]{1,0:T(8,128)(2,1)S(1)} %copy-done.33, ...), custom_call_target="tpu_custom_call" | custom-call | flops 6442450944 | bytes 7340032 | tf_op jit(solution)/shard_map/pallas_call | solution.py:522
  150.1 18.1 %all-to-all-done.2.returned_ref = bf16[32,144,256]{2,1,0:T(8,128)(2,1)S(1)} async-done(((bf16[32,144,256]{2,1,0:T(8,128)(2,1)}), bf16[32,144,256]{2,1,0:T(8,128)(2,1)S(1)}, u32[]{:S(2)}, u32[]{:S(2)}) %all-to-all-start.2) | async-done | bytes 2359328 | tf_op jit(solution)/shard_map/all_to_all | solution.py:520
  171.7 1.9 collective-permute-start.4
  175.3 7.0 %shard_map.153 = (bf16[2048,256]{1,0:T(8,128)(2,1)}, bf16[2048,256]{1,0:T(8,128)(2,1)S(1)}) custom-call(s32[4,32]{1,0:T(4,128)S(1)} %copy-done.25, s32[1]{0:T(128)} %bitcast.1.group_ref, s32[1]{0:T(128)} %bitcast.5.visit_ref.visit_to_ref, s32[32,2,128]{2,1,0:T(2,128)S(1)} %all-to-all-done.asked_ref, bf16[32,144,256]{2,1,0:T(8,128)(2,1)S(1)} %all-to-all-done.2.returned_ref, ...), custom_call_target="tpu_custom_call" | custom-call | tf_op jit(solution)/shard_map/pallas_call | solution.py:544
  182.2 1.8 broadcast_in_dim.2
  184.0 7.3 %all-to-all-start.3 = ((bf16[32,20,8,256]{3,2,1,0:T(8,128)(2,1)}), bf16[32,20,8,256]{3,2,1,0:T(8,128)(2,1)}, u32[]{:S(2)}, u32[]{:S(2)}) async-start(bf16[32,20,8,256]{3,2,1,0:T(8,128)(2,1)} %broadcast_in_dim.2), calls=%async_computation.3 | async-start | bytes 5242880 | tf_op jit(solution)/shard_map/all_to_all | solution.py:540
  192.9 4.7 %shard_map.154 = (bf16[2048,256]{1,0:T(8,128)(2,1)S(1)}, bf16[2048,256]{1,0:T(8,128)(2,1)S(1)}) custom-call(s32[4,32]{1,0:T(4,128)S(1)} %copy-done.25, s32[1]{0:T(128)} %bitcast.1.group_ref, s32[1]{0:T(128)} %bitcast.5.visit_ref.visit_to_ref, s32[32,2,128]{2,1,0:T(2,128)S(1)} %all-to-all-done.asked_ref, ...), custom_call_target="tpu_custom_call" | custom-call | tf_op jit(solution)/shard_map/pallas_call | solution.py:544
  202.7 40.5 %collective-permute-done.6.cross_ref = bf16[2048,256]{1,0:T(8,128)(2,1)S(1)} collective-permute-done((bf16[2048,256]{1,0:T(8,128)(2,1)S(1)}, bf16[2048,256]{1,0:T(8,128)(2,1)S(1)}, u32[]{:S(2)}, u32[]{:S(2)}) %collective-permute-start.6) | collective-permute-done | bytes 1048608 | tf_op jit(solution)/shard_map/ppermute | solution.py:452
  248.7 4.5 %shard_map.155 = (f32[1,2048,256]{2,1,0:T(8,128)}, f32[1,2048]{1,0:T(1,128)}) custom-call(f32[2048,256]{1,0:T(8,128)S(1)} %copy-done.9, bf16[2048,256]{1,0:T(8,128)(2,1)S(1)} %copy-done.21, bf16[2048,256]{1,0:T(8,128)(2,1)S(1)} %copy-done.23, bf16[2048,256]{1,0:T(8,128)(2,1)S(1)} %collective-permute-done.6.cross_ref, f32[1,2048,256]{2,1,0:T(8,128)S(1)} %copy-done.6, ...), custom_call_target="tpu_custom_call" | custom-call | tf_op jit(solution)/shard_map/pallas_call | solution.py:412
  253.2 4.0 %copy-done.1 = f32[40,256,256]{2,1,0:T(8,128)S(1)} copy-done((f32[40,256,256]{2,1,0:T(8,128)S(1)}, f32[40,256,256]{2,1,0:T(8,128)}, u32[]{:S(2)}) %copy-start.1) | copy-done | bytes 10485784
  257.2 10.0 %shard_map.156 = (f32[40,256,256]{2,1,0:T(8,128)}, f32[40,256]{1,0:T(8,128)}) custom-call(s32[1]{0:T(128)} %bitcast.12.core_ref, bf16[32,20,8,256]{3,2,1,0:T(8,128)(2,1)} %all-to-all-done.3.mine_ref, bf16[32,20,8,256]{3,2,1,0:T(8,128)(2,1)S(1)} %collective-permute-done.8.other_ref, f32[40,256,256]{2,1,0:T(8,128)S(1)} %copy-done.1, f32[40,256]{1,0:T(8,128)S(1)} %copy-done.24), custom_call_target="tpu_custom_call" | custom-call | tf_op jit(solution)/shard_map/pallas_call | solution.py:389
  (99 shorter events, 42.0 us)
Async XLA Ops:
  0.7 36.9 %copy-start.25 = (s32[4,32]{1,0:T(4,128)S(1)}, s32[4,32]{1,0:T(4,128)}, u32[]{:S(2)}) copy-start(s32[4,32]{1,0:T(4,128)} %partner_ref.5) | copy-start | bytes 1540
  2.4 30.9 %collective-permute-start = (bf16[2048,256]{1,0:T(8,128)(2,1)S(1)}, bf16[2048,256]{1,0:T(8,128)(2,1)S(1)}, u32[]{:S(2)}, u32[]{:S(2)}) collective-permute-start(bf16[2048,256]{1,0:T(8,128)(2,1)S(1)} %convert_bitcast_fusion.refs_0_), channel_id=1, source_target_pairs={{0,64},{32,96},{64,0},{96,32},{1,65},{33,97},{65,1},{97,33},{2,66}... | collective-permute-start | bytes 3145736 | tf_op jit(solution)/shard_map/ppermute | solution.py:452
  7.4 25.8 %all-to-all-start = ((s32[32,2,128]{2,1,0:T(2,128)}), s32[32,2,128]{2,1,0:T(2,128)S(1)}, u32[]{:S(2)}, u32[]{:S(2)}) async-start(s32[32,2,128]{2,1,0:T(2,128)} %get-tuple-element.33), calls=%async_computation | async-start | bytes 65536 | tf_op jit(solution)/shard_map/all_to_all | solution.py:468
  17.7 17.5 %collective-permute-start.1 = (bf16[2048,256]{1,0:T(8,128)(2,1)S(1)}, bf16[2048,256]{1,0:T(8,128)(2,1)S(1)}, u32[]{:S(2)}, u32[]{:S(2)}) collective-permute-start(bf16[2048,256]{1,0:T(8,128)(2,1)S(1)} %convert_bitcast_fusion.refs_0_), channel_id=1, source_target_pairs={{0,32},{32,0},{64,96},{96,64},{1,33},{33,1},{65,97},{97,65},{2,34}... | collective-permute-start | bytes 3145736 | tf_op jit(solution)/shard_map/ppermute | solution.py:452
  33.3 14.4 %copy-start.16 = (bf16[2048,256]{1,0:T(8,128)(2,1)}, bf16[2048,256]{1,0:T(8,128)(2,1)S(1)}, u32[]{:S(2)}) copy-start(bf16[2048,256]{1,0:T(8,128)(2,1)S(1)} %collective-permute-done.refs_2_) | copy-start | bytes 3145732
  33.3 4.3 %collective-permute-start.2 = (bf16[2048,256]{1,0:T(8,128)(2,1)S(1)}, bf16[2048,256]{1,0:T(8,128)(2,1)}, u32[]{:S(2)}, u32[]{:S(2)}) collective-permute-start(bf16[2048,256]{1,0:T(8,128)(2,1)S(1)} %collective-permute-done.refs_2_), channel_id=1, source_target_pairs={{0,32},{32,0},{64,96},{96,64},{1,33},{33,1},{65,97},{97,65},{2,34}... | collective-permute-start | bytes 3145736 | tf_op jit(solution)/shard_map/ppermute | solution.py:452
  35.1 12.5 %copy-start.18 = (bf16[2048,256]{1,0:T(8,128)(2,1)}, bf16[2048,256]{1,0:T(8,128)(2,1)S(1)}, u32[]{:S(2)}) copy-start(bf16[2048,256]{1,0:T(8,128)(2,1)S(1)} %collective-permute-done.1.refs_1_) | copy-start | bytes 3145732
  49.0 7.4 %copy-start.36 = (s32[1,2048]{1,0:T(1,128)S(1)}, s32[1,2048]{1,0:T(1,128)}, u32[]{:S(2)}) copy-start(s32[1,2048]{1,0:T(1,128)} %src_ref.3) | copy-start | bytes 24580
  49.0 7.4 %copy-start.37 = (s32[1,2,1024]{2,1,0:T(2,128)S(1)}, s32[1,2,1024]{2,1,0:T(2,128)}, u32[]{:S(2)}) copy-start(s32[1,2,1024]{2,1,0:T(2,128)} %param.21) | copy-start | bytes 24580
  49.0 7.4 %copy-start.38 = (s32[1,2,1024]{2,1,0:T(2,128)S(1)}, s32[1,2,1024]{2,1,0:T(2,128)}, u32[]{:S(2)}) copy-start(s32[1,2,1024]{2,1,0:T(2,128)} %param.22) | copy-start | bytes 24580
  49.0 35.3 %all-to-all-start.1 = ((bf16[32,128,256]{2,1,0:T(8,128)(2,1)}), bf16[32,128,256]{2,1,0:T(8,128)(2,1)S(1)}, u32[]{:S(2)}, u32[]{:S(2)}) async-start(bf16[32,128,256]{2,1,0:T(8,128)(2,1)} %copy-done.5), calls=%async_computation.1 | async-start | bytes 4194304 | tf_op jit(solution)/shard_map/all_to_all | solution.py:480
  84.3 4.0 %copy-start = (f32[40,256,256]{2,1,0:T(8,128)S(1)}, f32[40,256,256]{2,1,0:T(8,128)}, u32[]{:S(2)}) copy-start(f32[40,256,256]{2,1,0:T(8,128)} %relation_ref.3) | copy-start | bytes 31457284
  129.1 39.1 %all-to-all-start.2 = ((bf16[32,144,256]{2,1,0:T(8,128)(2,1)}), bf16[32,144,256]{2,1,0:T(8,128)(2,1)S(1)}, u32[]{:S(2)}, u32[]{:S(2)}) async-start(bf16[32,144,256]{2,1,0:T(8,128)(2,1)} %copy-done.7), calls=%async_computation.2 | async-start | bytes 4718592 | tf_op jit(solution)/shard_map/all_to_all | solution.py:520
  169.4 2.3 collective-permute-start.3
  171.7 10.5 %collective-permute-start.4 = (f32[20,8,256]{2,1,0:T(8,128)S(1)}, f32[20,8,256]{2,1,0:T(8,128)S(1)}, u32[]{:S(2)}, u32[]{:S(2)}) collective-permute-start(f32[20,8,256]{2,1,0:T(8,128)S(1)} %bitcast_add_fusion), channel_id=1, source_target_pairs={{0,64},{32,96},{64,0},{96,32},{1,65},{33,97},{65,1},{97,33},{2,66}... | collective-permute-start | bytes 491528 | tf_op jit(solution)/shard_map/ppermute | solution.py:452
  182.2 17.2 %collective-permute-start.5 = (bf16[2048,256]{1,0:T(8,128)(2,1)}, bf16[2048,256]{1,0:T(8,128)(2,1)}, u32[]{:S(2)}, u32[]{:S(2)}) collective-permute-start(bf16[2048,256]{1,0:T(8,128)(2,1)} %get-tuple-element.49), channel_id=1, source_target_pairs={{0,32},{32,0},{64,96},{96,64},{1,33},{33,1},{65,97},{97,65},{2,34}... | collective-permute-start | bytes 3145736 | tf_op jit(solution)/shard_map/ppermute | solution.py:452
  184.0 59.2 %all-to-all-start.3 = ((bf16[32,20,8,256]{3,2,1,0:T(8,128)(2,1)}), bf16[32,20,8,256]{3,2,1,0:T(8,128)(2,1)}, u32[]{:S(2)}, u32[]{:S(2)}) async-start(bf16[32,20,8,256]{3,2,1,0:T(8,128)(2,1)} %broadcast_in_dim.2), calls=%async_computation.3 | async-start | bytes 5242880 | tf_op jit(solution)/shard_map/all_to_all | solution.py:540
  197.6 47.0 %copy-start.6 = (f32[1,2048,256]{2,1,0:T(8,128)S(1)}, f32[1,2048,256]{2,1,0:T(8,128)}, u32[]{:S(2)}) copy-start(f32[1,2048,256]{2,1,0:T(8,128)} %entity_ref.1) | copy-start | bytes 6291460
  197.7 47.0 %copy-start.28 = (f32[1,2048]{1,0:T(1,128)S(1)}, f32[1,2048]{1,0:T(1,128)}, u32[]{:S(2)}) copy-start(f32[1,2048]{1,0:T(1,128)} %acc_ref.2) | copy-start | bytes 24580
  197.7 4.0 %collective-permute-start.7 = (bf16[2048,256]{1,0:T(8,128)(2,1)S(1)}, bf16[2048,256]{1,0:T(8,128)(2,1)S(1)}, u32[]{:S(2)}, u32[]{:S(2)}) collective-permute-start(bf16[2048,256]{1,0:T(8,128)(2,1)S(1)} %get-tuple-element.51), channel_id=1, source_target_pairs={{0,32},{32,0},{64,96},{96,64},{1,33},{33,1},{65,97},{97,65},{2,34}... | collective-permute-start | bytes 3145736 | tf_op jit(solution)/shard_map/ppermute | solution.py:452
  200.9 42.3 %collective-permute-start.6 = (bf16[2048,256]{1,0:T(8,128)(2,1)S(1)}, bf16[2048,256]{1,0:T(8,128)(2,1)S(1)}, u32[]{:S(2)}, u32[]{:S(2)}) collective-permute-start(bf16[2048,256]{1,0:T(8,128)(2,1)S(1)} %add_convert_fusion), channel_id=1, source_target_pairs={{0,64},{32,96},{64,0},{96,32},{1,65},{33,97},{65,1},{97,33},{2,66}... | collective-permute-start | bytes 3145736 | tf_op jit(solution)/shard_map/ppermute | solution.py:452
  243.3 9.9 %collective-permute-start.8 = (bf16[32,20,8,256]{3,2,1,0:T(8,128)(2,1)}, bf16[32,20,8,256]{3,2,1,0:T(8,128)(2,1)S(1)}, u32[]{:S(2)}, u32[]{:S(2)}) collective-permute-start(bf16[32,20,8,256]{3,2,1,0:T(8,128)(2,1)} %all-to-all-done.3.mine_ref), channel_id=1, source_target_pairs={{0,32},{32,0},{64,96},{96,64},{1,33},{33,1},{65,97},{97,65},{2,34}... | collective-permute-start | bytes 7864328 | tf_op jit(solution)/shard_map/ppermute | solution.py:452
  248.7 4.5 %copy-start.24 = (f32[40,256]{1,0:T(8,128)S(1)}, f32[40,256]{1,0:T(8,128)}, u32[]{:S(2)}) copy-start(f32[40,256]{1,0:T(8,128)} %acc_ref.3) | copy-start | bytes 122884
  253.2 4.0 %copy-start.1 = (f32[40,256,256]{2,1,0:T(8,128)S(1)}, f32[40,256,256]{2,1,0:T(8,128)}, u32[]{:S(2)}) copy-start(f32[40,256,256]{2,1,0:T(8,128)} %relation_ref.3) | copy-start | bytes 31457284
  (28 other events, 44.6 us)

commit v4 on v3

--- a/solution.py
+++ b/solution.py
@@ -13,6 +13,7 @@
 full = jnp.float32
 VMEM = pl.BlockSpec(memory_space=pltpu.VMEM)
 SMEM = pl.BlockSpec(memory_space=pltpu.SMEM)
+ANY = pl.BlockSpec(memory_space=pl.ANY)
 
 
 def dot(a, b, ca, cb):
@@ -40,12 +41,12 @@
     return jnp.where(row == line, 1.0, 0.0).astype(half)
 
 
-def call(body, outs, scratch=(), specs=None, cost=None, mebi=16, **kw):
+def call(body, shapes, scratch=(), specs=None, cost=None, outs=None, mebi=60, **kw):
     return pl.pallas_call(
         body,
-        out_shape=outs,
+        out_shape=shapes,
         in_specs=specs,
-        out_specs=jax.tree.map(lambda _: VMEM, outs),
+        out_specs=outs or jax.tree.map(lambda _: VMEM, shapes),
         scratch_shapes=list(scratch),
         compiler_params=pltpu.CompilerParams(vmem_limit_bytes=mebi * MEBI),
         cost_estimate=cost,
@@ -126,30 +127,88 @@
         lax.fori_loop(0, (count + 1) // 2, pair, 0)
 
 
-def rows_body(visit_ref, src_ref, neg_src_ref, neg_dst_ref, *refs):
-    tables, (src_out, neg_src_out, neg_dst_out, visit) = refs[:4], refs[4:]
-    rows = tables[0].shape[0]
-    for part in range(4):
+def operators_in(rel_ref, relation_ref, operator, sems):
+    copies = [
+        pltpu.make_async_copy(relation_ref.at[rel_ref[0, block]], operator.at[block], sems.at[block])
+        for block in range(rel_ref.shape[1])
+    ]
+    for copy in copies:
+        copy.start()
+    return copies
+
+
+def front_body(
+    rel_ref,
+    visit_ref,
+    src_ref,
+    neg_src_ref,
+    neg_dst_ref,
+    relation_ref,
+    own_table,
+    sibling_table,
+    cross_table,
+    cross_sibling_table,
+    src_out,
+    neg_src_out,
+    lhs_out,
+    terms_out,
+    pull_out,
+    stats_out,
+    own,
+    visit,
+    neg_dst,
+    operator,
+    op_sems,
+    own_sem,
+    visit_sem,
+):
+    rows = own.shape[0]
+    blocks, negs = neg_src_ref.shape
+    edges = src_ref.shape[1]
+    block_len = edges // blocks
+    step = 256
+    op_copies = operators_in(rel_ref, relation_ref, operator, op_sems)
+    own_copy = pltpu.make_async_copy(own_table, own, own_sem)
+    own_copy.start()
+    for part, table in enumerate((own_table, sibling_table, cross_table, cross_sibling_table)):
 
         @pl.when(visit_ref[0] == part)
-        def _(part=part):
-            visit[...] = tables[part][...]
-
-    step = 256
-    blocks, negs = neg_src_ref.shape
-    for at in range(0, src_ref.shape[1], step):
-        src_out[at : at + step] = dot(
-            pick(src_ref[:, at : at + step], rows), tables[0][...], 1, 0
-        ).astype(half)
+        def _(table=table):
+            pltpu.make_async_copy(table, visit, visit_sem).start()
+
+    own_copy.wait()
+    pltpu.make_async_copy(own_table, visit, visit_sem).wait()
+    for copy in op_copies:
+        copy.wait()
     for block in range(blocks):
         for at in range(0, negs, step):
             to = block * negs + at
             neg_src_out[to : to + step] = dot(
-                pick(neg_src_ref[block : block + 1, at : at + step], rows), tables[0][...], 1, 0
+                pick(neg_src_ref[block : block + 1, at : at + step], rows), own[...], 1, 0
             ).astype(half)
-            neg_dst_out[to : to + step] = dot(
+            neg_dst[at : at + step] = dot(
                 pick(neg_dst_ref[block : block + 1, at : at + step], rows), visit[...], 1, 0
             ).astype(half)
+
+        def chunk(t, carry, block=block):
+            at = pl.multiple_of(block * block_len + t * step, step)
+            here = pl.ds(at, step)
+            op = operator[block].astype(half)
+            src = dot(pick(src_ref[:, here], rows), own[...], 1, 0).astype(half)
+            lhs = dot(src, op, 1, 0).astype(half)
+            scores = dot(lhs, neg_dst[...], 1, 1)
+            highest = jnp.max(scores, axis=1, keepdims=True)
+            terms = jnp.exp(scores - highest)
+            lane = lax.broadcasted_iota(jnp.int32, (step, 128), 1)
+            stats_out[here, :] = jnp.where(lane < 64, highest, jnp.sum(terms, axis=1, keepdims=True))
+            terms = terms.astype(half)
+            src_out[here, :] = src
+            lhs_out[here, :] = lhs
+            terms_out[here, :] = terms
+            pull_out[here, :] = dot(terms, neg_dst[...], 1, 0)
+            return carry
+
+        lax.fori_loop(0, block_len // step, chunk, 0, unroll=2)
 
 
 def model_body(
@@ -157,25 +216,39 @@
     count_ref,
     slot_ref,
     fetched_ref,
+    relation_ref,
+    src_in,
+    neg_src_in,
+    lhs_in,
+    terms_in,
+    pull_in,
+    stats_in,
+    outgoing_ref,
+    d_src_out,
+    d_neg_src_out,
+    d_neg_dst_out,
     src_ref,
     neg_src_ref,
-    neg_dst_ref,
-    relation_ref,
-    outgoing_ref,
+    lhs_ref,
+    terms_ref,
+    pull_ref,
+    stats_ref,
     d_src_ref,
     d_neg_src_ref,
     d_neg_dst_ref,
+    dst_ref,
     d_dst,
     operator,
-    op_half,
     neg_dst_sum,
     neg_src_sum,
     op_sum,
     op_turned_sum,
-    op_sem,
+    op_sems,
+    in_sems,
+    out_sems,
 ):
     slots, width = fetched_ref.shape
-    edges = src_ref.shape[0]
+    edges = slot_ref.shape[1]
     blocks = rel_ref.shape[1]
     block_len = edges // blocks
     negs = neg_src_ref.shape[0] // blocks
@@ -183,17 +256,28 @@
     extra = width // peers
     places = slots // peers
     step = 256
-    copies = []
+    copies = operators_in(rel_ref, relation_ref, operator, op_sems)
+    pairs = (
+        (src_in, src_ref),
+        (neg_src_in, neg_src_ref),
+        (lhs_in, lhs_ref),
+        (pull_in, pull_ref),
+        (stats_in, stats_ref),
+        (terms_in, terms_ref),
+    )
+    for i, (there, here) in enumerate(pairs):
+        copies.append(pltpu.make_async_copy(there, here, in_sems.at[i]))
+        copies[-1].start()
+
+    def fetch(t, carry):
+        here = pl.ds(pl.multiple_of(t * step, step), step)
+        dst_ref[here, :] = dot(pick(slot_ref[:, here], slots), fetched_ref[...], 1, 0).astype(half)
+        return carry
+
+    lax.fori_loop(0, edges // step, fetch, 0, unroll=4)
+    for copy in copies:
+        copy.wait()
     for block in range(blocks):
-        copies.append(
-            pltpu.make_async_copy(
-                relation_ref.at[rel_ref[0, block]], operator.at[block], op_sem.at[block]
-            )
-        )
-        copies[-1].start()
-    for block in range(blocks):
-        copies[block].wait()
-        op_half[...] = operator[block].astype(half)
         neg_dst_sum[...] = jnp.zeros_like(neg_dst_sum)
         neg_src_sum[...] = jnp.zeros_like(neg_src_sum)
         op_sum[...] = jnp.zeros_like(op_sum)
@@ -202,32 +286,38 @@
         def chunk(t, carry, block=block):
             at = pl.multiple_of(block * block_len + t * step, step)
             here = pl.ds(at, step)
-            op = op_half[...]
-            dst = dot(pick(slot_ref[:, here], slots), fetched_ref[...], 1, 0).astype(half)
+            op = operator[block].astype(half)
+            dst = dst_ref[here, :]
             src = src_ref[here, :]
-            negs_at = pl.ds(block * negs, negs)
-            neg_dst = neg_dst_ref[negs_at, :]
-            neg_src = neg_src_ref[negs_at, :]
+            lhs = lhs_ref[here, :]
+            neg_src = neg_src_ref[block * negs : (block + 1) * negs, :]
             line = lax.broadcasted_iota(jnp.int32, (step, 1), 0) + at
             live = jnp.where(line < count_ref[0, 0], 1.0, 0.0)
-            lhs = dot(src, op, 1, 0).astype(half)
             rhs = dot(dst, op, 1, 1).astype(half)
             positive = jnp.sum(lhs.astype(full) * dst.astype(full), axis=1, keepdims=True)
 
-            def softmax(scores):
-                highest = jnp.maximum(jnp.max(scores, axis=1, keepdims=True), positive)
-                terms = jnp.exp(scores - highest)
-                own = jnp.exp(positive - highest)
-                scale = live / (own + jnp.sum(terms, axis=1, keepdims=True))
-                return (terms * scale).astype(half), own * scale - live
-
-            dst_terms, dst_own = softmax(dot(lhs, neg_dst, 1, 1))
-            src_terms, src_own = softmax(dot(rhs, neg_src, 1, 1))
-            d_positive = dst_own + src_own
-            d_lhs = dot(dst_terms, neg_dst, 1, 0).astype(half)
+            scores = dot(rhs, neg_src, 1, 1)
+            highest = jnp.maximum(jnp.max(scores, axis=1, keepdims=True), positive)
+            terms = jnp.exp(scores - highest)
+            own = jnp.exp(positive - highest)
+            scale = live / (own + jnp.sum(terms, axis=1, keepdims=True))
+            src_terms = (terms * scale).astype(half)
+            d_positive = own * scale - live
+
+            top = stats_ref[here, :]
+            top, total = top[:, :1], top[:, 64:65]
+            highest = jnp.maximum(top, positive)
+            lower = jnp.exp(top - highest)
+            own = jnp.exp(positive - highest)
+            scale = live / (own + total * lower)
+            d_positive += own * scale - live
+            scale = lower * scale
+
+            d_lhs = (pull_ref[here, :] * scale).astype(half)
             d_lhs = d_lhs + (d_positive * dst.astype(full)).astype(half)
             d_rhs = dot(src_terms, neg_src, 1, 0).astype(half)
-            neg_dst_sum[...] += dot(lhs, dst_terms, 0, 0)
+            scaled = (lhs.astype(full) * scale).astype(half)
+            neg_dst_sum[...] += dot(scaled, terms_ref[here, :], 0, 0)
             neg_src_sum[...] += dot(rhs, src_terms, 0, 0)
             d_src_ref[here, :] = dot(d_lhs, op, 1, 1).astype(half)
             op_sum[...] += dot(src, d_lhs, 0, 0)
@@ -237,13 +327,19 @@
             ).astype(half)
             return carry
 
-        lax.fori_loop(0, block_len // step, chunk, 0)
+        lax.fori_loop(0, block_len // step, chunk, 0, unroll=4)
         d_neg_dst_ref[block * negs : (block + 1) * negs, :] = neg_dst_sum[...].T.astype(half)
         d_neg_src_ref[block * negs : (block + 1) * negs, :] = neg_src_sum[...].T.astype(half)
         d_op = op_sum[...].astype(half) + op_turned_sum[...].astype(half)
         outgoing_ref[:, places + block * extra : places + (block + 1) * extra, :] = d_op.reshape(
             peers, extra, width
         )
+    backs = []
+    for i, (here, there) in enumerate(
+        ((d_src_ref, d_src_out), (d_neg_src_ref, d_neg_src_out), (d_neg_dst_ref, d_neg_dst_out))
+    ):
+        backs.append(pltpu.make_async_copy(here, there, out_sems.at[i]))
+        backs[-1].start()
 
     def send(t, carry):
         spot = place(slot_ref[...], t * 2 * places, 2 * places)
@@ -251,7 +347,73 @@
         outgoing_ref[pl.ds(2 * t, 2), :places, :] = out.reshape(2, places, width)
         return carry
 
-    lax.fori_loop(0, peers // 2, send, 0)
+    lax.fori_loop(0, peers // 2, send, 0, unroll=4)
+    for copy in backs:
+        copy.wait()
+
+
+def front(rel_ids, visit_to, src_row, neg_src, neg_dst, relation, tables):
+    rows, width = tables[0].shape
+    edges = src_row.shape[1]
+    blocks, negs = neg_src.shape
+    sds = jax.ShapeDtypeStruct
+    return call(
+        front_body,
+        (
+            sds((edges, width), half),
+            sds((blocks * negs, width), half),
+            sds((edges, width), half),
+            sds((edges, negs), half),
+            sds((edges, width), full),
+            sds((edges, 128), full),
+        ),
+        [
+            pltpu.VMEM((rows, width), half),
+            pltpu.VMEM((rows, width), half),
+            pltpu.VMEM((negs, width), half),
+            pltpu.VMEM((blocks, width, width), full),
+            pltpu.SemaphoreType.DMA((blocks,)),
+            pltpu.SemaphoreType.DMA,
+            pltpu.SemaphoreType.DMA,
+        ],
+        [SMEM] * 2 + [VMEM] * 3 + [ANY] * 5,
+        cost(2 * edges * width * (3 * rows + 2 * negs), 12 * MEBI),
+    )(rel_ids, visit_to, src_row, neg_src, neg_dst, relation, *tables)
+
+
+def model(rel_ids, edge_count, slot, fetched, relation, peers, room, rest):
+    slots, width = fetched.shape
+    edges = slot.shape[1]
+    blocks = rel_ids.shape[1]
+    negs = rest[1].shape[0] // blocks
+    sds = jax.ShapeDtypeStruct
+    return call(
+        model_body,
+        (
+            sds((peers, room + blocks * (width // peers), width), half),
+            sds((edges, width), half),
+            sds((blocks * negs, width), half),
+            sds((blocks * negs, width), half),
+        ),
+        [pltpu.VMEM(x.shape, x.dtype) for x in rest]
+        + [
+            pltpu.VMEM((edges, width), half),
+            pltpu.VMEM((blocks * negs, width), half),
+            pltpu.VMEM((blocks * negs, width), half),
+            pltpu.VMEM((edges, width), half),
+            pltpu.VMEM((edges, width), half),
+            pltpu.VMEM((blocks, width, width), full),
+            pltpu.VMEM((width, negs), full),
+            pltpu.VMEM((width, negs), full),
+            pltpu.VMEM((width, width), full),
+            pltpu.VMEM((width, width), full),
+            pltpu.SemaphoreType.DMA((blocks,)),
+            pltpu.SemaphoreType.DMA((6,)),
+            pltpu.SemaphoreType.DMA((3,)),
+        ],
+        [SMEM] * 2 + [VMEM] * 2 + [ANY] * 7,
+        outs=[VMEM] + [ANY] * 3,
+    )(rel_ids, edge_count, slot, fetched, relation, *rest)
 
 
 def sums_body(src_ref, neg_src_ref, neg_dst_ref, d_src, d_neg_src, d_neg_dst, own_ref, visit_ref):
@@ -399,7 +561,7 @@
             jax.ShapeDtypeStruct(relation.shape, full),
             jax.ShapeDtypeStruct(relation_acc.shape, full),
         ],
-        compiler_params=pltpu.CompilerParams(vmem_limit_bytes=16 * MEBI),
+        compiler_params=pltpu.CompilerParams(vmem_limit_bytes=60 * MEBI),
     )(core, mine, other, relation, relation_acc)
 
 
@@ -418,7 +580,7 @@
             jax.ShapeDtypeStruct(entity.shape, full),
             jax.ShapeDtypeStruct(entity_acc.shape, full),
         ],
-        compiler_params=pltpu.CompilerParams(vmem_limit_bytes=16 * MEBI),
+        compiler_params=pltpu.CompilerParams(vmem_limit_bytes=60 * MEBI),
     )(grad, home, sibling, cross, entity, entity_acc)
 
 
@@ -479,43 +641,9 @@
     )(partner, group, asked, *tables)
     fetched = lax.all_to_all(found, "dev", split_axis=0, concat_axis=0, tiled=True)
 
-    src_rows, neg_src_rows, neg_dst_rows = call(
-        rows_body,
-        (sds((edges, width), half), sds((blocks * negs, width), half), sds((blocks * negs, width), half)),
-        [pltpu.VMEM((rows, width), half)],
-        [SMEM] + [VMEM] * 7,
-        cost(2 * 3 * edges * rows * width, 6 * rows * width * 2),
-    )(visit_to, src_row, neg_src, neg_dst, *tables)
-
-    outgoing, d_src, d_neg_src, d_neg_dst = call(
-        model_body,
-        (
-            sds((peers, room + blocks * extra, width), half),
-            sds((edges, width), half),
-            sds((blocks * negs, width), half),
-            sds((blocks * negs, width), half),
-        ),
-        [
-            pltpu.VMEM((edges, width), half),
-            pltpu.VMEM((blocks, width, width), full),
-            pltpu.VMEM((width, width), half),
-            pltpu.VMEM((width, negs), full),
-            pltpu.VMEM((width, negs), full),
-            pltpu.VMEM((width, width), full),
-            pltpu.VMEM((width, width), full),
-            pltpu.SemaphoreType.DMA((blocks,)),
-        ],
-        [SMEM] * 2 + [VMEM] * 5 + [pl.BlockSpec(memory_space=pl.ANY)],
-        mebi=28,
-    )(
-        rel_ids,
-        edge_count,
-        slot,
-        fetched.reshape(peers * room, width),
-        src_rows,
-        neg_src_rows,
-        neg_dst_rows,
-        relation,
+    rest = front(rel_ids, visit_to, src_row, neg_src, neg_dst, relation, tables)
+    outgoing, d_src, d_neg_src, d_neg_dst = model(
+        rel_ids, edge_count, slot, fetched.reshape(peers * room, width), relation, peers, room, rest
     )
     returned = lax.all_to_all(outgoing, "dev", split_axis=0, concat_axis=0, tiled=True)
 
@@ -537,10 +665,20 @@
     other = lax.dynamic_index_in_dim(halves, 1 - core, 0, keepdims=False)
     chip = mine + neighbour(other, 1)
     pair = (chip + neighbour(chip, 2)).astype(half)
+    near = lax.ppermute(pair, "dev", [(d, d ^ 1) for d in range(peers)])
+    low = (place_id & 1) == 0
+    planes = jnp.stack([jnp.where(low, pair, near), jnp.where(low, near, pair)])
+    planes, returned_later = lax.optimization_barrier((planes, returned))
     gathered = lax.all_to_all(
-        jnp.broadcast_to(pair[None], (peers,) + pair.shape), "dev", split_axis=0, concat_axis=0, tiled=True
-    )
-    def home(parts):
+        jnp.broadcast_to(planes[None], (peers // 2,) + planes.shape),
+        "dev",
+        split_axis=0,
+        concat_axis=0,
+        axis_index_groups=[list(range(k, peers, 2)) for k in range(2)],
+        tiled=True,
+    ).reshape((peers,) + pair.shape)
+
+    def home(parts, returned):
         return call(
             functools.partial(home_body, parts),
             tuple(sds((rows, width), half) for _ in parts),
@@ -548,10 +686,10 @@
             [SMEM] * 3 + [VMEM] * 3,
         )(partner, group, visit_to, asked, returned, visit_grad)
 
-    home_cross_sibling, home_cross = home((3, 2))
+    home_cross_sibling, home_cross = home((3, 2), returned)
     chip_cross = (home_cross.astype(full) + neighbour(home_cross_sibling, 1).astype(full)).astype(half)
     from_cross = neighbour(chip_cross, 2)
-    home_sibling, home_own = home((1, 0))
+    home_sibling, home_own = home((1, 0), returned_later)
     from_sibling = neighbour(home_sibling, 1)
     gathered, from_cross, home_own, from_sibling = lax.optimization_barrier(
         (gathered, from_cross, home_own, from_sibling)

time: 271 us -> 242 us (0.89)
  local copies, waits for them, and re-layouts: 39.8 us -> 7.71 us
  Pallas kernels: 88.9 us -> 112 us
  waiting for transfers between devices: 91.5 us -> 71.6 us
    unnamed x78 -> x18, local copies, waits for them, and re-layouts: 37.4 us -> 2.34 us
    ppermute x9, waiting for transfers between devices: 44.7 us -> 31 us  [neighbour(): return lax.ppermute(x, 'grp', [(g, g ^ flip) for g in range(4)])]
    all_to_all x1, waiting for transfers between devices: 14.4 us -> 6.84 us  [on_device(): lax.all_to_all(found, 'dev', split_axis=0, concat_axis=0, tiled=True)]
    pallas_call x2, Pallas kernels: 11.7 us -> 16.8 us  [home(): call(functools.partial(home_body, parts), tuple((sds((rows, width), half)...]
    pallas_call x1, Pallas kernels: 10 us -> 14.2 us  [relation_update(): pl.pallas_call(relation_body, grid_spec=pltpu.PrefetchScalarGridSpec(num_...]
    pallas_call x1, Pallas kernels: 7.84 us -> 11.8 us  [on_device(): call(sums_body, (sds((rows, width), full), sds((rows, width), full)), (),...]
    pallas_call x1, Pallas kernels: 4.49 us -> 7.88 us  [entity_update(): pl.pallas_call(entity_body, grid=(rows // step,), in_specs=[part] * 4 + [...]
    pallas_call x2, Pallas kernels: 40.7 us -> 44 us  [the longest x1 23.9 us: model(): call(model_body, (sds((peers, room + blocks * (width // peers), width), h...]
  transfers between devices with their start and end apart: 13 -> 14, of which waited for: 7 -> 8; matrix products, arithmetic and copies ran while one was open for 1% -> 2% of each run, Pallas kernels for 13% -> 25%
where the time goes in v4:
time: 242 us; the launch traced here: 240 us
  Pallas kernels  112 us (46%)
  waiting for transfers between devices  71.6 us (30%)
  starting transfers between devices  42.1 us (17%)
  local copies, waits for them, and re-layouts  7.71 us (3%)
  other arithmetic  4.49 us (2%)
    ppermute x9, waiting for transfers between devices, neighbour(): return lax.ppermute(x, 'grp', [(g, g ^ flip) for g in range(4)])  31 us
    pallas_call x1, Pallas kernels, model(): call(model_body, (sds((peers, room + blocks * (width // peers), width), h...  23.9 us
    pallas_call x1, Pallas kernels, front(): call(front_body, (sds((edges, width), half), sds((blocks * negs, width),...  20.2 us
    all_to_all x1, waiting for transfers between devices, on_device(): lax.all_to_all(outgoing, 'dev', split_axis=0, concat_axis=0, tiled=True)  19.7 us
    pallas_call x2, Pallas kernels, home(): call(functools.partial(home_body, parts), tuple((sds((rows, width), half)...  16.8 us
    pallas_call x1, Pallas kernels, relation_update(): pl.pallas_call(relation_body, grid_spec=pltpu.PrefetchScalarGridSpec(num_...  14.2 us
    all_to_all x1, waiting for transfers between devices, on_device(): lax.all_to_all(wanted, 'dev', split_axis=0, concat_axis=0, tiled=True)  14.1 us
    ppermute x9, starting transfers between devices, neighbour(): return lax.ppermute(x, 'grp', [(g, g ^ flip) for g in range(4)])  12.5 us
  transfers between devices with their start and end apart: 14, of which 8 were waited for; matrix products, arithmetic and copies ran while one was open for 2% of the time, Pallas kernels for 25%

profile of v4, /device:TPU:1, one launch (start us, length us, event | category | flops | bytes accessed | tf_op | source)
XLA Modules:
  0.0 240.3 jit_solution(5014598413839142458)
XLA Ops:
  2.3 2.2 collective-permute-start
  4.5 3.0 %shard_map.147 = (s32[1,2048]{1,0:T(1,128)}, s32[32,2,128]{2,1,0:T(2,128)}) custom-call(s32[1,2]{1,0:T(1,128)} %rel_ref.5, s32[1,2048]{1,0:T(1,128)} %bitcast.27, s32[1,2048]{1,0:T(1,128)} %row_ref.1), custom_call_target="tpu_custom_call" | custom-call | tf_op jit(solution)/shard_map/pallas_call | solution.py:625
  7.6 10.2 %all-to-all-start = ((s32[32,2,128]{2,1,0:T(2,128)}), s32[32,2,128]{2,1,0:T(2,128)S(1)}, u32[]{:S(2)}, u32[]{:S(2)}) async-start(s32[32,2,128]{2,1,0:T(2,128)} %get-tuple-element.38), calls=%async_computation | async-start | bytes 65536 | tf_op jit(solution)/shard_map/all_to_all | solution.py:630
  19.1 14.1 %all-to-all-done.asked_ref = s32[32,2,128]{2,1,0:T(2,128)S(1)} async-done(((s32[32,2,128]{2,1,0:T(2,128)}), s32[32,2,128]{2,1,0:T(2,128)S(1)}, u32[]{:S(2)}, u32[]{:S(2)}) %all-to-all-start) | async-done | bytes 32800 | tf_op jit(solution)/shard_map/all_to_all | solution.py:630
  33.2 1.9 collective-permute-start.2
  35.2 2.4 %collective-permute-done.2.refs_3_.cross_sibling_table = bf16[2048,256]{1,0:T(8,128)(2,1)} collective-permute-done((bf16[2048,256]{1,0:T(8,128)(2,1)S(1)}, bf16[2048,256]{1,0:T(8,128)(2,1)}, u32[]{:S(2)}, u32[]{:S(2)}) %collective-permute-start.2) | collective-permute-done | bytes 1048608 | tf_op jit(solution)/shard_map/ppermute | solution.py:614
  37.6 12.4 %shard_map.148 = bf16[32,128,256]{2,1,0:T(8,128)(2,1)} custom-call(s32[4,32]{1,0:T(4,128)} %partner_ref.5, s32[1]{0:T(128)} %bitcast.1.group_ref, s32[32,2,128]{2,1,0:T(2,128)} %copy-done.7, bf16[2048,256]{1,0:T(8,128)(2,1)} %copy-done.3, bf16[2048,256]{1,0:T(8,128)(2,1)} %copy-done.5, bf16[2048,256]{1,0:T(8,128)(2,1)} %copy-done.4, ...), custom_call_target="tpu_custom_call" | custom-call | tf_op jit(solution)/shard_map/pallas_call | solution.py:636
  50.0 5.6 %all-to-all-start.1 = ((bf16[32,128,256]{2,1,0:T(8,128)(2,1)}), bf16[32,128,256]{2,1,0:T(8,128)(2,1)S(1)}, u32[]{:S(2)}, u32[]{:S(2)}) async-start(bf16[32,128,256]{2,1,0:T(8,128)(2,1)} %shard_map.148), calls=%async_computation.1 | async-start | bytes 4194304 | tf_op jit(solution)/shard_map/all_to_all | solution.py:642
  58.1 20.2 %shard_map.149 = (bf16[2048,256]{1,0:T(8,128)(2,1)}, bf16[2048,256]{1,0:T(8,128)(2,1)}, bf16[2048,256]{1,0:T(8,128)(2,1)}, bf16[2048,1024]{1,0:T(8,128)(2,1)}, f32[2048,256]{1,0:T(8,128)}, /*index=5*/f32[2048,128]{1,0:T(8,128)}) custom-call(s32[1,2]{1,0:T(1,128)} %rel_ref.5, s32[1]{0:T(128)} %bitcast.5.visit_ref.visit_to_ref, s32[1,2048]{1,0:T(1,128)} %src_ref.3, ...), custom_call_target="tpu_custom_call" | custom-call | flops 8589934592 | bytes 12582912 | tf_op jit(solution)/shard_map/pallas_call | solution.py:360
  78.3 6.8 %all-to-all-done.1 = bf16[32,128,256]{2,1,0:T(8,128)(2,1)S(1)} async-done(((bf16[32,128,256]{2,1,0:T(8,128)(2,1)}), bf16[32,128,256]{2,1,0:T(8,128)(2,1)S(1)}, u32[]{:S(2)}, u32[]{:S(2)}) %all-to-all-start.1) | async-done | bytes 2097184 | tf_op jit(solution)/shard_map/all_to_all | solution.py:642
  86.5 23.9 %shard_map.150 = (bf16[32,144,256]{2,1,0:T(8,128)(2,1)}, bf16[2048,256]{1,0:T(8,128)(2,1)}, bf16[2048,256]{1,0:T(8,128)(2,1)}, bf16[2048,256]{1,0:T(8,128)(2,1)}) custom-call(s32[1,2]{1,0:T(1,128)} %rel_ref.5, s32[1,1]{1,0:T(1,128)S(6)} %copy.19.count_ref, s32[1,2048]{1,0:T(1,128)} %get-tuple-element.37.slot_ref, bf16[4096,256]{1,0:T(8,128)(2,1)} %bitcast.23, ...), custom_call_target="tpu_custom_call" | custom-call | tf_op jit(solution)/shard_map/pallas_call | solution.py:390
  110.4 7.0 %all-to-all-start.2 = ((bf16[32,144,256]{2,1,0:T(8,128)(2,1)}), bf16[32,144,256]{2,1,0:T(8,128)(2,1)S(1)}, u32[]{:S(2)}, u32[]{:S(2)}) async-start(bf16[32,144,256]{2,1,0:T(8,128)(2,1)} %get-tuple-element.47), calls=%async_computation.2 | async-start | bytes 4718592 | tf_op jit(solution)/shard_map/all_to_all | solution.py:648
  118.0 11.8 %shard_map.151 = (f32[2048,256]{1,0:T(8,128)}, f32[2048,256]{1,0:T(8,128)}) custom-call(s32[1,2048]{1,0:T(1,128)} %src_ref.3, s32[2,1024]{1,0:T(2,128)} %bitcast.29, s32[2,1024]{1,0:T(2,128)} %bitcast.31, bf16[2048,256]{1,0:T(8,128)(2,1)} %get-tuple-element.48.d_src, bf16[2048,256]{1,0:T(8,128)(2,1)} %get-tuple-element.49.d_neg_src, ...), custom_call_target="tpu_custom_call" | custom-call | flops 6442450944 | bytes 7340032 | tf_op jit(solution)/shard_map/pallas_call | solution.py:650
  129.7 19.7 %all-to-all-done.2.returned_ref = bf16[32,144,256]{2,1,0:T(8,128)(2,1)S(1)} async-done(((bf16[32,144,256]{2,1,0:T(8,128)(2,1)}), bf16[32,144,256]{2,1,0:T(8,128)(2,1)S(1)}, u32[]{:S(2)}, u32[]{:S(2)}) %all-to-all-start.2) | async-done | bytes 2359328 | tf_op jit(solution)/shard_map/all_to_all | solution.py:648
  150.2 2.2 shard_map.152
  158.2 4.1 %collective-permute-done.4 = f32[20,8,256]{2,1,0:T(8,128)S(1)} collective-permute-done((f32[20,8,256]{2,1,0:T(8,128)S(1)}, f32[20,8,256]{2,1,0:T(8,128)S(1)}, u32[]{:S(2)}, u32[]{:S(2)}) %collective-permute-start.4) | collective-permute-done | bytes 163872 | tf_op jit(solution)/shard_map/ppermute | solution.py:614
  162.3 1.9 collective-permute-start.5
  164.2 9.6 %shard_map.153 = (bf16[2048,256]{1,0:T(8,128)(2,1)}, bf16[2048,256]{1,0:T(8,128)(2,1)}) custom-call(s32[4,32]{1,0:T(4,128)} %partner_ref.5, s32[1]{0:T(128)} %bitcast.1.group_ref, s32[1]{0:T(128)} %bitcast.5.visit_ref.visit_to_ref, s32[32,2,128]{2,1,0:T(2,128)} %copy-done.7, bf16[32,144,256]{2,1,0:T(8,128)(2,1)} %copy-done, ...), custom_call_target="tpu_custom_call" | custom-call | tf_op jit(solution)/shard_map/pallas_call | solution.py:682
  175.7 5.0 %all-to-all-start.3 = ((bf16[16,2,20,8,256]{4,3,2,1,0:T(8,128)(2,1)}), bf16[16,2,20,8,256]{4,3,2,1,0:T(8,128)(2,1)S(1)}, u32[]{:S(2)}, u32[]{:S(2)}) async-start(bf16[16,2,20,8,256]{4,3,2,1,0:T(8,128)(2,1)} %broadcast_in_dim.2), calls=%async_computation.3 | async-start | bytes 5242880 | tf_op jit(solution)/shard_map/all_to_all | solution.py:672
  180.7 7.3 %shard_map.154 = (bf16[2048,256]{1,0:T(8,128)(2,1)}, bf16[2048,256]{1,0:T(8,128)(2,1)}) custom-call(s32[4,32]{1,0:T(4,128)} %partner_ref.5, s32[1]{0:T(128)} %bitcast.1.group_ref, s32[1]{0:T(128)} %bitcast.5.visit_ref.visit_to_ref, s32[32,2,128]{2,1,0:T(2,128)} %copy-done.7, bf16[32,144,256]{2,1,0:T(8,128)(2,1)} %copy-done, ...), custom_call_target="tpu_custom_call" | custom-call | tf_op jit(solution)/shard_map/pallas_call | solution.py:682
  188.0 2.1 collective-permute-start.8
  193.6 23.3 %collective-permute-done.7.cross_ref = bf16[2048,256]{1,0:T(8,128)(2,1)} collective-permute-done((bf16[2048,256]{1,0:T(8,128)(2,1)S(1)}, bf16[2048,256]{1,0:T(8,128)(2,1)}, u32[]{:S(2)}, u32[]{:S(2)}) %collective-permute-start.7) | collective-permute-done | bytes 1048608 | tf_op jit(solution)/shard_map/ppermute | solution.py:614
  218.2 7.9 %shard_map.155 = (f32[1,2048,256]{2,1,0:T(8,128)}, f32[1,2048]{1,0:T(1,128)}) custom-call(f32[2048,256]{1,0:T(8,128)} %get-tuple-element.53.grad_ref, bf16[2048,256]{1,0:T(8,128)(2,1)} %get-tuple-element.62.home_ref, bf16[2048,256]{1,0:T(8,128)(2,1)} %copy-done.6, bf16[2048,256]{1,0:T(8,128)(2,1)} %collective-permute-done.7.cross_ref, ...), custom_call_target="tpu_custom_call" | custom-call | tf_op jit(solution)/shard_map/pallas_call | solution.py:574
  226.1 14.2 %shard_map.156 = (f32[40,256,256]{2,1,0:T(8,128)}, f32[40,256]{1,0:T(8,128)}) custom-call(s32[1]{0:T(128)} %bitcast.15.core_ref, bf16[32,20,8,256]{3,2,1,0:T(8,128)(2,1)} %bitcast.22, bf16[32,20,8,256]{3,2,1,0:T(8,128)(2,1)} %collective-permute-done.9.other_ref, f32[40,256,256]{2,1,0:T(8,128)} %relation_ref.5, f32[40,256]{1,0:T(8,128)} %acc_ref.3), custom_call_target="tpu_custom_call" | custom-call | tf_op jit(solution)/shard_map/pallas_call | solution.py:551
  (43 shorter events, 19.6 us)
Async XLA Ops:
  2.3 35.3 %copy-start.3 = (bf16[2048,256]{1,0:T(8,128)(2,1)}, bf16[2048,256]{1,0:T(8,128)(2,1)S(1)}, u32[]{:S(2)}) copy-start(bf16[2048,256]{1,0:T(8,128)(2,1)S(1)} %convert_bitcast_fusion.refs_0_.own_table) | copy-start | bytes 3145732
  2.3 30.9 %collective-permute-start = (bf16[2048,256]{1,0:T(8,128)(2,1)S(1)}, bf16[2048,256]{1,0:T(8,128)(2,1)S(1)}, u32[]{:S(2)}, u32[]{:S(2)}) collective-permute-start(bf16[2048,256]{1,0:T(8,128)(2,1)S(1)} %convert_bitcast_fusion.refs_0_.own_table), channel_id=1, source_target_pairs={{0,64},{32,96},{64,0},{96,32},{1,65},{33,97},{65,1},{97,33},{2,66}... | collective-permute-start | bytes 3145736 | tf_op jit(solution)/shard_map/ppermute | solution.py:614
  7.6 25.7 %all-to-all-start = ((s32[32,2,128]{2,1,0:T(2,128)}), s32[32,2,128]{2,1,0:T(2,128)S(1)}, u32[]{:S(2)}, u32[]{:S(2)}) async-start(s32[32,2,128]{2,1,0:T(2,128)} %get-tuple-element.38), calls=%async_computation | async-start | bytes 65536 | tf_op jit(solution)/shard_map/all_to_all | solution.py:630
  17.8 17.4 %collective-permute-start.1 = (bf16[2048,256]{1,0:T(8,128)(2,1)S(1)}, bf16[2048,256]{1,0:T(8,128)(2,1)S(1)}, u32[]{:S(2)}, u32[]{:S(2)}) collective-permute-start(bf16[2048,256]{1,0:T(8,128)(2,1)S(1)} %convert_bitcast_fusion.refs_0_.own_table), channel_id=1, source_target_pairs={{0,32},{32,0},{64,96},{96,64},{1,33},{33,1},{65,97},{97,65},{2,34}... | collective-permute-start | bytes 3145736 | tf_op jit(solution)/shard_map/ppermute | solution.py:614
  33.2 4.4 %copy-start.7 = (s32[32,2,128]{2,1,0:T(2,128)}, s32[32,2,128]{2,1,0:T(2,128)S(1)}, u32[]{:S(2)}) copy-start(s32[32,2,128]{2,1,0:T(2,128)S(1)} %all-to-all-done.asked_ref) | copy-start | bytes 98308
  33.2 4.4 %copy-start.4 = (bf16[2048,256]{1,0:T(8,128)(2,1)}, bf16[2048,256]{1,0:T(8,128)(2,1)S(1)}, u32[]{:S(2)}) copy-start(bf16[2048,256]{1,0:T(8,128)(2,1)S(1)} %collective-permute-done.refs_2_.cross_table) | copy-start | bytes 3145732
  33.2 4.3 %collective-permute-start.2 = (bf16[2048,256]{1,0:T(8,128)(2,1)S(1)}, bf16[2048,256]{1,0:T(8,128)(2,1)}, u32[]{:S(2)}, u32[]{:S(2)}) collective-permute-start(bf16[2048,256]{1,0:T(8,128)(2,1)S(1)} %collective-permute-done.refs_2_.cross_table), channel_id=1, source_target_pairs={{0,32},{32,0},{64,96},{96,64},{1,33},{33,1},{65,97},{97,65},{2,34}... | collective-permute-start | bytes 3145736 | tf_op jit(solution)/shard_map/ppermute | solution.py:614
  35.2 2.4 %copy-start.5 = (bf16[2048,256]{1,0:T(8,128)(2,1)}, bf16[2048,256]{1,0:T(8,128)(2,1)S(1)}, u32[]{:S(2)}) copy-start(bf16[2048,256]{1,0:T(8,128)(2,1)S(1)} %collective-permute-done.1.refs_1_.sibling_table) | copy-start | bytes 3145732
  50.0 35.1 %all-to-all-start.1 = ((bf16[32,128,256]{2,1,0:T(8,128)(2,1)}), bf16[32,128,256]{2,1,0:T(8,128)(2,1)S(1)}, u32[]{:S(2)}, u32[]{:S(2)}) async-start(bf16[32,128,256]{2,1,0:T(8,128)(2,1)} %shard_map.148), calls=%async_computation.1 | async-start | bytes 4194304 | tf_op jit(solution)/shard_map/all_to_all | solution.py:642
  85.1 1.3 copy-start.2
  110.3 7.0 %copy-start.8 = (s32[32,2,128]{2,1,0:T(2,128)S(1)}, s32[32,2,128]{2,1,0:T(2,128)}, u32[]{:S(2)}) copy-start(s32[32,2,128]{2,1,0:T(2,128)} %copy-done.7) | copy-start | bytes 98308
  110.4 39.1 %all-to-all-start.2 = ((bf16[32,144,256]{2,1,0:T(8,128)(2,1)}), bf16[32,144,256]{2,1,0:T(8,128)(2,1)S(1)}, u32[]{:S(2)}, u32[]{:S(2)}) async-start(bf16[32,144,256]{2,1,0:T(8,128)(2,1)} %get-tuple-element.47), calls=%async_computation.2 | async-start | bytes 4718592 | tf_op jit(solution)/shard_map/all_to_all | solution.py:648
  149.5 14.7 %copy-start = (bf16[32,144,256]{2,1,0:T(8,128)(2,1)}, bf16[32,144,256]{2,1,0:T(8,128)(2,1)S(1)}, u32[]{:S(2)}) copy-start(bf16[32,144,256]{2,1,0:T(8,128)(2,1)S(1)} %all-to-all-done.2.returned_ref) | copy-start | bytes 7077892
  153.3 2.3 collective-permute-start.3
  156.5 5.7 %collective-permute-start.4 = (f32[20,8,256]{2,1,0:T(8,128)S(1)}, f32[20,8,256]{2,1,0:T(8,128)S(1)}, u32[]{:S(2)}, u32[]{:S(2)}) collective-permute-start(f32[20,8,256]{2,1,0:T(8,128)S(1)} %bitcast_add_fusion), channel_id=1, source_target_pairs={{0,64},{32,96},{64,0},{96,32},{1,65},{33,97},{65,1},{97,33},{2,66}... | collective-permute-start | bytes 491528 | tf_op jit(solution)/shard_map/ppermute | solution.py:614
  162.3 11.6 %collective-permute-start.5 = (bf16[20,8,256]{2,1,0:T(8,128)(2,1)S(1)}, bf16[20,8,256]{2,1,0:T(8,128)(2,1)S(1)}, u32[]{:S(2)}, u32[]{:S(2)}) collective-permute-start(bf16[20,8,256]{2,1,0:T(8,128)(2,1)S(1)} %add_convert_fusion.1), channel_id=1, source_target_pairs={{0,1},{1,0},{2,3},{3,2},{4,5},{5,4},{6,7},{7,6},{8,9},{9,8},{10,11... | collective-permute-start | bytes 245768 | tf_op jit(solution)/shard_map/ppermute | solution.py:668
  173.7 16.4 %collective-permute-start.6 = (bf16[2048,256]{1,0:T(8,128)(2,1)}, bf16[2048,256]{1,0:T(8,128)(2,1)}, u32[]{:S(2)}, u32[]{:S(2)}) collective-permute-start(bf16[2048,256]{1,0:T(8,128)(2,1)} %get-tuple-element.58), channel_id=1, source_target_pairs={{0,32},{32,0},{64,96},{96,64},{1,33},{33,1},{65,97},{97,65},{2,34}... | collective-permute-start | bytes 3145736 | tf_op jit(solution)/shard_map/ppermute | solution.py:614
  175.7 41.2 %all-to-all-start.3 = ((bf16[16,2,20,8,256]{4,3,2,1,0:T(8,128)(2,1)}), bf16[16,2,20,8,256]{4,3,2,1,0:T(8,128)(2,1)S(1)}, u32[]{:S(2)}, u32[]{:S(2)}) async-start(bf16[16,2,20,8,256]{4,3,2,1,0:T(8,128)(2,1)} %broadcast_in_dim.2), calls=%async_computation.3 | async-start | bytes 5242880 | tf_op jit(solution)/shard_map/all_to_all | solution.py:672
  188.0 4.6 %collective-permute-start.8 = (bf16[2048,256]{1,0:T(8,128)(2,1)}, bf16[2048,256]{1,0:T(8,128)(2,1)S(1)}, u32[]{:S(2)}, u32[]{:S(2)}) collective-permute-start(bf16[2048,256]{1,0:T(8,128)(2,1)} %get-tuple-element.61), channel_id=1, source_target_pairs={{0,32},{32,0},{64,96},{96,64},{1,33},{33,1},{65,97},{97,65},{2,34}... | collective-permute-start | bytes 3145736 | tf_op jit(solution)/shard_map/ppermute | solution.py:614
  191.9 25.0 %collective-permute-start.7 = (bf16[2048,256]{1,0:T(8,128)(2,1)S(1)}, bf16[2048,256]{1,0:T(8,128)(2,1)}, u32[]{:S(2)}, u32[]{:S(2)}) collective-permute-start(bf16[2048,256]{1,0:T(8,128)(2,1)S(1)} %add_convert_fusion), channel_id=1, source_target_pairs={{0,64},{32,96},{64,0},{96,32},{1,65},{33,97},{65,1},{97,33},{2,66}... | collective-permute-start | bytes 3145736 | tf_op jit(solution)/shard_map/ppermute | solution.py:614
  192.6 1.0 copy-start.6
  216.9 9.2 %copy-start.1 = (bf16[16,2,20,8,256]{4,3,2,1,0:T(8,128)(2,1)}, bf16[16,2,20,8,256]{4,3,2,1,0:T(8,128)(2,1)S(1)}, u32[]{:S(2)}) copy-start(bf16[16,2,20,8,256]{4,3,2,1,0:T(8,128)(2,1)S(1)} %all-to-all-done.3) | copy-start | bytes 7864324
  216.9 9.2 %collective-permute-start.9 = (bf16[32,20,8,256]{3,2,1,0:T(8,128)(2,1)S(1)}, bf16[32,20,8,256]{3,2,1,0:T(8,128)(2,1)}, u32[]{:S(2)}, u32[]{:S(2)}) collective-permute-start(bf16[32,20,8,256]{3,2,1,0:T(8,128)(2,1)S(1)} %bitcast.21), channel_id=1, source_target_pairs={{0,32},{32,0},{64,96},{96,64},{1,33},{33,1},{65,97},{97,65},{2,34}... | collective-permute-start | bytes 7864328 | tf_op jit(solution)/shard_map/ppermute | solution.py:614

commit v5 on v4

--- a/solution.py
+++ b/solution.py
@@ -106,25 +106,29 @@
 
 
 def answer_body(partner_ref, group_ref, asked_ref, *refs):
-    tables, (found_ref, list_ref, count_ref) = refs[:4], refs[4:]
-    rows, width = tables[0].shape
-    room = asked_ref.shape[2]
-    list_peers(partner_ref, group_ref, list_ref, count_ref)
-    for part in range(4):
-        count = count_ref[part]
-
-        def pair(t, carry, part=part, count=count):
-            one = list_ref[part, 2 * t]
-            two = list_ref[part, jnp.minimum(2 * t + 1, count - 1)]
-            ask = jnp.concatenate(
-                [asked_ref[pl.ds(one, 1), 0, :], asked_ref[pl.ds(two, 1), 0, :]], axis=1
-            )
-            got = dot(pick(ask, rows), tables[part][...], 1, 0).astype(half)
-            found_ref[pl.ds(one, 1)] = got[:room].reshape(1, room, width)
-            found_ref[pl.ds(two, 1)] = got[room:].reshape(1, room, width)
-            return carry
-
-        lax.fori_loop(0, (count + 1) // 2, pair, 0)
+    tables_in, (found_out, tables, found, sems, out_sem) = refs[:4], refs[4:]
+    copies = [
+        pltpu.make_async_copy(table, tables.at[part], sems.at[part])
+        for part, table in enumerate(tables_in)
+    ]
+    for copy in copies:
+        copy.start()
+    peers, _, room = asked_ref.shape
+    rows, width = tables.shape[1:]
+    me = group_ref[0]
+    for copy in copies:
+        copy.wait()
+
+    def answer(peer, carry):
+        table = tables[partner_ref[me, peer] ^ me]
+        got = dot(pick(asked_ref[pl.ds(peer, 1), 0, :], rows), table, 1, 0)
+        found[pl.ds(peer, 1)] = got.astype(half).reshape(1, room, width)
+        return carry
+
+    lax.fori_loop(0, peers, answer, 0, unroll=4)
+    back = pltpu.make_async_copy(found, found_out, out_sem)
+    back.start()
+    back.wait()
 
 
 def operators_in(rel_ref, relation_ref, operator, sems):
@@ -443,28 +447,26 @@
     outs, (total, list_ref, count_ref) = refs[: len(parts)], refs[len(parts) :]
     rows, width = visit_ref.shape
     places = asked_ref.shape[2]
+    together = 4
     list_peers(partner_ref, group_ref, list_ref, count_ref)
     for part, out_ref in zip(parts, outs):
         count = count_ref[part]
         total[...] = jnp.where(visit_to_ref[0] == part, visit_ref[...], 0.0)
 
-        def pair(t, carry, part=part, count=count):
-            one = list_ref[part, 2 * t]
-            two = list_ref[part, jnp.minimum(2 * t + 1, count - 1)]
-            ask_two = jnp.where(2 * t + 1 < count, asked_ref[pl.ds(two, 1), 0, :], -1)
-            ask = jnp.concatenate([asked_ref[pl.ds(one, 1), 0, :], ask_two], axis=1)
-            back = jnp.concatenate(
-                [
-                    returned_ref[pl.ds(one, 1), :places, :].reshape(places, width),
-                    returned_ref[pl.ds(two, 1), :places, :].reshape(places, width),
-                ],
-                axis=0,
-            )
+        def add(t, carry, part=part, count=count):
+            asks, backs = [], []
+            for k in range(together):
+                peer = list_ref[part, jnp.minimum(together * t + k, count - 1)]
+                ask = asked_ref[pl.ds(peer, 1), 0, :]
+                asks.append(jnp.where(together * t + k < count, ask, -1))
+                backs.append(returned_ref[pl.ds(peer, 1), :places, :].reshape(places, width))
+            ask = jnp.concatenate(asks, axis=1)
+            back = jnp.concatenate(backs, axis=0)
             for first in range(0, rows, 512):
                 total[first : first + 512] += dot(place(ask, first, 512), back, 1, 0)
             return carry
 
-        lax.fori_loop(0, (count + 1) // 2, pair, 0)
+        lax.fori_loop(0, (count + together - 1) // together, add, 0)
         out_ref[...] = total[...].astype(half)
 
 
@@ -488,28 +490,28 @@
     return jnp.broadcast_to(column, (column.shape[0], 128)).T[:1, :]
 
 
-def relation_body(
-    core_ref, mine_ref, other_ref, relation_ref, acc_ref, new_ref, acc_new_ref, acc_turned, acc_found
-):
+def relation_body(part_ref, grad_ref, relation_ref, acc_ref, *refs):
+    (new_ref, acc_new_ref, acc_turned, acc_found), before = refs[-4:], refs[:-4]
     step, rows, width = relation_ref.shape
     relations = acc_ref.shape[0]
     at = pl.program_id(0)
-    own_half = at // (pl.num_programs(0) // 2) == core_ref[0]
+    first = part_ref[0] * (relations // 2) + at * step
     lane = lax.broadcasted_iota(jnp.int32, (rows, 128), 1)
 
     @pl.when(at == 0)
     def _():
         short = jnp.zeros((128 - relations, rows), full)
         acc_turned[...] = jnp.concatenate([acc_ref[...], short], axis=0).T
-        acc_found[...] = jnp.zeros_like(acc_found)
+        if before:
+            acc_found[...] = jnp.concatenate([before[1][...], short], axis=0).T
+        else:
+            acc_found[...] = jnp.zeros_like(acc_found)
 
     for k in range(step):
-        here = lane == at * step + k
-        mine = mine_ref[:, k].astype(full).reshape(rows, width)
-        other = other_ref[:, k].astype(full).reshape(rows, width)
-        grad = jnp.where(own_half, mine, other)
+        here = lane == first + k
+        grad = grad_ref[:, k].astype(full).reshape(rows, width)
         square = grad * grad
-        parts = sum(square[:, first : first + 128] for first in range(0, width, 128))
+        parts = sum(square[:, at : at + 128] for at in range(0, width, 128))
         acc = jnp.sum(
             parts * (1.0 / width) + jnp.where(here, acc_turned[...], 0.0), axis=1, keepdims=True
         )
@@ -534,26 +536,24 @@
     new_ref[0] = entity_ref[0] - grad * (step_rate / jnp.sqrt(turned(acc)[:, :1] + square))
 
 
-def relation_update(core, mine, other, relation, relation_acc):
-    peers, count, extra, width = mine.shape
+def relation_update(part, grad, relation, relation_acc, before=()):
+    peers, count, extra, width = grad.shape
     relations, rows = relation_acc.shape
-    step = 4 if count % 4 == 0 else 1
+    step = 10 if count % 10 == 0 else 1
     steps = count // step
-
-    def near(flip):
-        def at(i, core):
-            return (0, jnp.clip(i - steps * (core[0] ^ flip), 0, steps - 1), 0, 0)
-
-        return pl.BlockSpec((peers, step, extra, width), at)
-
-    whole = pl.BlockSpec((relations, rows), lambda i, core: (0, 0))
-    block = pl.BlockSpec((step, rows, width), lambda i, core: (i, 0, 0))
+    whole = pl.BlockSpec((relations, rows), lambda i, part: (0, 0))
+    block = pl.BlockSpec((step, rows, width), lambda i, part: (part[0] * steps + i, 0, 0))
     return pl.pallas_call(
         relation_body,
         grid_spec=pltpu.PrefetchScalarGridSpec(
             num_scalar_prefetch=1,
-            grid=(2 * steps,),
-            in_specs=[near(0), near(1), block, whole],
+            grid=(steps,),
+            in_specs=[
+                pl.BlockSpec((peers, step, extra, width), lambda i, part: (0, i, 0, 0)),
+                block,
+                whole,
+            ]
+            + [ANY, whole][: len(before)],
             out_specs=[block, whole],
             scratch_shapes=[pltpu.VMEM((rows, 128), full), pltpu.VMEM((rows, 128), full)],
         ),
@@ -561,8 +561,10 @@
             jax.ShapeDtypeStruct(relation.shape, full),
             jax.ShapeDtypeStruct(relation_acc.shape, full),
         ],
+        input_output_aliases={4: 0} if before else {},
         compiler_params=pltpu.CompilerParams(vmem_limit_bytes=60 * MEBI),
-    )(core, mine, other, relation, relation_acc)
+        cost_estimate=cost(0, 24 * MEBI),
+    )(part, grad, relation, relation_acc, *before)
 
 
 def entity_update(grad, home, sibling, cross, entity, entity_acc):
@@ -581,6 +583,7 @@
             jax.ShapeDtypeStruct(entity_acc.shape, full),
         ],
         compiler_params=pltpu.CompilerParams(vmem_limit_bytes=60 * MEBI),
+        cost_estimate=cost(0, 24 * MEBI),
     )(grad, home, sibling, cross, entity, entity_acc)
 
 
@@ -636,8 +639,14 @@
     found = call(
         answer_body,
         sds((peers, room, width), half),
-        lists,
-        [SMEM] * 2 + [VMEM] * 5,
+        [
+            pltpu.VMEM((4, rows, width), half),
+            pltpu.VMEM((peers, room, width), half),
+            pltpu.SemaphoreType.DMA((4,)),
+            pltpu.SemaphoreType.DMA,
+        ],
+        [SMEM] * 2 + [VMEM] + [ANY] * 4,
+        outs=ANY,
     )(partner, group, asked, *tables)
     fetched = lax.all_to_all(found, "dev", split_axis=0, concat_axis=0, tiled=True)
 
@@ -656,6 +665,20 @@
     )(src_row, neg_src, neg_dst, d_src, d_neg_src, d_neg_dst)
 
     returned, own_grad, visit_grad = lax.optimization_barrier((returned, own_grad, visit_grad))
+
+    def home(parts, returned):
+        return call(
+            functools.partial(home_body, parts),
+            tuple(sds((rows, width), half) for _ in parts),
+            [pltpu.VMEM((rows, width), full)] + lists,
+            [SMEM] * 3 + [VMEM] * 3,
+            cost(0, 24 * MEBI),
+        )(partner, group, visit_to, asked, returned, visit_grad)
+
+    home_cross_sibling, home_cross = home((3, 2), returned)
+    returned, home_cross_sibling = lax.optimization_barrier((returned, home_cross_sibling))
+    chip_cross = (home_cross.astype(full) + neighbour(home_cross_sibling, 1).astype(full)).astype(half)
+
     rel_part = call(operators_body, sds((relations, extra, width), full), (), [SMEM, VMEM])(
         asked[:, 1, :blocks], returned[:, room:, :]
     )
@@ -668,7 +691,8 @@
     near = lax.ppermute(pair, "dev", [(d, d ^ 1) for d in range(peers)])
     low = (place_id & 1) == 0
     planes = jnp.stack([jnp.where(low, pair, near), jnp.where(low, near, pair)])
-    planes, returned_later = lax.optimization_barrier((planes, returned))
+    planes, chip_cross, returned = lax.optimization_barrier((planes, chip_cross, returned))
+    from_cross = neighbour(chip_cross, 2)
     gathered = lax.all_to_all(
         jnp.broadcast_to(planes[None], (peers // 2,) + planes.shape),
         "dev",
@@ -678,28 +702,16 @@
         tiled=True,
     ).reshape((peers,) + pair.shape)
 
-    def home(parts, returned):
-        return call(
-            functools.partial(home_body, parts),
-            tuple(sds((rows, width), half) for _ in parts),
-            [pltpu.VMEM((rows, width), full)] + lists,
-            [SMEM] * 3 + [VMEM] * 3,
-        )(partner, group, visit_to, asked, returned, visit_grad)
-
-    home_cross_sibling, home_cross = home((3, 2), returned)
-    chip_cross = (home_cross.astype(full) + neighbour(home_cross_sibling, 1).astype(full)).astype(half)
-    from_cross = neighbour(chip_cross, 2)
-    home_sibling, home_own = home((1, 0), returned_later)
+    home_sibling, home_own = home((1, 0), returned)
     from_sibling = neighbour(home_sibling, 1)
-    gathered, from_cross, home_own, from_sibling = lax.optimization_barrier(
-        (gathered, from_cross, home_own, from_sibling)
-    )
-    other_half = neighbour(gathered, 1)
     entity_new, acc_new = entity_update(
         own_grad, home_own, from_sibling, from_cross, entity, entity_acc
     )
+    gathered, entity_new, acc_new = lax.optimization_barrier((gathered, entity_new, acc_new))
+    other_half = neighbour(gathered, 1)
+    before = relation_update(core.reshape(1), gathered, relation, relation_acc)
     relation_new, relation_acc_new = relation_update(
-        core.reshape(1), gathered, other_half, relation, relation_acc
+        (1 - core).reshape(1), other_half, relation, relation_acc, before
     )
     return (entity_new, acc_new, relation_new, relation_acc_new)
 

time: 242 us -> 243 us (level)
  Pallas kernels: 112 us -> 107 us
  waiting for transfers between devices: 71.6 us -> 74.7 us
    ppermute x1, waiting for transfers between devices: 0.01 us -> 2.97 us  [on_device(): near = lax.ppermute(pair, 'dev', [(d, d ^ 1) for d in range(peers)])]
    pallas_call x1 -> x2, Pallas kernels: 14.2 us -> 11.8 us  [relation_update(): pl.pallas_call(relation_body, grid_spec=pltpu.PrefetchScalarGridSpec(num_...]
  transfers between devices with their start and end apart: 14 -> 14, of which waited for: 8 -> 9; matrix products, arithmetic and copies ran while one was open for 2% -> 1% of each run, Pallas kernels for 25% -> 24%
where the time goes in v5:
time: 243 us; the launch traced here: 242 us
  Pallas kernels  107 us (44%)
  waiting for transfers between devices  74.7 us (31%)
  starting transfers between devices  43.7 us (18%)
  local copies, waits for them, and re-layouts  9.81 us (4%)
  other arithmetic  3.94 us (2%)
    ppermute x9, waiting for transfers between devices, neighbour(): return lax.ppermute(x, 'grp', [(g, g ^ flip) for g in range(4)])  31.1 us
    pallas_call x1, Pallas kernels, model(): call(model_body, (sds((peers, room + blocks * (width // peers), width), h...  23.8 us
    pallas_call x1, Pallas kernels, front(): call(front_body, (sds((edges, width), half), sds((blocks * negs, width),...  20.2 us
    all_to_all x1, waiting for transfers between devices, on_device(): lax.all_to_all(outgoing, 'dev', split_axis=0, concat_axis=0, tiled=True)  19.7 us
    pallas_call x2, Pallas kernels, home(): call(functools.partial(home_body, parts), tuple((sds((rows, width), half)...  16.4 us
    all_to_all x1, waiting for transfers between devices, on_device(): lax.all_to_all(wanted, 'dev', split_axis=0, concat_axis=0, tiled=True)  14.1 us
    ppermute x9, starting transfers between devices, neighbour(): return lax.ppermute(x, 'grp', [(g, g ^ flip) for g in range(4)])  13.1 us
    pallas_call x2, Pallas kernels, relation_update(): pl.pallas_call(relation_body, grid_spec=pltpu.PrefetchScalarGridSpec(num_...  11.8 us
  transfers between devices with their start and end apart: 14, of which 9 were waited for; matrix products, arithmetic and copies ran while one was open for 1% of the time, Pallas kernels for 24%

profile of v5, /device:TPU:1, one launch (start us, length us, event | category | flops | bytes accessed | tf_op | source)
XLA Modules:
  0.0 241.5 jit_solution(18080558628817923458)
XLA Ops:
  2.3 2.2 collective-permute-start
  4.5 3.0 %shard_map.147 = (s32[1,2048]{1,0:T(1,128)}, s32[32,2,128]{2,1,0:T(2,128)}) custom-call(s32[1,2]{1,0:T(1,128)} %rel_ref.5, s32[1,2048]{1,0:T(1,128)} %bitcast.28, s32[1,2048]{1,0:T(1,128)} %row_ref.1), custom_call_target="tpu_custom_call" | custom-call | tf_op jit(solution)/shard_map/pallas_call | solution.py:628
  7.6 10.2 %all-to-all-start = ((s32[32,2,128]{2,1,0:T(2,128)}), s32[32,2,128]{2,1,0:T(2,128)S(1)}, u32[]{:S(2)}, u32[]{:S(2)}) async-start(s32[32,2,128]{2,1,0:T(2,128)} %get-tuple-element.41), calls=%async_computation | async-start | bytes 65536 | tf_op jit(solution)/shard_map/all_to_all | solution.py:633
  19.1 14.1 %all-to-all-done.asked_ref = s32[32,2,128]{2,1,0:T(2,128)S(1)} async-done(((s32[32,2,128]{2,1,0:T(2,128)}), s32[32,2,128]{2,1,0:T(2,128)S(1)}, u32[]{:S(2)}, u32[]{:S(2)}) %all-to-all-start) | async-done | bytes 32800 | tf_op jit(solution)/shard_map/all_to_all | solution.py:633
  35.2 2.4 collective-permute-done.2.refs_3_.cross_sibling_table
  37.6 10.4 %shard_map.148 = bf16[32,128,256]{2,1,0:T(8,128)(2,1)} custom-call(s32[4,32]{1,0:T(4,128)} %partner_ref.5, s32[1]{0:T(128)} %bitcast.3.group_ref, s32[32,2,128]{2,1,0:T(2,128)} %copy-done.7, bf16[2048,256]{1,0:T(8,128)(2,1)} %copy-done.3, bf16[2048,256]{1,0:T(8,128)(2,1)} %copy-done.6, bf16[2048,256]{1,0:T(8,128)(2,1)} %copy-done.5, ...), custom_call_target="tpu_custom_call" | custom-call | tf_op jit(solution)/shard_map/pallas_call | solution.py:639
  48.0 5.6 %all-to-all-start.1 = ((bf16[32,128,256]{2,1,0:T(8,128)(2,1)}), bf16[32,128,256]{2,1,0:T(8,128)(2,1)S(1)}, u32[]{:S(2)}, u32[]{:S(2)}) async-start(bf16[32,128,256]{2,1,0:T(8,128)(2,1)} %shard_map.148), calls=%async_computation.1 | async-start | bytes 4194304 | tf_op jit(solution)/shard_map/all_to_all | solution.py:651
  56.2 20.2 %shard_map.149 = (bf16[2048,256]{1,0:T(8,128)(2,1)}, bf16[2048,256]{1,0:T(8,128)(2,1)}, bf16[2048,256]{1,0:T(8,128)(2,1)}, bf16[2048,1024]{1,0:T(8,128)(2,1)}, f32[2048,256]{1,0:T(8,128)}, /*index=5*/f32[2048,128]{1,0:T(8,128)}) custom-call(s32[1,2]{1,0:T(1,128)} %rel_ref.5, s32[1]{0:T(128)} %bitcast.6.visit_ref.visit_to_ref, s32[1,2048]{1,0:T(1,128)} %src_ref.3, ...), custom_call_target="tpu_custom_call" | custom-call | flops 8589934592 | bytes 12582912 | tf_op jit(solution)/shard_map/pallas_call | solution.py:364
  76.4 6.8 %all-to-all-done.1 = bf16[32,128,256]{2,1,0:T(8,128)(2,1)S(1)} async-done(((bf16[32,128,256]{2,1,0:T(8,128)(2,1)}), bf16[32,128,256]{2,1,0:T(8,128)(2,1)S(1)}, u32[]{:S(2)}, u32[]{:S(2)}) %all-to-all-start.1) | async-done | bytes 2097184 | tf_op jit(solution)/shard_map/all_to_all | solution.py:651
  84.5 23.8 %shard_map.150 = (bf16[32,144,256]{2,1,0:T(8,128)(2,1)}, bf16[2048,256]{1,0:T(8,128)(2,1)}, bf16[2048,256]{1,0:T(8,128)(2,1)}, bf16[2048,256]{1,0:T(8,128)(2,1)}) custom-call(s32[1,2]{1,0:T(1,128)} %rel_ref.5, s32[1,1]{1,0:T(1,128)S(6)} %copy.21.count_ref, s32[1,2048]{1,0:T(1,128)} %get-tuple-element.43.slot_ref, bf16[4096,256]{1,0:T(8,128)(2,1)} %bitcast.24, ...), custom_call_target="tpu_custom_call" | custom-call | tf_op jit(solution)/shard_map/pallas_call | solution.py:394
  108.4 7.0 %all-to-all-start.2 = ((bf16[32,144,256]{2,1,0:T(8,128)(2,1)}), bf16[32,144,256]{2,1,0:T(8,128)(2,1)S(1)}, u32[]{:S(2)}, u32[]{:S(2)}) async-start(bf16[32,144,256]{2,1,0:T(8,128)(2,1)} %get-tuple-element.51), calls=%async_computation.2 | async-start | bytes 4718592 | tf_op jit(solution)/shard_map/all_to_all | solution.py:657
  116.0 11.8 %shard_map.151 = (f32[2048,256]{1,0:T(8,128)}, f32[2048,256]{1,0:T(8,128)}) custom-call(s32[1,2048]{1,0:T(1,128)} %src_ref.3, s32[2,1024]{1,0:T(2,128)} %bitcast.30, s32[2,1024]{1,0:T(2,128)} %bitcast.32, bf16[2048,256]{1,0:T(8,128)(2,1)} %get-tuple-element.52.d_src, bf16[2048,256]{1,0:T(8,128)(2,1)} %get-tuple-element.53.d_neg_src, ...), custom_call_target="tpu_custom_call" | custom-call | flops 6442450944 | bytes 7340032 | tf_op jit(solution)/shard_map/pallas_call | solution.py:659
  127.7 19.7 %all-to-all-done.2.returned_ref = bf16[32,144,256]{2,1,0:T(8,128)(2,1)S(1)} async-done(((bf16[32,144,256]{2,1,0:T(8,128)(2,1)}), bf16[32,144,256]{2,1,0:T(8,128)(2,1)S(1)}, u32[]{:S(2)}, u32[]{:S(2)}) %all-to-all-start.2) | async-done | bytes 2359328 | tf_op jit(solution)/shard_map/all_to_all | solution.py:657
  148.9 8.2 %shard_map.152 = (bf16[2048,256]{1,0:T(8,128)(2,1)}, bf16[2048,256]{1,0:T(8,128)(2,1)}) custom-call(s32[4,32]{1,0:T(4,128)} %partner_ref.5, s32[1]{0:T(128)} %bitcast.3.group_ref, s32[1]{0:T(128)} %bitcast.6.visit_ref.visit_to_ref, s32[32,2,128]{2,1,0:T(2,128)} %copy-done.7, bf16[32,144,256]{2,1,0:T(8,128)(2,1)} %copy-done, ...), custom_call_target="tpu_custom_call" | custom-call | bytes 25165824 | tf_op jit(solution)/shard_map/pallas_call | solution.py:670
  158.8 2.0 shard_map.153
  166.7 4.1 %collective-permute-done.4 = f32[20,8,256]{2,1,0:T(8,128)S(1)} collective-permute-done((f32[20,8,256]{2,1,0:T(8,128)S(1)}, f32[20,8,256]{2,1,0:T(8,128)S(1)}, u32[]{:S(2)}, u32[]{:S(2)}) %collective-permute-start.4) | collective-permute-done | bytes 163872 | tf_op jit(solution)/shard_map/ppermute | solution.py:617
  172.7 3.0 %collective-permute-done.5 = bf16[20,8,256]{2,1,0:T(8,128)(2,1)S(1)} collective-permute-done((bf16[20,8,256]{2,1,0:T(8,128)(2,1)S(1)}, bf16[20,8,256]{2,1,0:T(8,128)(2,1)S(1)}, u32[]{:S(2)}, u32[]{:S(2)}) %collective-permute-start.5) | collective-permute-done | bytes 81952 | tf_op jit(solution)/shard_map/ppermute | solution.py:691
  178.7 5.9 %all-to-all-start.3 = ((bf16[16,2,20,8,256]{4,3,2,1,0:T(8,128)(2,1)}), bf16[16,2,20,8,256]{4,3,2,1,0:T(8,128)(2,1)S(1)}, u32[]{:S(2)}, u32[]{:S(2)}) async-start(bf16[16,2,20,8,256]{4,3,2,1,0:T(8,128)(2,1)} %broadcast_in_dim.2), calls=%async_computation.3 | async-start | bytes 5242880 | tf_op jit(solution)/shard_map/all_to_all | solution.py:696
  184.7 8.2 %shard_map.154 = (bf16[2048,256]{1,0:T(8,128)(2,1)}, bf16[2048,256]{1,0:T(8,128)(2,1)}) custom-call(s32[4,32]{1,0:T(4,128)} %partner_ref.5, s32[1]{0:T(128)} %bitcast.3.group_ref, s32[1]{0:T(128)} %bitcast.6.visit_ref.visit_to_ref, s32[32,2,128]{2,1,0:T(2,128)} %copy-done.7, bf16[32,144,256]{2,1,0:T(8,128)(2,1)} %copy-done, ...), custom_call_target="tpu_custom_call" | custom-call | bytes 25165824 | tf_op jit(solution)/shard_map/pallas_call | solution.py:670
  192.9 2.3 collective-permute-start.7
  197.8 22.5 %collective-permute-done.8.cross_ref = bf16[2048,256]{1,0:T(8,128)(2,1)} collective-permute-done((bf16[2048,256]{1,0:T(8,128)(2,1)}, bf16[2048,256]{1,0:T(8,128)(2,1)}, u32[]{:S(2)}, u32[]{:S(2)}) %collective-permute-start.8) | collective-permute-done | bytes 1048608 | tf_op jit(solution)/shard_map/ppermute | solution.py:617
  220.3 7.9 %shard_map.155 = (f32[1,2048,256]{2,1,0:T(8,128)}, f32[1,2048]{1,0:T(1,128)}) custom-call(f32[2048,256]{1,0:T(8,128)} %get-tuple-element.64.grad_ref, bf16[2048,256]{1,0:T(8,128)(2,1)} %get-tuple-element.66.home_ref, bf16[2048,256]{1,0:T(8,128)(2,1)} %collective-permute-done.7.sibling_ref, bf16[2048,256]{1,0:T(8,128)(2,1)} %collective-permute-done.8.cross_ref, ...), custom_call_target="tpu_custom_call" | custom-call | bytes 25165824 | tf_op jit(solution)/shard_map/pallas_call | solution.py:576
  229.7 5.9 %shard_map.156 = (f32[40,256,256]{2,1,0:T(8,128)}, f32[40,256]{1,0:T(8,128)}) custom-call(s32[1]{0:T(128)} %bitcast.16.part_ref, bf16[32,20,8,256]{3,2,1,0:T(8,128)(2,1)} %bitcast.23, f32[40,256,256]{2,1,0:T(8,128)} %relation_ref.7, f32[40,256]{1,0:T(8,128)} %acc_ref.5), custom_call_target="tpu_custom_call" | custom-call | bytes 25165824 | tf_op jit(solution)/shard_map/pallas_call | solution.py:546
  235.6 5.9 %shard_map.157 = (f32[40,256,256]{2,1,0:T(8,128)}, f32[40,256]{1,0:T(8,128)}) custom-call(s32[1]{0:T(128)} %bitcast.15.part_ref, bf16[32,20,8,256]{3,2,1,0:T(8,128)(2,1)} %collective-permute-done.9.grad_ref, f32[40,256,256]{2,1,0:T(8,128)} %relation_ref.7, f32[40,256]{1,0:T(8,128)} %acc_ref.5, ...), custom_call_target="tpu_custom_call", output_to_operand_aliasing={{0}: (4, {})} | custom-call | bytes 25165824 | tf_op jit(solution)/shard_map/pallas_call | solution.py:546
  (44 shorter events, 26.3 us)
Async XLA Ops:
  2.3 35.3 %copy-start.3 = (bf16[2048,256]{1,0:T(8,128)(2,1)}, bf16[2048,256]{1,0:T(8,128)(2,1)S(1)}, u32[]{:S(2)}) copy-start(bf16[2048,256]{1,0:T(8,128)(2,1)S(1)} %convert_bitcast_fusion.refs_0_.own_table) | copy-start | bytes 3145732
  2.3 30.9 %collective-permute-start = (bf16[2048,256]{1,0:T(8,128)(2,1)S(1)}, bf16[2048,256]{1,0:T(8,128)(2,1)S(1)}, u32[]{:S(2)}, u32[]{:S(2)}) collective-permute-start(bf16[2048,256]{1,0:T(8,128)(2,1)S(1)} %convert_bitcast_fusion.refs_0_.own_table), channel_id=1, source_target_pairs={{0,64},{32,96},{64,0},{96,32},{1,65},{33,97},{65,1},{97,33},{2,66}... | collective-permute-start | bytes 3145736 | tf_op jit(solution)/shard_map/ppermute | solution.py:617
  7.6 25.7 %all-to-all-start = ((s32[32,2,128]{2,1,0:T(2,128)}), s32[32,2,128]{2,1,0:T(2,128)S(1)}, u32[]{:S(2)}, u32[]{:S(2)}) async-start(s32[32,2,128]{2,1,0:T(2,128)} %get-tuple-element.41), calls=%async_computation | async-start | bytes 65536 | tf_op jit(solution)/shard_map/all_to_all | solution.py:633
  17.8 17.4 %collective-permute-start.1 = (bf16[2048,256]{1,0:T(8,128)(2,1)S(1)}, bf16[2048,256]{1,0:T(8,128)(2,1)S(1)}, u32[]{:S(2)}, u32[]{:S(2)}) collective-permute-start(bf16[2048,256]{1,0:T(8,128)(2,1)S(1)} %convert_bitcast_fusion.refs_0_.own_table), channel_id=1, source_target_pairs={{0,32},{32,0},{64,96},{96,64},{1,33},{33,1},{65,97},{97,65},{2,34}... | collective-permute-start | bytes 3145736 | tf_op jit(solution)/shard_map/ppermute | solution.py:617
  33.2 4.4 %copy-start.7 = (s32[32,2,128]{2,1,0:T(2,128)}, s32[32,2,128]{2,1,0:T(2,128)S(1)}, u32[]{:S(2)}) copy-start(s32[32,2,128]{2,1,0:T(2,128)S(1)} %all-to-all-done.asked_ref) | copy-start | bytes 98308
  33.2 4.4 %copy-start.5 = (bf16[2048,256]{1,0:T(8,128)(2,1)}, bf16[2048,256]{1,0:T(8,128)(2,1)S(1)}, u32[]{:S(2)}) copy-start(bf16[2048,256]{1,0:T(8,128)(2,1)S(1)} %collective-permute-done.refs_2_.cross_table) | copy-start | bytes 3145732
  33.2 4.3 %collective-permute-start.2 = (bf16[2048,256]{1,0:T(8,128)(2,1)S(1)}, bf16[2048,256]{1,0:T(8,128)(2,1)}, u32[]{:S(2)}, u32[]{:S(2)}) collective-permute-start(bf16[2048,256]{1,0:T(8,128)(2,1)S(1)} %collective-permute-done.refs_2_.cross_table), channel_id=1, source_target_pairs={{0,32},{32,0},{64,96},{96,64},{1,33},{33,1},{65,97},{97,65},{2,34}... | collective-permute-start | bytes 3145736 | tf_op jit(solution)/shard_map/ppermute | solution.py:617
  35.2 2.4 %copy-start.6 = (bf16[2048,256]{1,0:T(8,128)(2,1)}, bf16[2048,256]{1,0:T(8,128)(2,1)S(1)}, u32[]{:S(2)}) copy-start(bf16[2048,256]{1,0:T(8,128)(2,1)S(1)} %collective-permute-done.1.refs_1_.sibling_table) | copy-start | bytes 3145732
  48.0 35.2 %all-to-all-start.1 = ((bf16[32,128,256]{2,1,0:T(8,128)(2,1)}), bf16[32,128,256]{2,1,0:T(8,128)(2,1)S(1)}, u32[]{:S(2)}, u32[]{:S(2)}) async-start(bf16[32,128,256]{2,1,0:T(8,128)(2,1)} %shard_map.148), calls=%async_computation.1 | async-start | bytes 4194304 | tf_op jit(solution)/shard_map/all_to_all | solution.py:651
  83.2 1.3 copy-start.2
  108.4 7.0 %copy-start.8 = (s32[32,2,128]{2,1,0:T(2,128)S(1)}, s32[32,2,128]{2,1,0:T(2,128)}, u32[]{:S(2)}) copy-start(s32[32,2,128]{2,1,0:T(2,128)} %copy-done.7) | copy-start | bytes 98308
  108.4 39.1 %all-to-all-start.2 = ((bf16[32,144,256]{2,1,0:T(8,128)(2,1)}), bf16[32,144,256]{2,1,0:T(8,128)(2,1)S(1)}, u32[]{:S(2)}, u32[]{:S(2)}) async-start(bf16[32,144,256]{2,1,0:T(8,128)(2,1)} %get-tuple-element.51), calls=%async_computation.2 | async-start | bytes 4718592 | tf_op jit(solution)/shard_map/all_to_all | solution.py:657
  147.5 1.4 copy-start
  157.1 18.6 %copy-start.4 = (bf16[2048,256]{1,0:T(8,128)(2,1)S(1)}, bf16[2048,256]{1,0:T(8,128)(2,1)}, u32[]{:S(2)}) copy-start(bf16[2048,256]{1,0:T(8,128)(2,1)} %get-tuple-element.61) | copy-start | bytes 3145732
  161.8 2.3 collective-permute-start.3
  163.1 12.6 %collective-permute-start.6 = (bf16[2048,256]{1,0:T(8,128)(2,1)}, bf16[2048,256]{1,0:T(8,128)(2,1)S(1)}, u32[]{:S(2)}, u32[]{:S(2)}) collective-permute-start(bf16[2048,256]{1,0:T(8,128)(2,1)} %get-tuple-element.62), channel_id=1, source_target_pairs={{0,32},{32,0},{64,96},{96,64},{1,33},{33,1},{65,97},{97,65},{2,34}... | collective-permute-start | bytes 3145736 | tf_op jit(solution)/shard_map/ppermute | solution.py:617
  165.0 5.7 %collective-permute-start.4 = (f32[20,8,256]{2,1,0:T(8,128)S(1)}, f32[20,8,256]{2,1,0:T(8,128)S(1)}, u32[]{:S(2)}, u32[]{:S(2)}) collective-permute-start(f32[20,8,256]{2,1,0:T(8,128)S(1)} %bitcast_add_fusion), channel_id=1, source_target_pairs={{0,64},{32,96},{64,0},{96,32},{1,65},{33,97},{65,1},{97,33},{2,66}... | collective-permute-start | bytes 491528 | tf_op jit(solution)/shard_map/ppermute | solution.py:617
  170.8 4.9 %collective-permute-start.5 = (bf16[20,8,256]{2,1,0:T(8,128)(2,1)S(1)}, bf16[20,8,256]{2,1,0:T(8,128)(2,1)S(1)}, u32[]{:S(2)}, u32[]{:S(2)}) collective-permute-start(bf16[20,8,256]{2,1,0:T(8,128)(2,1)S(1)} %add_convert_fusion.1), channel_id=1, source_target_pairs={{0,1},{1,0},{2,3},{3,2},{4,5},{5,4},{6,7},{7,6},{8,9},{9,8},{10,11... | collective-permute-start | bytes 245768 | tf_op jit(solution)/shard_map/ppermute | solution.py:691
  178.7 49.4 %all-to-all-start.3 = ((bf16[16,2,20,8,256]{4,3,2,1,0:T(8,128)(2,1)}), bf16[16,2,20,8,256]{4,3,2,1,0:T(8,128)(2,1)S(1)}, u32[]{:S(2)}, u32[]{:S(2)}) async-start(bf16[16,2,20,8,256]{4,3,2,1,0:T(8,128)(2,1)} %broadcast_in_dim.2), calls=%async_computation.3 | async-start | bytes 5242880 | tf_op jit(solution)/shard_map/all_to_all | solution.py:696
  192.9 4.9 %collective-permute-start.7 = (bf16[2048,256]{1,0:T(8,128)(2,1)}, bf16[2048,256]{1,0:T(8,128)(2,1)}, u32[]{:S(2)}, u32[]{:S(2)}) collective-permute-start(bf16[2048,256]{1,0:T(8,128)(2,1)} %get-tuple-element.67), channel_id=1, source_target_pairs={{0,32},{32,0},{64,96},{96,64},{1,33},{33,1},{65,97},{97,65},{2,34}... | collective-permute-start | bytes 3145736 | tf_op jit(solution)/shard_map/ppermute | solution.py:617
  195.2 25.1 %collective-permute-start.8 = (bf16[2048,256]{1,0:T(8,128)(2,1)}, bf16[2048,256]{1,0:T(8,128)(2,1)}, u32[]{:S(2)}, u32[]{:S(2)}) collective-permute-start(bf16[2048,256]{1,0:T(8,128)(2,1)} %add_convert_fusion), channel_id=1, source_target_pairs={{0,64},{32,96},{64,0},{96,32},{1,65},{33,97},{65,1},{97,33},{2,66}... | collective-permute-start | bytes 3145736 | tf_op jit(solution)/shard_map/ppermute | solution.py:617
  228.2 1.5 copy-start.1
  228.2 7.4 %collective-permute-start.9 = (bf16[32,20,8,256]{3,2,1,0:T(8,128)(2,1)S(1)}, bf16[32,20,8,256]{3,2,1,0:T(8,128)(2,1)}, u32[]{:S(2)}, u32[]{:S(2)}) collective-permute-start(bf16[32,20,8,256]{3,2,1,0:T(8,128)(2,1)S(1)} %bitcast.22), channel_id=1, source_target_pairs={{0,32},{32,0},{64,96},{96,64},{1,33},{33,1},{65,97},{97,65},{2,34}... | collective-permute-start | bytes 7864328 | tf_op jit(solution)/shard_map/ppermute | solution.py:617

commit v6 on v5

--- a/solution.py
+++ b/solution.py
@@ -13,7 +13,7 @@
 full = jnp.float32
 VMEM = pl.BlockSpec(memory_space=pltpu.VMEM)
 SMEM = pl.BlockSpec(memory_space=pltpu.SMEM)
-ANY = pl.BlockSpec(memory_space=pl.ANY)
+HBM = pl.BlockSpec(memory_space=pltpu.HBM)
 
 
 def dot(a, b, ca, cb):
@@ -41,7 +41,7 @@
     return jnp.where(row == line, 1.0, 0.0).astype(half)
 
 
-def call(body, shapes, scratch=(), specs=None, cost=None, outs=None, mebi=60, **kw):
+def call(body, shapes, scratch=(), specs=None, cost=None, outs=None, mebi=40, **kw):
     return pl.pallas_call(
         body,
         out_shape=shapes,
@@ -380,7 +380,7 @@
             pltpu.SemaphoreType.DMA,
             pltpu.SemaphoreType.DMA,
         ],
-        [SMEM] * 2 + [VMEM] * 3 + [ANY] * 5,
+        [SMEM] * 2 + [VMEM] * 3 + [HBM] * 5,
         cost(2 * edges * width * (3 * rows + 2 * negs), 12 * MEBI),
     )(rel_ids, visit_to, src_row, neg_src, neg_dst, relation, *tables)
 
@@ -415,8 +415,8 @@
             pltpu.SemaphoreType.DMA((6,)),
             pltpu.SemaphoreType.DMA((3,)),
         ],
-        [SMEM] * 2 + [VMEM] * 2 + [ANY] * 7,
-        outs=[VMEM] + [ANY] * 3,
+        [SMEM] * 2 + [VMEM] * 2 + [HBM] * 7,
+        outs=[VMEM] + [HBM] * 3,
     )(rel_ids, edge_count, slot, fetched, relation, *rest)
 
 
@@ -553,7 +553,7 @@
                 block,
                 whole,
             ]
-            + [ANY, whole][: len(before)],
+            + [HBM, whole][: len(before)],
             out_specs=[block, whole],
             scratch_shapes=[pltpu.VMEM((rows, 128), full), pltpu.VMEM((rows, 128), full)],
         ),
@@ -645,8 +645,8 @@
             pltpu.SemaphoreType.DMA((4,)),
             pltpu.SemaphoreType.DMA,
         ],
-        [SMEM] * 2 + [VMEM] + [ANY] * 4,
-        outs=ANY,
+        [SMEM] * 2 + [VMEM] + [HBM] * 4,
+        outs=HBM,
     )(partner, group, asked, *tables)
     fetched = lax.all_to_all(found, "dev", split_axis=0, concat_axis=0, tiled=True)
 
@@ -676,7 +676,6 @@
         )(partner, group, visit_to, asked, returned, visit_grad)
 
     home_cross_sibling, home_cross = home((3, 2), returned)
-    returned, home_cross_sibling = lax.optimization_barrier((returned, home_cross_sibling))
     chip_cross = (home_cross.astype(full) + neighbour(home_cross_sibling, 1).astype(full)).astype(half)
 
     rel_part = call(operators_body, sds((relations, extra, width), full), (), [SMEM, VMEM])(
@@ -691,8 +690,12 @@
     near = lax.ppermute(pair, "dev", [(d, d ^ 1) for d in range(peers)])
     low = (place_id & 1) == 0
     planes = jnp.stack([jnp.where(low, pair, near), jnp.where(low, near, pair)])
-    planes, chip_cross, returned = lax.optimization_barrier((planes, chip_cross, returned))
+    home_sibling, home_own = home((1, 0), returned)
+    planes, chip_cross, home_sibling, home_own = lax.optimization_barrier(
+        (planes, chip_cross, home_sibling, home_own)
+    )
     from_cross = neighbour(chip_cross, 2)
+    from_sibling = neighbour(home_sibling, 1)
     gathered = lax.all_to_all(
         jnp.broadcast_to(planes[None], (peers // 2,) + planes.shape),
         "dev",
@@ -702,8 +705,6 @@
         tiled=True,
     ).reshape((peers,) + pair.shape)
 
-    home_sibling, home_own = home((1, 0), returned)
-    from_sibling = neighbour(home_sibling, 1)
     entity_new, acc_new = entity_update(
         own_grad, home_own, from_sibling, from_cross, entity, entity_acc
     )

time: 243 us -> 243 us (level)
  local copies, waits for them, and re-layouts: 9.81 us -> 33.1 us
  Pallas kernels: 107 us -> 91.5 us
  waiting for transfers between devices: 74.7 us -> 65.2 us
    unnamed x18 -> x78, local copies, waits for them, and re-layouts: 3.44 us -> 30.6 us
    pallas_call x2, Pallas kernels: 16.4 us -> 10.5 us  [home(): call(functools.partial(home_body, parts), tuple((sds((rows, width), half)...]
    all_to_all x1, waiting for transfers between devices: 6.79 us -> 1.96 us  [on_device(): lax.all_to_all(found, 'dev', split_axis=0, concat_axis=0, tiled=True)]
    pallas_call x1, Pallas kernels: 11.8 us -> 7.84 us  [on_device(): call(sums_body, (sds((rows, width), full), sds((rows, width), full)), (),...]
    ppermute x1, waiting for transfers between devices: 2.97 us -> 0.01 us  [on_device(): near = lax.ppermute(pair, 'dev', [(d, d ^ 1) for d in range(peers)])]
    all_to_all x1, waiting for transfers between devices: 19.7 us -> 17.2 us  [on_device(): lax.all_to_all(outgoing, 'dev', split_axis=0, concat_axis=0, tiled=True)]
  transfers between devices with their start and end apart: 14 -> 14, of which waited for: 9 -> 8; matrix products, arithmetic and copies ran while one was open for 1% -> 0% of each run, Pallas kernels for 24% -> 22%
where the time goes in v6:
time: 243 us; the launch traced here: 242 us
  Pallas kernels  91.5 us (38%)
  waiting for transfers between devices  65.2 us (27%)
  starting transfers between devices  45.7 us (19%)
  local copies, waits for them, and re-layouts  33.1 us (14%)
  other arithmetic  3.95 us (2%)
    unnamed x78, local copies, waits for them, and re-layouts  30.6 us
    ppermute x9, waiting for transfers between devices, neighbour(): return lax.ppermute(x, 'grp', [(g, g ^ flip) for g in range(4)])  30.4 us
    pallas_call x1, Pallas kernels, model(): call(model_body, (sds((peers, room + blocks * (width // peers), width), h...  21.9 us
    pallas_call x1, Pallas kernels, front(): call(front_body, (sds((edges, width), half), sds((blocks * negs, width),...  18.1 us
    all_to_all x1, waiting for transfers between devices, on_device(): lax.all_to_all(outgoing, 'dev', split_axis=0, concat_axis=0, tiled=True)  17.2 us
    ppermute x9, starting transfers between devices, neighbour(): return lax.ppermute(x, 'grp', [(g, g ^ flip) for g in range(4)])  15.1 us
    all_to_all x1, waiting for transfers between devices, on_device(): lax.all_to_all(wanted, 'dev', split_axis=0, concat_axis=0, tiled=True)  14.3 us
    pallas_call x2, Pallas kernels, relation_update(): pl.pallas_call(relation_body, grid_spec=pltpu.PrefetchScalarGridSpec(num_...  11.8 us
  transfers between devices with their start and end apart: 14, of which 8 were waited for; matrix products, arithmetic and copies ran while one was open for 0% of the time, Pallas kernels for 22%

profile of v6, /device:TPU:1, one launch (start us, length us, event | category | flops | bytes accessed | tf_op | source)
XLA Modules:
  0.0 241.8 jit_solution(14624226965133742205)
XLA Ops:
  2.4 2.2 collective-permute-start
  4.6 2.8 %shard_map.147 = (s32[1,2048]{1,0:T(1,128)S(1)}, s32[32,2,128]{2,1,0:T(2,128)}) custom-call(s32[1,2]{1,0:T(1,128)S(1)} %copy-done.25, s32[1,2048]{1,0:T(1,128)S(1)} %bitcast.26, s32[1,2048]{1,0:T(1,128)S(1)} %copy-done.24), custom_call_target="tpu_custom_call" | custom-call | tf_op jit(solution)/shard_map/pallas_call | solution.py:628
  7.4 10.2 %all-to-all-start = ((s32[32,2,128]{2,1,0:T(2,128)}), s32[32,2,128]{2,1,0:T(2,128)S(1)}, u32[]{:S(2)}, u32[]{:S(2)}) async-start(s32[32,2,128]{2,1,0:T(2,128)} %get-tuple-element.40), calls=%async_computation | async-start | bytes 65536 | tf_op jit(solution)/shard_map/all_to_all | solution.py:633
  19.0 14.3 %all-to-all-done.asked_ref = s32[32,2,128]{2,1,0:T(2,128)S(1)} async-done(((s32[32,2,128]{2,1,0:T(2,128)}), s32[32,2,128]{2,1,0:T(2,128)S(1)}, u32[]{:S(2)}, u32[]{:S(2)}) %all-to-all-start) | async-done | bytes 32800 | tf_op jit(solution)/shard_map/all_to_all | solution.py:633
  35.1 2.4 collective-permute-done.2.refs_3_.cross_sibling_table
  37.6 9.5 %shard_map.148 = bf16[32,128,256]{2,1,0:T(8,128)(2,1)} custom-call(s32[4,32]{1,0:T(4,128)S(1)} %copy-done.22, s32[1]{0:T(128)} %bitcast.3.group_ref, s32[32,2,128]{2,1,0:T(2,128)S(1)} %all-to-all-done.asked_ref, bf16[2048,256]{1,0:T(8,128)(2,1)S(1)} %convert_bitcast_fusion.refs_0_.own_table, ...), custom_call_target="tpu_custom_call" | custom-call | tf_op jit(solution)/shard_map/pallas_call | solution.py:639
  47.1 5.5 %all-to-all-start.1 = ((bf16[32,128,256]{2,1,0:T(8,128)(2,1)}), bf16[32,128,256]{2,1,0:T(8,128)(2,1)S(1)}, u32[]{:S(2)}, u32[]{:S(2)}) async-start(bf16[32,128,256]{2,1,0:T(8,128)(2,1)} %shard_map.148), calls=%async_computation.1 | async-start | bytes 4194304 | tf_op jit(solution)/shard_map/all_to_all | solution.py:651
  57.0 18.1 %shard_map.149 = (bf16[2048,256]{1,0:T(8,128)(2,1)S(1)}, bf16[2048,256]{1,0:T(8,128)(2,1)S(1)}, bf16[2048,256]{1,0:T(8,128)(2,1)S(1)}, bf16[2048,1024]{1,0:T(8,1...) custom-call(s32[1,2]{1,0:T(1,128)S(1)} %copy-done.25, s32[1]{0:T(128)} %bitcast.6.visit_ref.visit_to_ref, ...), custom_call_target="tpu_custom_call" | custom-call | flops 8589934592 | bytes 12582912 | tf_op jit(solution)/shard_map/pallas_call | solution.py:364
  80.5 2.0 all-to-all-done.1
  88.9 21.9 %shard_map.150 = (bf16[32,144,256]{2,1,0:T(8,128)(2,1)S(1)}, bf16[2048,256]{1,0:T(8,128)(2,1)S(1)}, bf16[2048,256]{1,0:T(8,128)(2,1)S(1)}, bf16[2048,256]{1,0:T(8,128)(2,1)S(1)}) custom-call(s32[1,2]{1,0:T(1,128)S(1)} %copy-done.25, s32[1,1]{1,0:T(1,128)S(6)} %copy.21.count_ref, s32[1,2048]{1,0:T(1,128)S(1)} %get-tuple-element.42.slot_ref, ...), custom_call_target="tpu_custom_call" | custom-call | tf_op jit(solution)/shard_map/pallas_call | solution.py:394
  115.3 8.0 %all-to-all-start.2 = ((bf16[32,144,256]{2,1,0:T(8,128)(2,1)}), bf16[32,144,256]{2,1,0:T(8,128)(2,1)S(1)}, u32[]{:S(2)}, u32[]{:S(2)}) async-start(bf16[32,144,256]{2,1,0:T(8,128)(2,1)} %copy-done.3), calls=%async_computation.2 | async-start | bytes 4718592 | tf_op jit(solution)/shard_map/all_to_all | solution.py:657
  127.0 7.8 %shard_map.151 = (f32[2048,256]{1,0:T(8,128)S(1)}, f32[2048,256]{1,0:T(8,128)S(1)}) custom-call(s32[1,2048]{1,0:T(1,128)S(1)} %copy-done.34, s32[2,1024]{1,0:T(2,128)S(1)} %bitcast.28, s32[2,1024]{1,0:T(2,128)S(1)} %bitcast.30, bf16[2048,256]{1,0:T(8,128)(2,1)S(1)} %copy-done.29, bf16[2048,256]{1,0:T(8,128)(2,1)S(1)} %copy-done.31, ...), custom_call_target="tpu_custom_call" | custom-call | flops 6442450944 | bytes 7340032 | tf_op jit(solution)/shard_map/pallas_call | solution.py:659
  137.5 17.2 %all-to-all-done.2.returned_ref = bf16[32,144,256]{2,1,0:T(8,128)(2,1)S(1)} async-done(((bf16[32,144,256]{2,1,0:T(8,128)(2,1)}), bf16[32,144,256]{2,1,0:T(8,128)(2,1)S(1)}, u32[]{:S(2)}, u32[]{:S(2)}) %all-to-all-start.2) | async-done | bytes 2359328 | tf_op jit(solution)/shard_map/all_to_all | solution.py:657
  159.5 5.3 %shard_map.153 = (bf16[2048,256]{1,0:T(8,128)(2,1)}, bf16[2048,256]{1,0:T(8,128)(2,1)S(1)}) custom-call(s32[4,32]{1,0:T(4,128)S(1)} %copy-done.22, s32[1]{0:T(128)} %bitcast.3.group_ref, s32[1]{0:T(128)} %bitcast.6.visit_ref.visit_to_ref, s32[32,2,128]{2,1,0:T(2,128)S(1)} %all-to-all-done.asked_ref, bf16[32,144,256]{2,1,0:T(8,128)(2,1)S(1)} %all-to-all-done.2.returned_ref, ...), custom_call_target="tpu_custom_call" | custom-call | bytes 25165824 | tf_op jit(solution)/shard_map/pallas_call | solution.py:670
  167.3 2.3 collective-permute-start.4
  169.6 4.1 %collective-permute-done.4 = f32[20,8,256]{2,1,0:T(8,128)S(1)} collective-permute-done((f32[20,8,256]{2,1,0:T(8,128)S(1)}, f32[20,8,256]{2,1,0:T(8,128)S(1)}, u32[]{:S(2)}, u32[]{:S(2)}) %collective-permute-start.4) | collective-permute-done | bytes 163872 | tf_op jit(solution)/shard_map/ppermute | solution.py:617
  176.8 5.2 %shard_map.154 = (bf16[2048,256]{1,0:T(8,128)(2,1)S(1)}, bf16[2048,256]{1,0:T(8,128)(2,1)S(1)}) custom-call(s32[4,32]{1,0:T(4,128)S(1)} %copy-done.22, s32[1]{0:T(128)} %bitcast.3.group_ref, s32[1]{0:T(128)} %bitcast.6.visit_ref.visit_to_ref, s32[32,2,128]{2,1,0:T(2,128)S(1)} %all-to-all-done.asked_ref, ...), custom_call_target="tpu_custom_call" | custom-call | bytes 25165824 | tf_op jit(solution)/shard_map/pallas_call | solution.py:670
  182.1 2.2 add_convert_fusion
  186.1 5.3 %all-to-all-start.3 = ((bf16[16,2,20,8,256]{4,3,2,1,0:T(8,128)(2,1)}), bf16[16,2,20,8,256]{4,3,2,1,0:T(8,128)(2,1)}, u32[]{:S(2)}, u32[]{:S(2)}) async-start(bf16[16,2,20,8,256]{4,3,2,1,0:T(8,128)(2,1)} %broadcast_in_dim.2), calls=%async_computation.3 | async-start | bytes 5242880 | tf_op jit(solution)/shard_map/all_to_all | solution.py:699
  194.4 22.5 %collective-permute-done.8.cross_ref = bf16[2048,256]{1,0:T(8,128)(2,1)} collective-permute-done((bf16[2048,256]{1,0:T(8,128)(2,1)S(1)}, bf16[2048,256]{1,0:T(8,128)(2,1)}, u32[]{:S(2)}, u32[]{:S(2)}) %collective-permute-start.8) | collective-permute-done | bytes 1048608 | tf_op jit(solution)/shard_map/ppermute | solution.py:617
  217.0 7.9 %shard_map.155 = (f32[1,2048,256]{2,1,0:T(8,128)}, f32[1,2048]{1,0:T(1,128)}) custom-call(f32[2048,256]{1,0:T(8,128)} %copy-done.4, bf16[2048,256]{1,0:T(8,128)(2,1)} %copy-done.13, bf16[2048,256]{1,0:T(8,128)(2,1)} %copy-done.38, bf16[2048,256]{1,0:T(8,128)(2,1)} %collective-permute-done.8.cross_ref, f32[1,2048,256]{2,1,0:T(8,128)} %entity_ref.1, ...), custom_call_target="tpu_custom_call" | custom-call | bytes 25165824 | tf_op jit(solution)/shard_map/pallas_call | solution.py:576
  226.2 2.4 %collective-permute-start.9 = (bf16[32,20,8,256]{3,2,1,0:T(8,128)(2,1)}, bf16[32,20,8,256]{3,2,1,0:T(8,128)(2,1)S(1)}, u32[]{:S(2)}, u32[]{:S(2)}) collective-permute-start(bf16[32,20,8,256]{3,2,1,0:T(8,128)(2,1)} %bitcast.14.grad_ref), channel_id=1, source_target_pairs={{0,32},{32,0},{64,96},{96,64},{1,33},{33,1},{65,97},{97,65},{2,34}... | collective-permute-start | bytes 7864328 | tf_op jit(solution)/shard_map/ppermute | solution.py:617
  228.6 5.9 %shard_map.156 = (f32[40,256,256]{2,1,0:T(8,128)}, f32[40,256]{1,0:T(8,128)}) custom-call(s32[1]{0:T(128)} %bitcast.16.part_ref, bf16[32,20,8,256]{3,2,1,0:T(8,128)(2,1)} %bitcast.14.grad_ref, f32[40,256,256]{2,1,0:T(8,128)} %relation_ref.7, f32[40,256]{1,0:T(8,128)} %acc_ref.5), custom_call_target="tpu_custom_call" | custom-call | bytes 25165824 | tf_op jit(solution)/shard_map/pallas_call | solution.py:546
  235.9 5.9 %shard_map.157 = (f32[40,256,256]{2,1,0:T(8,128)}, f32[40,256]{1,0:T(8,128)}) custom-call(s32[1]{0:T(128)} %bitcast.15.part_ref, bf16[32,20,8,256]{3,2,1,0:T(8,128)(2,1)} %copy-done.37, f32[40,256,256]{2,1,0:T(8,128)} %relation_ref.7, f32[40,256]{1,0:T(8,128)} %acc_ref.5, ...), custom_call_target="tpu_custom_call", output_to_operand_aliasing={{0}: (4, {})} | custom-call | bytes 25165824 | tf_op jit(solution)/shard_map/pallas_call | solution.py:546
  (104 shorter events, 48.3 us)
Async XLA Ops:
  0.6 4.0 %copy-start.25 = (s32[1,2]{1,0:T(1,128)S(1)}, s32[1,2]{1,0:T(1,128)}, u32[]{:S(2)}) copy-start(s32[1,2]{1,0:T(1,128)} %rel_ref.5) | copy-start | bytes 28
  0.7 36.9 %copy-start.22 = (s32[4,32]{1,0:T(4,128)S(1)}, s32[4,32]{1,0:T(4,128)}, u32[]{:S(2)}) copy-start(s32[4,32]{1,0:T(4,128)} %partner_ref.5) | copy-start | bytes 1540
  2.4 30.9 %collective-permute-start = (bf16[2048,256]{1,0:T(8,128)(2,1)S(1)}, bf16[2048,256]{1,0:T(8,128)(2,1)S(1)}, u32[]{:S(2)}, u32[]{:S(2)}) collective-permute-start(bf16[2048,256]{1,0:T(8,128)(2,1)S(1)} %convert_bitcast_fusion.refs_0_.own_table), channel_id=1, source_target_pairs={{0,64},{32,96},{64,0},{96,32},{1,65},{33,97},{65,1},{97,33},{2,66}... | collective-permute-start | bytes 3145736 | tf_op jit(solution)/shard_map/ppermute | solution.py:617
  7.4 25.8 %all-to-all-start = ((s32[32,2,128]{2,1,0:T(2,128)}), s32[32,2,128]{2,1,0:T(2,128)S(1)}, u32[]{:S(2)}, u32[]{:S(2)}) async-start(s32[32,2,128]{2,1,0:T(2,128)} %get-tuple-element.40), calls=%async_computation | async-start | bytes 65536 | tf_op jit(solution)/shard_map/all_to_all | solution.py:633
  17.7 17.5 %collective-permute-start.1 = (bf16[2048,256]{1,0:T(8,128)(2,1)S(1)}, bf16[2048,256]{1,0:T(8,128)(2,1)S(1)}, u32[]{:S(2)}, u32[]{:S(2)}) collective-permute-start(bf16[2048,256]{1,0:T(8,128)(2,1)S(1)} %convert_bitcast_fusion.refs_0_.own_table), channel_id=1, source_target_pairs={{0,32},{32,0},{64,96},{96,64},{1,33},{33,1},{65,97},{97,65},{2,34}... | collective-permute-start | bytes 3145736 | tf_op jit(solution)/shard_map/ppermute | solution.py:617
  33.3 13.8 %copy-start.9 = (bf16[2048,256]{1,0:T(8,128)(2,1)}, bf16[2048,256]{1,0:T(8,128)(2,1)S(1)}, u32[]{:S(2)}) copy-start(bf16[2048,256]{1,0:T(8,128)(2,1)S(1)} %collective-permute-done.refs_2_.cross_table) | copy-start | bytes 3145732
  33.3 4.3 %collective-permute-start.2 = (bf16[2048,256]{1,0:T(8,128)(2,1)S(1)}, bf16[2048,256]{1,0:T(8,128)(2,1)}, u32[]{:S(2)}, u32[]{:S(2)}) collective-permute-start(bf16[2048,256]{1,0:T(8,128)(2,1)S(1)} %collective-permute-done.refs_2_.cross_table), channel_id=1, source_target_pairs={{0,32},{32,0},{64,96},{96,64},{1,33},{33,1},{65,97},{97,65},{2,34}... | collective-permute-start | bytes 3145736 | tf_op jit(solution)/shard_map/ppermute | solution.py:617
  35.1 11.9 %copy-start.11 = (bf16[2048,256]{1,0:T(8,128)(2,1)}, bf16[2048,256]{1,0:T(8,128)(2,1)S(1)}, u32[]{:S(2)}) copy-start(bf16[2048,256]{1,0:T(8,128)(2,1)S(1)} %collective-permute-done.1.refs_1_.sibling_table) | copy-start | bytes 3145732
  47.1 7.5 %copy-start.34 = (s32[1,2048]{1,0:T(1,128)S(1)}, s32[1,2048]{1,0:T(1,128)}, u32[]{:S(2)}) copy-start(s32[1,2048]{1,0:T(1,128)} %src_ref.3) | copy-start | bytes 24580
  47.1 7.5 %copy-start.35 = (s32[1,2,1024]{2,1,0:T(2,128)S(1)}, s32[1,2,1024]{2,1,0:T(2,128)}, u32[]{:S(2)}) copy-start(s32[1,2,1024]{2,1,0:T(2,128)} %param.21) | copy-start | bytes 24580
  47.1 7.5 %copy-start.36 = (s32[1,2,1024]{2,1,0:T(2,128)S(1)}, s32[1,2,1024]{2,1,0:T(2,128)}, u32[]{:S(2)}) copy-start(s32[1,2,1024]{2,1,0:T(2,128)} %param.22) | copy-start | bytes 24580
  47.1 35.3 %all-to-all-start.1 = ((bf16[32,128,256]{2,1,0:T(8,128)(2,1)}), bf16[32,128,256]{2,1,0:T(8,128)(2,1)S(1)}, u32[]{:S(2)}, u32[]{:S(2)}) async-start(bf16[32,128,256]{2,1,0:T(8,128)(2,1)} %shard_map.148), calls=%async_computation.1 | async-start | bytes 4194304 | tf_op jit(solution)/shard_map/all_to_all | solution.py:651
  115.3 39.5 %all-to-all-start.2 = ((bf16[32,144,256]{2,1,0:T(8,128)(2,1)}), bf16[32,144,256]{2,1,0:T(8,128)(2,1)S(1)}, u32[]{:S(2)}, u32[]{:S(2)}) async-start(bf16[32,144,256]{2,1,0:T(8,128)(2,1)} %copy-done.3), calls=%async_computation.2 | async-start | bytes 4718592 | tf_op jit(solution)/shard_map/all_to_all | solution.py:657
  156.0 11.3 %collective-permute-start.3 = (f32[20,8,256]{2,1,0:T(8,128)S(1)}, f32[20,8,256]{2,1,0:T(8,128)S(1)}, u32[]{:S(2)}, u32[]{:S(2)}) collective-permute-start(f32[20,8,256]{2,1,0:T(8,128)S(1)} %dynamic-slice_bitcast_fusion), channel_id=1, source_target_pairs={{0,32},{32,0},{64,96},{96,64},{1,33},{33,1},{65,97},{97,65},{2,34}... | collective-permute-start | bytes 491528 | tf_op jit(solution)/shard_map/ppermute | solution.py:617
  165.8 16.3 %collective-permute-start.6 = (bf16[2048,256]{1,0:T(8,128)(2,1)}, bf16[2048,256]{1,0:T(8,128)(2,1)}, u32[]{:S(2)}, u32[]{:S(2)}) collective-permute-start(bf16[2048,256]{1,0:T(8,128)(2,1)} %get-tuple-element.59), channel_id=1, source_target_pairs={{0,32},{32,0},{64,96},{96,64},{1,33},{33,1},{65,97},{97,65},{2,34}... | collective-permute-start | bytes 3145736 | tf_op jit(solution)/shard_map/ppermute | solution.py:617
  167.3 6.4 %collective-permute-start.4 = (f32[20,8,256]{2,1,0:T(8,128)S(1)}, f32[20,8,256]{2,1,0:T(8,128)S(1)}, u32[]{:S(2)}, u32[]{:S(2)}) collective-permute-start(f32[20,8,256]{2,1,0:T(8,128)S(1)} %bitcast_add_fusion), channel_id=1, source_target_pairs={{0,64},{32,96},{64,0},{96,32},{1,65},{33,97},{65,1},{97,33},{2,66}... | collective-permute-start | bytes 491528 | tf_op jit(solution)/shard_map/ppermute | solution.py:617
  173.7 8.3 %collective-permute-start.5 = (bf16[20,8,256]{2,1,0:T(8,128)(2,1)S(1)}, bf16[20,8,256]{2,1,0:T(8,128)(2,1)S(1)}, u32[]{:S(2)}, u32[]{:S(2)}) collective-permute-start(bf16[20,8,256]{2,1,0:T(8,128)(2,1)S(1)} %add_convert_fusion.1), channel_id=1, source_target_pairs={{0,1},{1,0},{2,3},{3,2},{4,5},{5,4},{6,7},{7,6},{8,9},{9,8},{10,11... | collective-permute-start | bytes 245768 | tf_op jit(solution)/shard_map/ppermute | solution.py:690
  176.8 5.3 %copy-start.8 = (bf16[2048,256]{1,0:T(8,128)(2,1)S(1)}, bf16[2048,256]{1,0:T(8,128)(2,1)}, u32[]{:S(2)}) copy-start(bf16[2048,256]{1,0:T(8,128)(2,1)} %copy-done.7) | copy-start | bytes 3145732
  186.1 5.3 %copy-start.27 = (bf16[2048,256]{1,0:T(8,128)(2,1)S(1)}, bf16[2048,256]{1,0:T(8,128)(2,1)}, u32[]{:S(2)}) copy-start(bf16[2048,256]{1,0:T(8,128)(2,1)} %copy-done.26) | copy-start | bytes 3145732
  186.1 40.1 %all-to-all-start.3 = ((bf16[16,2,20,8,256]{4,3,2,1,0:T(8,128)(2,1)}), bf16[16,2,20,8,256]{4,3,2,1,0:T(8,128)(2,1)}, u32[]{:S(2)}, u32[]{:S(2)}) async-start(bf16[16,2,20,8,256]{4,3,2,1,0:T(8,128)(2,1)} %broadcast_in_dim.2), calls=%async_computation.3 | async-start | bytes 5242880 | tf_op jit(solution)/shard_map/all_to_all | solution.py:699
  191.4 3.0 %collective-permute-start.7 = (bf16[2048,256]{1,0:T(8,128)(2,1)S(1)}, bf16[2048,256]{1,0:T(8,128)(2,1)S(1)}, u32[]{:S(2)}, u32[]{:S(2)}) collective-permute-start(bf16[2048,256]{1,0:T(8,128)(2,1)S(1)} %copy-done.27), channel_id=1, source_target_pairs={{0,32},{32,0},{64,96},{96,64},{1,33},{33,1},{65,97},{97,65},{2,34}... | collective-permute-start | bytes 3145736 | tf_op jit(solution)/shard_map/ppermute | solution.py:617
  192.2 24.8 %collective-permute-start.8 = (bf16[2048,256]{1,0:T(8,128)(2,1)S(1)}, bf16[2048,256]{1,0:T(8,128)(2,1)}, u32[]{:S(2)}, u32[]{:S(2)}) collective-permute-start(bf16[2048,256]{1,0:T(8,128)(2,1)S(1)} %add_convert_fusion), channel_id=1, source_target_pairs={{0,64},{32,96},{64,0},{96,32},{1,65},{33,97},{65,1},{97,33},{2,66}... | collective-permute-start | bytes 3145736 | tf_op jit(solution)/shard_map/ppermute | solution.py:617
  194.4 22.5 %copy-start.38 = (bf16[2048,256]{1,0:T(8,128)(2,1)}, bf16[2048,256]{1,0:T(8,128)(2,1)S(1)}, u32[]{:S(2)}) copy-start(bf16[2048,256]{1,0:T(8,128)(2,1)S(1)} %collective-permute-done.7.sibling_ref) | copy-start | bytes 3145732
  226.2 8.3 %collective-permute-start.9 = (bf16[32,20,8,256]{3,2,1,0:T(8,128)(2,1)}, bf16[32,20,8,256]{3,2,1,0:T(8,128)(2,1)S(1)}, u32[]{:S(2)}, u32[]{:S(2)}) collective-permute-start(bf16[32,20,8,256]{3,2,1,0:T(8,128)(2,1)} %bitcast.14.grad_ref), channel_id=1, source_target_pairs={{0,32},{32,0},{64,96},{96,64},{1,33},{33,1},{65,97},{97,65},{2,34}... | collective-permute-start | bytes 7864328 | tf_op jit(solution)/shard_map/ppermute | solution.py:617
  (29 other events, 43.1 us)

commit v7 on v6

--- a/solution.py
+++ b/solution.py
@@ -41,7 +41,7 @@
     return jnp.where(row == line, 1.0, 0.0).astype(half)
 
 
-def call(body, shapes, scratch=(), specs=None, cost=None, outs=None, mebi=40, **kw):
+def call(body, shapes, scratch=(), specs=None, cost=None, outs=None, mebi=60, **kw):
     return pl.pallas_call(
         body,
         out_shape=shapes,
@@ -227,7 +227,8 @@
     terms_in,
     pull_in,
     stats_in,
-    outgoing_ref,
+    d_op_ref,
+    d_dst_out,
     d_src_out,
     d_neg_src_out,
     d_neg_dst_out,
@@ -256,9 +257,8 @@
     blocks = rel_ref.shape[1]
     block_len = edges // blocks
     negs = neg_src_ref.shape[0] // blocks
-    peers, room, _ = outgoing_ref.shape
+    peers = d_op_ref.shape[0]
     extra = width // peers
-    places = slots // peers
     step = 256
     copies = operators_in(rel_ref, relation_ref, operator, op_sems)
     pairs = (
@@ -335,25 +335,33 @@
         d_neg_dst_ref[block * negs : (block + 1) * negs, :] = neg_dst_sum[...].T.astype(half)
         d_neg_src_ref[block * negs : (block + 1) * negs, :] = neg_src_sum[...].T.astype(half)
         d_op = op_sum[...].astype(half) + op_turned_sum[...].astype(half)
-        outgoing_ref[:, places + block * extra : places + (block + 1) * extra, :] = d_op.reshape(
-            peers, extra, width
-        )
+        d_op_ref[:, block * extra : (block + 1) * extra, :] = d_op.reshape(peers, extra, width)
     backs = []
     for i, (here, there) in enumerate(
-        ((d_src_ref, d_src_out), (d_neg_src_ref, d_neg_src_out), (d_neg_dst_ref, d_neg_dst_out))
+        (
+            (d_dst, d_dst_out),
+            (d_src_ref, d_src_out),
+            (d_neg_src_ref, d_neg_src_out),
+            (d_neg_dst_ref, d_neg_dst_out),
+        )
     ):
         backs.append(pltpu.make_async_copy(here, there, out_sems.at[i]))
         backs[-1].start()
 
+    for copy in backs:
+        copy.wait()
+
+
+def send_body(slot_ref, d_dst, outgoing_ref):
+    peers, places, width = outgoing_ref.shape
+
     def send(t, carry):
         spot = place(slot_ref[...], t * 2 * places, 2 * places)
         out = dot(spot, d_dst[...], 1, 0).astype(half)
-        outgoing_ref[pl.ds(2 * t, 2), :places, :] = out.reshape(2, places, width)
+        outgoing_ref[pl.ds(2 * t, 2), :, :] = out.reshape(2, places, width)
         return carry
 
     lax.fori_loop(0, peers // 2, send, 0, unroll=4)
-    for copy in backs:
-        copy.wait()
 
 
 def front(rel_ids, visit_to, src_row, neg_src, neg_dst, relation, tables):
@@ -385,7 +393,7 @@
     )(rel_ids, visit_to, src_row, neg_src, neg_dst, relation, *tables)
 
 
-def model(rel_ids, edge_count, slot, fetched, relation, peers, room, rest):
+def model(rel_ids, edge_count, slot, fetched, relation, peers, rest):
     slots, width = fetched.shape
     edges = slot.shape[1]
     blocks = rel_ids.shape[1]
@@ -394,7 +402,8 @@
     return call(
         model_body,
         (
-            sds((peers, room + blocks * (width // peers), width), half),
+            sds((peers, blocks * (width // peers), width), half),
+            sds((edges, width), half),
             sds((edges, width), half),
             sds((blocks * negs, width), half),
             sds((blocks * negs, width), half),
@@ -413,10 +422,10 @@
             pltpu.VMEM((width, width), full),
             pltpu.SemaphoreType.DMA((blocks,)),
             pltpu.SemaphoreType.DMA((6,)),
-            pltpu.SemaphoreType.DMA((3,)),
+            pltpu.SemaphoreType.DMA((4,)),
         ],
         [SMEM] * 2 + [VMEM] * 2 + [HBM] * 7,
-        outs=[VMEM] + [HBM] * 3,
+        outs=[VMEM] + [HBM] * 4,
     )(rel_ids, edge_count, slot, fetched, relation, *rest)
 
 
@@ -651,35 +660,24 @@
     fetched = lax.all_to_all(found, "dev", split_axis=0, concat_axis=0, tiled=True)
 
     rest = front(rel_ids, visit_to, src_row, neg_src, neg_dst, relation, tables)
-    outgoing, d_src, d_neg_src, d_neg_dst = model(
-        rel_ids, edge_count, slot, fetched.reshape(peers * room, width), relation, peers, room, rest
+    d_op, d_dst, d_src, d_neg_src, d_neg_dst = model(
+        rel_ids, edge_count, slot, fetched.reshape(peers * room, width), relation, peers, rest
+    )
+    d_op_here = lax.all_to_all(d_op, "dev", split_axis=0, concat_axis=0, tiled=True)
+    outgoing = call(
+        send_body,
+        sds((peers, room, width), half),
+        (),
+        [VMEM] * 2,
+        cost(2 * peers * room * edges * width, 4 * MEBI),
+    )(slot, d_dst)
+    d_op_here, outgoing, d_src, d_neg_src, d_neg_dst = lax.optimization_barrier(
+        (d_op_here, outgoing, d_src, d_neg_src, d_neg_dst)
     )
     returned = lax.all_to_all(outgoing, "dev", split_axis=0, concat_axis=0, tiled=True)
 
-    own_grad, visit_grad = call(
-        sums_body,
-        (sds((rows, width), full), sds((rows, width), full)),
-        (),
-        [VMEM] * 6,
-        cost(2 * 3 * edges * rows * width, 7 * rows * width * 2),
-    )(src_row, neg_src, neg_dst, d_src, d_neg_src, d_neg_dst)
-
-    returned, own_grad, visit_grad = lax.optimization_barrier((returned, own_grad, visit_grad))
-
-    def home(parts, returned):
-        return call(
-            functools.partial(home_body, parts),
-            tuple(sds((rows, width), half) for _ in parts),
-            [pltpu.VMEM((rows, width), full)] + lists,
-            [SMEM] * 3 + [VMEM] * 3,
-            cost(0, 24 * MEBI),
-        )(partner, group, visit_to, asked, returned, visit_grad)
-
-    home_cross_sibling, home_cross = home((3, 2), returned)
-    chip_cross = (home_cross.astype(full) + neighbour(home_cross_sibling, 1).astype(full)).astype(half)
-
     rel_part = call(operators_body, sds((relations, extra, width), full), (), [SMEM, VMEM])(
-        asked[:, 1, :blocks], returned[:, room:, :]
+        asked[:, 1, :blocks], d_op_here
     )
     core = me & 1
     halves = rel_part.reshape(2, relations // 2, extra, width)
@@ -690,12 +688,30 @@
     near = lax.ppermute(pair, "dev", [(d, d ^ 1) for d in range(peers)])
     low = (place_id & 1) == 0
     planes = jnp.stack([jnp.where(low, pair, near), jnp.where(low, near, pair)])
-    home_sibling, home_own = home((1, 0), returned)
-    planes, chip_cross, home_sibling, home_own = lax.optimization_barrier(
-        (planes, chip_cross, home_sibling, home_own)
-    )
+    own_grad, visit_grad = call(
+        sums_body,
+        (sds((rows, width), full), sds((rows, width), full)),
+        (),
+        [VMEM] * 6,
+        cost(2 * 3 * edges * rows * width, 7 * rows * width * 2),
+    )(src_row, neg_src, neg_dst, d_src, d_neg_src, d_neg_dst)
+
+    returned, own_grad, visit_grad, planes = lax.optimization_barrier(
+        (returned, own_grad, visit_grad, planes)
+    )
+
+    def home(parts, returned):
+        return call(
+            functools.partial(home_body, parts),
+            tuple(sds((rows, width), half) for _ in parts),
+            [pltpu.VMEM((rows, width), full)] + lists,
+            [SMEM] * 3 + [VMEM] * 3,
+            cost(0, 24 * MEBI),
+        )(partner, group, visit_to, asked, returned, visit_grad)
+
+    home_cross_sibling, home_cross = home((3, 2), returned)
+    chip_cross = (home_cross.astype(full) + neighbour(home_cross_sibling, 1).astype(full)).astype(half)
     from_cross = neighbour(chip_cross, 2)
-    from_sibling = neighbour(home_sibling, 1)
     gathered = lax.all_to_all(
         jnp.broadcast_to(planes[None], (peers // 2,) + planes.shape),
         "dev",
@@ -705,10 +721,12 @@
         tiled=True,
     ).reshape((peers,) + pair.shape)
 
+    home_sibling, home_own = home((1, 0), returned)
+    from_sibling = neighbour(home_sibling, 1)
+    gathered, from_cross = lax.optimization_barrier((gathered, from_cross))
     entity_new, acc_new = entity_update(
         own_grad, home_own, from_sibling, from_cross, entity, entity_acc
     )
-    gathered, entity_new, acc_new = lax.optimization_barrier((gathered, entity_new, acc_new))
     other_half = neighbour(gathered, 1)
     before = relation_update(core.reshape(1), gathered, relation, relation_acc)
     relation_new, relation_acc_new = relation_update(

time: 243 us -> 259 us (1.066)
  local copies, waits for them, and re-layouts: 33.1 us -> 8.04 us
  Pallas kernels: 91.5 us -> 110 us
  waiting for transfers between devices: 65.2 us -> 77.3 us
  starting transfers between devices: 45.7 us -> 55.9 us
    unnamed x78 -> x18, local copies, waits for them, and re-layouts: 30.6 us -> 3.43 us
    all_to_all x1, waiting for transfers between devices: 17.2 us -> 0.01 us  [on_device(): lax.all_to_all(outgoing, 'dev', split_axis=0, concat_axis=0, tiled=True)]
    ppermute x9, waiting for transfers between devices: 30.4 us -> 45.8 us  [neighbour(): return lax.ppermute(x, 'grp', [(g, g ^ flip) for g in range(4)])]
    all_to_all x1, waiting for transfers between devices: 1.29 us -> 8.6 us  [on_device(): lax.all_to_all(jnp.broadcast_to(planes[None], (peers // 2,) + planes.shap...]
    all_to_all x0 -> x1, starting transfers between devices: none -> 6.71 us  [on_device(): lax.all_to_all(d_op, 'dev', split_axis=0, concat_axis=0, tiled=True)]
    pallas_call x1 -> x2, Pallas kernels: 21.9 us -> 27.6 us  [the longest x1 20 us: model(): call(model_body, (sds((peers, blocks * (width // peers), width), half), s...]
    pallas_call x2, Pallas kernels: 10.5 us -> 15.6 us  [home(): call(functools.partial(home_body, parts), tuple((sds((rows, width), half)...]
    all_to_all x1, waiting for transfers between devices: 1.96 us -> 6.83 us  [on_device(): lax.all_to_all(found, 'dev', split_axis=0, concat_axis=0, tiled=True)]
  transfers between devices with their start and end apart: 14 -> 15, of which waited for: 8 -> 8; matrix products, arithmetic and copies ran while one was open for 0% -> 3% of each run, Pallas kernels for 22% -> 26%
where the time goes in v7:
time: 259 us; the launch traced here: 258 us
  Pallas kernels  110 us (42%)
  waiting for transfers between devices  77.3 us (30%)
  starting transfers between devices  55.9 us (22%)
  local copies, waits for them, and re-layouts  8.04 us (3%)
  other arithmetic  4.49 us (2%)
    ppermute x9, waiting for transfers between devices, neighbour(): return lax.ppermute(x, 'grp', [(g, g ^ flip) for g in range(4)])  45.8 us
    pallas_call x1, Pallas kernels, front(): call(front_body, (sds((edges, width), half), sds((blocks * negs, width),...  20.2 us
    pallas_call x1, Pallas kernels, model(): call(model_body, (sds((peers, blocks * (width // peers), width), half), s...  20 us
    pallas_call x2, Pallas kernels, home(): call(functools.partial(home_body, parts), tuple((sds((rows, width), half)...  15.6 us
    all_to_all x1, waiting for transfers between devices, on_device(): lax.all_to_all(wanted, 'dev', split_axis=0, concat_axis=0, tiled=True)  14.1 us
    ppermute x9, starting transfers between devices, neighbour(): return lax.ppermute(x, 'grp', [(g, g ^ flip) for g in range(4)])  13.7 us
    pallas_call x2, Pallas kernels, relation_update(): pl.pallas_call(relation_body, grid_spec=pltpu.PrefetchScalarGridSpec(num_...  11.8 us
    pallas_call x1, Pallas kernels, on_device(): call(sums_body, (sds((rows, width), full), sds((rows, width), full)), (),...  11.8 us
  transfers between devices with their start and end apart: 15, of which 8 were waited for; matrix products, arithmetic and copies ran while one was open for 3% of the time, Pallas kernels for 26%

profile of v7, /device:TPU:1, one launch (start us, length us, event | category | flops | bytes accessed | tf_op | source)
XLA Modules:
  0.0 258.1 jit_solution(18136502530543003036)
XLA Ops:
  4.5 3.0 %shard_map.147 = (s32[1,2048]{1,0:T(1,128)}, s32[32,2,128]{2,1,0:T(2,128)}) custom-call(s32[1,2]{1,0:T(1,128)} %rel_ref.5, s32[1,2048]{1,0:T(1,128)} %bitcast.28, s32[1,2048]{1,0:T(1,128)} %row_ref.1), custom_call_target="tpu_custom_call" | custom-call | tf_op jit(solution)/shard_map/pallas_call | solution.py:637
  7.6 10.2 %all-to-all-start = ((s32[32,2,128]{2,1,0:T(2,128)}), s32[32,2,128]{2,1,0:T(2,128)S(1)}, u32[]{:S(2)}, u32[]{:S(2)}) async-start(s32[32,2,128]{2,1,0:T(2,128)} %get-tuple-element.43), calls=%async_computation | async-start | bytes 65536 | tf_op jit(solution)/shard_map/all_to_all | solution.py:642
  19.1 14.1 %all-to-all-done.asked_ref = s32[32,2,128]{2,1,0:T(2,128)S(1)} async-done(((s32[32,2,128]{2,1,0:T(2,128)}), s32[32,2,128]{2,1,0:T(2,128)S(1)}, u32[]{:S(2)}, u32[]{:S(2)}) %all-to-all-start) | async-done | bytes 32800 | tf_op jit(solution)/shard_map/all_to_all | solution.py:642
  35.2 2.4 collective-permute-done.2.refs_3_.cross_sibling_table
  37.6 10.4 %shard_map.148 = bf16[32,128,256]{2,1,0:T(8,128)(2,1)} custom-call(s32[4,32]{1,0:T(4,128)} %partner_ref.5, s32[1]{0:T(128)} %bitcast.1.group_ref, s32[32,2,128]{2,1,0:T(2,128)} %copy-done.7, bf16[2048,256]{1,0:T(8,128)(2,1)} %copy-done.3, bf16[2048,256]{1,0:T(8,128)(2,1)} %copy-done.6, bf16[2048,256]{1,0:T(8,128)(2,1)} %copy-done.5, ...), custom_call_target="tpu_custom_call" | custom-call | tf_op jit(solution)/shard_map/pallas_call | solution.py:648
  48.0 5.6 %all-to-all-start.1 = ((bf16[32,128,256]{2,1,0:T(8,128)(2,1)}), bf16[32,128,256]{2,1,0:T(8,128)(2,1)S(1)}, u32[]{:S(2)}, u32[]{:S(2)}) async-start(bf16[32,128,256]{2,1,0:T(8,128)(2,1)} %shard_map.148), calls=%async_computation.1 | async-start | bytes 4194304 | tf_op jit(solution)/shard_map/all_to_all | solution.py:660
  56.2 20.2 %shard_map.149 = (bf16[2048,256]{1,0:T(8,128)(2,1)}, bf16[2048,256]{1,0:T(8,128)(2,1)}, bf16[2048,256]{1,0:T(8,128)(2,1)}, bf16[2048,1024]{1,0:T(8,128)(2,1)}, f32[2048,256]{1,0:T(8,128)}, /*index=5*/f32[2048,128]{1,0:T(8,128)}) custom-call(s32[1,2]{1,0:T(1,128)} %rel_ref.5, s32[1]{0:T(128)} %bitcast.5.visit_ref.visit_to_ref, s32[1,2048]{1,0:T(1,128)} %src_ref.3, ...), custom_call_target="tpu_custom_call" | custom-call | flops 8589934592 | bytes 12582912 | tf_op jit(solution)/shard_map/pallas_call | solution.py:372
  76.4 6.8 %all-to-all-done.1 = bf16[32,128,256]{2,1,0:T(8,128)(2,1)S(1)} async-done(((bf16[32,128,256]{2,1,0:T(8,128)(2,1)}), bf16[32,128,256]{2,1,0:T(8,128)(2,1)S(1)}, u32[]{:S(2)}, u32[]{:S(2)}) %all-to-all-start.1) | async-done | bytes 2097184 | tf_op jit(solution)/shard_map/all_to_all | solution.py:660
  84.5 20.0 %shard_map.150 = (bf16[32,16,256]{2,1,0:T(8,128)(2,1)}, bf16[2048,256]{1,0:T(8,128)(2,1)}, bf16[2048,256]{1,0:T(8,128)(2,1)}, bf16[2048,256]{1,0:T(8,128)(2,1)}, bf16[2048,256]{1,0:T(8,128)(2,1)}) custom-call(s32[1,2]{1,0:T(1,128)} %rel_ref.5, s32[1,1]{1,0:T(1,128)S(6)} %copy.21.count_ref, s32[1,2048]{1,0:T(1,128)} %get-tuple-element.42.slot_ref, ...), custom_call_target="tpu_custom_call" | custom-call | tf_op jit(solution)/shard_map/pallas_call | solution.py:402
  104.5 6.7 %all-to-all-start.2 = ((bf16[32,16,256]{2,1,0:T(8,128)(2,1)}), bf16[32,16,256]{2,1,0:T(8,128)(2,1)S(1)}, u32[]{:S(2)}, u32[]{:S(2)}) async-start(bf16[32,16,256]{2,1,0:T(8,128)(2,1)} %get-tuple-element.52), calls=%async_computation.2 | async-start | bytes 524288 | tf_op jit(solution)/shard_map/all_to_all | solution.py:666
  111.2 7.6 %shard_map.151 = bf16[32,128,256]{2,1,0:T(8,128)(2,1)} custom-call(s32[1,2048]{1,0:T(1,128)} %get-tuple-element.42.slot_ref, bf16[2048,256]{1,0:T(8,128)(2,1)} %get-tuple-element.53.d_dst), custom_call_target="tpu_custom_call" | custom-call | flops 4294967296 | bytes 4194304 | tf_op jit(solution)/shard_map/pallas_call | solution.py:667
  121.5 7.5 %all-to-all-start.3 = ((bf16[32,128,256]{2,1,0:T(8,128)(2,1)}), bf16[32,128,256]{2,1,0:T(8,128)(2,1)S(1)}, u32[]{:S(2)}, u32[]{:S(2)}) async-start(bf16[32,128,256]{2,1,0:T(8,128)(2,1)} %shard_map.151), calls=%async_computation.3 | async-start | bytes 4194304 | tf_op jit(solution)/shard_map/all_to_all | solution.py:677
  137.0 17.8 %collective-permute-done.4 = f32[20,8,256]{2,1,0:T(8,128)S(1)} collective-permute-done((f32[20,8,256]{2,1,0:T(8,128)S(1)}, f32[20,8,256]{2,1,0:T(8,128)S(1)}, u32[]{:S(2)}, u32[]{:S(2)}) %collective-permute-start.4) | collective-permute-done | bytes 163872 | tf_op jit(solution)/shard_map/ppermute | solution.py:626
  154.8 5.6 %collective-permute-start.5 = (bf16[20,8,256]{2,1,0:T(8,128)(2,1)S(1)}, bf16[20,8,256]{2,1,0:T(8,128)(2,1)S(1)}, u32[]{:S(2)}, u32[]{:S(2)}) collective-permute-start(bf16[20,8,256]{2,1,0:T(8,128)(2,1)S(1)} %add_convert_fusion.1), channel_id=1, source_target_pairs={{0,1},{1,0},{2,3},{3,2},{4,5},{5,4},{6,7},{7,6},{8,9},{9,8},{10,11... | collective-permute-start | bytes 245768 | tf_op jit(solution)/shard_map/ppermute | solution.py:688
  160.4 11.8 %shard_map.152 = (f32[2048,256]{1,0:T(8,128)}, f32[2048,256]{1,0:T(8,128)}) custom-call(s32[1,2048]{1,0:T(1,128)} %src_ref.3, s32[2,1024]{1,0:T(2,128)} %bitcast.30, s32[2,1024]{1,0:T(2,128)} %bitcast.32, bf16[2048,256]{1,0:T(8,128)(2,1)} %get-tuple-element.58.d_src, bf16[2048,256]{1,0:T(8,128)(2,1)} %get-tuple-element.59.d_neg_src, ...), custom_call_target="tpu_custom_call" | custom-call | flops 6442450944 | bytes 7340032 | tf_op jit(solution)/shard_map/pallas_call | solution.py:691
  173.6 7.4 %shard_map.155 = (bf16[2048,256]{1,0:T(8,128)(2,1)}, bf16[2048,256]{1,0:T(8,128)(2,1)}) custom-call(s32[4,32]{1,0:T(4,128)} %partner_ref.5, s32[1]{0:T(128)} %bitcast.1.group_ref, s32[1]{0:T(128)} %bitcast.5.visit_ref.visit_to_ref, s32[32,2,128]{2,1,0:T(2,128)} %copy-done.7, bf16[32,128,256]{2,1,0:T(8,128)(2,1)} %copy-done, ...), custom_call_target="tpu_custom_call" | custom-call | bytes 25165824 | tf_op jit(solution)/shard_map/pallas_call | solution.py:704
  181.0 2.9 %collective-permute-start.7 = (bf16[2048,256]{1,0:T(8,128)(2,1)}, bf16[2048,256]{1,0:T(8,128)(2,1)}, u32[]{:S(2)}, u32[]{:S(2)}) collective-permute-start(bf16[2048,256]{1,0:T(8,128)(2,1)} %get-tuple-element.71), channel_id=1, source_target_pairs={{0,32},{32,0},{64,96},{96,64},{1,33},{33,1},{65,97},{97,65},{2,34}... | collective-permute-start | bytes 3145736 | tf_op jit(solution)/shard_map/ppermute | solution.py:626
  185.7 6.6 %all-to-all-start.4 = ((bf16[16,2,20,8,256]{4,3,2,1,0:T(8,128)(2,1)}), bf16[16,2,20,8,256]{4,3,2,1,0:T(8,128)(2,1)S(1)}, u32[]{:S(2)}, u32[]{:S(2)}) async-start(bf16[16,2,20,8,256]{4,3,2,1,0:T(8,128)(2,1)} %broadcast_in_dim.2), calls=%async_computation.4 | async-start | bytes 5242880 | tf_op jit(solution)/shard_map/all_to_all | solution.py:715
  194.2 24.6 %collective-permute-done.8.cross_ref = bf16[2048,256]{1,0:T(8,128)(2,1)} collective-permute-done((bf16[2048,256]{1,0:T(8,128)(2,1)S(1)}, bf16[2048,256]{1,0:T(8,128)(2,1)}, u32[]{:S(2)}, u32[]{:S(2)}) %collective-permute-start.8) | collective-permute-done | bytes 1048608 | tf_op jit(solution)/shard_map/ppermute | solution.py:626
  218.8 8.6 %all-to-all-done.4 = bf16[16,2,20,8,256]{4,3,2,1,0:T(8,128)(2,1)S(1)} async-done(((bf16[16,2,20,8,256]{4,3,2,1,0:T(8,128)(2,1)}), bf16[16,2,20,8,256]{4,3,2,1,0:T(8,128)(2,1)S(1)}, u32[]{:S(2)}, u32[]{:S(2)}) %all-to-all-start.4) | async-done | bytes 2621472 | tf_op jit(solution)/shard_map/all_to_all | solution.py:715
  229.3 8.2 %shard_map.154 = (bf16[2048,256]{1,0:T(8,128)(2,1)}, bf16[2048,256]{1,0:T(8,128)(2,1)}) custom-call(s32[4,32]{1,0:T(4,128)} %partner_ref.5, s32[1]{0:T(128)} %bitcast.1.group_ref, s32[1]{0:T(128)} %bitcast.5.visit_ref.visit_to_ref, s32[32,2,128]{2,1,0:T(2,128)} %copy-done.7, bf16[32,128,256]{2,1,0:T(8,128)(2,1)} %copy-done, ...), custom_call_target="tpu_custom_call" | custom-call | bytes 25165824 | tf_op jit(solution)/shard_map/pallas_call | solution.py:704
  238.4 5.9 %shard_map.157 = (f32[40,256,256]{2,1,0:T(8,128)}, f32[40,256]{1,0:T(8,128)}) custom-call(s32[1]{0:T(128)} %bitcast.16.part_ref, bf16[32,20,8,256]{3,2,1,0:T(8,128)(2,1)} %bitcast.23, f32[40,256,256]{2,1,0:T(8,128)} %relation_ref.7, f32[40,256]{1,0:T(8,128)} %acc_ref.5), custom_call_target="tpu_custom_call" | custom-call | bytes 25165824 | tf_op jit(solution)/shard_map/pallas_call | solution.py:555
  244.3 7.9 %shard_map.156 = (f32[1,2048,256]{2,1,0:T(8,128)}, f32[1,2048]{1,0:T(1,128)}) custom-call(f32[2048,256]{1,0:T(8,128)} %get-tuple-element.64.grad_ref, bf16[2048,256]{1,0:T(8,128)(2,1)} %get-tuple-element.67.home_ref, bf16[2048,256]{1,0:T(8,128)(2,1)} %collective-permute-done.6.sibling_ref, bf16[2048,256]{1,0:T(8,128)(2,1)} %collective-permute-done.8.cross_ref, ...), custom_call_target="tpu_custom_call" | custom-call | bytes 25165824 | tf_op jit(solution)/shard_map/pallas_call | solution.py:585
  252.2 5.9 %shard_map.158 = (f32[40,256,256]{2,1,0:T(8,128)}, f32[40,256]{1,0:T(8,128)}) custom-call(s32[1]{0:T(128)} %bitcast.15.part_ref, bf16[32,20,8,256]{3,2,1,0:T(8,128)(2,1)} %collective-permute-done.9.grad_ref, f32[40,256,256]{2,1,0:T(8,128)} %relation_ref.7, f32[40,256]{1,0:T(8,128)} %acc_ref.5, ...), custom_call_target="tpu_custom_call", output_to_operand_aliasing={{0}: (4, {})} | custom-call | bytes 25165824 | tf_op jit(solution)/shard_map/pallas_call | solution.py:555
  (46 shorter events, 28.3 us)
Async XLA Ops:
  2.3 35.3 %copy-start.3 = (bf16[2048,256]{1,0:T(8,128)(2,1)}, bf16[2048,256]{1,0:T(8,128)(2,1)S(1)}, u32[]{:S(2)}) copy-start(bf16[2048,256]{1,0:T(8,128)(2,1)S(1)} %convert_bitcast_fusion.refs_0_.own_table) | copy-start | bytes 3145732
  2.3 30.9 %collective-permute-start = (bf16[2048,256]{1,0:T(8,128)(2,1)S(1)}, bf16[2048,256]{1,0:T(8,128)(2,1)S(1)}, u32[]{:S(2)}, u32[]{:S(2)}) collective-permute-start(bf16[2048,256]{1,0:T(8,128)(2,1)S(1)} %convert_bitcast_fusion.refs_0_.own_table), channel_id=1, source_target_pairs={{0,64},{32,96},{64,0},{96,32},{1,65},{33,97},{65,1},{97,33},{2,66}... | collective-permute-start | bytes 3145736 | tf_op jit(solution)/shard_map/ppermute | solution.py:626
  7.6 25.7 %all-to-all-start = ((s32[32,2,128]{2,1,0:T(2,128)}), s32[32,2,128]{2,1,0:T(2,128)S(1)}, u32[]{:S(2)}, u32[]{:S(2)}) async-start(s32[32,2,128]{2,1,0:T(2,128)} %get-tuple-element.43), calls=%async_computation | async-start | bytes 65536 | tf_op jit(solution)/shard_map/all_to_all | solution.py:642
  17.8 17.4 %collective-permute-start.1 = (bf16[2048,256]{1,0:T(8,128)(2,1)S(1)}, bf16[2048,256]{1,0:T(8,128)(2,1)S(1)}, u32[]{:S(2)}, u32[]{:S(2)}) collective-permute-start(bf16[2048,256]{1,0:T(8,128)(2,1)S(1)} %convert_bitcast_fusion.refs_0_.own_table), channel_id=1, source_target_pairs={{0,32},{32,0},{64,96},{96,64},{1,33},{33,1},{65,97},{97,65},{2,34}... | collective-permute-start | bytes 3145736 | tf_op jit(solution)/shard_map/ppermute | solution.py:626
  33.2 4.4 %copy-start.7 = (s32[32,2,128]{2,1,0:T(2,128)}, s32[32,2,128]{2,1,0:T(2,128)S(1)}, u32[]{:S(2)}) copy-start(s32[32,2,128]{2,1,0:T(2,128)S(1)} %all-to-all-done.asked_ref) | copy-start | bytes 98308
  33.2 4.4 %copy-start.5 = (bf16[2048,256]{1,0:T(8,128)(2,1)}, bf16[2048,256]{1,0:T(8,128)(2,1)S(1)}, u32[]{:S(2)}) copy-start(bf16[2048,256]{1,0:T(8,128)(2,1)S(1)} %collective-permute-done.refs_2_.cross_table) | copy-start | bytes 3145732
  33.2 4.3 %collective-permute-start.2 = (bf16[2048,256]{1,0:T(8,128)(2,1)S(1)}, bf16[2048,256]{1,0:T(8,128)(2,1)}, u32[]{:S(2)}, u32[]{:S(2)}) collective-permute-start(bf16[2048,256]{1,0:T(8,128)(2,1)S(1)} %collective-permute-done.refs_2_.cross_table), channel_id=1, source_target_pairs={{0,32},{32,0},{64,96},{96,64},{1,33},{33,1},{65,97},{97,65},{2,34}... | collective-permute-start | bytes 3145736 | tf_op jit(solution)/shard_map/ppermute | solution.py:626
  35.2 2.4 copy-start.6
  48.0 35.2 %all-to-all-start.1 = ((bf16[32,128,256]{2,1,0:T(8,128)(2,1)}), bf16[32,128,256]{2,1,0:T(8,128)(2,1)S(1)}, u32[]{:S(2)}, u32[]{:S(2)}) async-start(bf16[32,128,256]{2,1,0:T(8,128)(2,1)} %shard_map.148), calls=%async_computation.1 | async-start | bytes 4194304 | tf_op jit(solution)/shard_map/all_to_all | solution.py:660
  83.2 1.3 copy-start.2
  104.5 16.3 %all-to-all-start.2 = ((bf16[32,16,256]{2,1,0:T(8,128)(2,1)}), bf16[32,16,256]{2,1,0:T(8,128)(2,1)S(1)}, u32[]{:S(2)}, u32[]{:S(2)}) async-start(bf16[32,16,256]{2,1,0:T(8,128)(2,1)} %get-tuple-element.52), calls=%async_computation.2 | async-start | bytes 524288 | tf_op jit(solution)/shard_map/all_to_all | solution.py:666
  120.8 0.7 copy-start.4
  120.8 8.2 %copy-start.8 = (s32[32,2,128]{2,1,0:T(2,128)S(1)}, s32[32,2,128]{2,1,0:T(2,128)}, u32[]{:S(2)}) copy-start(s32[32,2,128]{2,1,0:T(2,128)} %copy-done.7) | copy-start | bytes 98308
  121.5 50.6 %all-to-all-start.3 = ((bf16[32,128,256]{2,1,0:T(8,128)(2,1)}), bf16[32,128,256]{2,1,0:T(8,128)(2,1)S(1)}, u32[]{:S(2)}, u32[]{:S(2)}) async-start(bf16[32,128,256]{2,1,0:T(8,128)(2,1)} %shard_map.151), calls=%async_computation.3 | async-start | bytes 4194304 | tf_op jit(solution)/shard_map/all_to_all | solution.py:677
  132.7 2.5 collective-permute-start.3
  136.1 18.7 %collective-permute-start.4 = (f32[20,8,256]{2,1,0:T(8,128)S(1)}, f32[20,8,256]{2,1,0:T(8,128)S(1)}, u32[]{:S(2)}, u32[]{:S(2)}) collective-permute-start(f32[20,8,256]{2,1,0:T(8,128)S(1)} %bitcast_add_fusion), channel_id=1, source_target_pairs={{0,64},{32,96},{64,0},{96,32},{1,65},{33,97},{65,1},{97,33},{2,66}... | collective-permute-start | bytes 491528 | tf_op jit(solution)/shard_map/ppermute | solution.py:626
  154.8 17.3 %collective-permute-start.5 = (bf16[20,8,256]{2,1,0:T(8,128)(2,1)S(1)}, bf16[20,8,256]{2,1,0:T(8,128)(2,1)S(1)}, u32[]{:S(2)}, u32[]{:S(2)}) collective-permute-start(bf16[20,8,256]{2,1,0:T(8,128)(2,1)S(1)} %add_convert_fusion.1), channel_id=1, source_target_pairs={{0,1},{1,0},{2,3},{3,2},{4,5},{5,4},{6,7},{7,6},{8,9},{9,8},{10,11... | collective-permute-start | bytes 245768 | tf_op jit(solution)/shard_map/ppermute | solution.py:688
  172.2 1.4 copy-start
  181.0 11.3 %collective-permute-start.7 = (bf16[2048,256]{1,0:T(8,128)(2,1)}, bf16[2048,256]{1,0:T(8,128)(2,1)}, u32[]{:S(2)}, u32[]{:S(2)}) collective-permute-start(bf16[2048,256]{1,0:T(8,128)(2,1)} %get-tuple-element.71), channel_id=1, source_target_pairs={{0,32},{32,0},{64,96},{96,64},{1,33},{33,1},{65,97},{97,65},{2,34}... | collective-permute-start | bytes 3145736 | tf_op jit(solution)/shard_map/ppermute | solution.py:626
  185.7 41.7 %all-to-all-start.4 = ((bf16[16,2,20,8,256]{4,3,2,1,0:T(8,128)(2,1)}), bf16[16,2,20,8,256]{4,3,2,1,0:T(8,128)(2,1)S(1)}, u32[]{:S(2)}, u32[]{:S(2)}) async-start(bf16[16,2,20,8,256]{4,3,2,1,0:T(8,128)(2,1)} %broadcast_in_dim.2), calls=%async_computation.4 | async-start | bytes 5242880 | tf_op jit(solution)/shard_map/all_to_all | solution.py:715
  194.1 24.7 %collective-permute-start.8 = (bf16[2048,256]{1,0:T(8,128)(2,1)S(1)}, bf16[2048,256]{1,0:T(8,128)(2,1)}, u32[]{:S(2)}, u32[]{:S(2)}) collective-permute-start(bf16[2048,256]{1,0:T(8,128)(2,1)S(1)} %add_convert_fusion), channel_id=1, source_target_pairs={{0,64},{32,96},{64,0},{96,32},{1,65},{33,97},{65,1},{97,33},{2,66}... | collective-permute-start | bytes 3145736 | tf_op jit(solution)/shard_map/ppermute | solution.py:626
  227.4 10.0 %copy-start.1 = (bf16[16,2,20,8,256]{4,3,2,1,0:T(8,128)(2,1)}, bf16[16,2,20,8,256]{4,3,2,1,0:T(8,128)(2,1)S(1)}, u32[]{:S(2)}) copy-start(bf16[16,2,20,8,256]{4,3,2,1,0:T(8,128)(2,1)S(1)} %all-to-all-done.4) | copy-start | bytes 7864324
  227.4 24.8 %collective-permute-start.9 = (bf16[32,20,8,256]{3,2,1,0:T(8,128)(2,1)S(1)}, bf16[32,20,8,256]{3,2,1,0:T(8,128)(2,1)}, u32[]{:S(2)}, u32[]{:S(2)}) collective-permute-start(bf16[32,20,8,256]{3,2,1,0:T(8,128)(2,1)S(1)} %bitcast.22), channel_id=1, source_target_pairs={{0,32},{32,0},{64,96},{96,64},{1,33},{33,1},{65,97},{97,65},{2,34}... | collective-permute-start | bytes 7864328 | tf_op jit(solution)/shard_map/ppermute | solution.py:626
  237.4 6.8 %collective-permute-start.6 = (bf16[2048,256]{1,0:T(8,128)(2,1)}, bf16[2048,256]{1,0:T(8,128)(2,1)}, u32[]{:S(2)}, u32[]{:S(2)}) collective-permute-start(bf16[2048,256]{1,0:T(8,128)(2,1)} %get-tuple-element.68), channel_id=1, source_target_pairs={{0,32},{32,0},{64,96},{96,64},{1,33},{33,1},{65,97},{97,65},{2,34}... | collective-permute-start | bytes 3145736 | tf_op jit(solution)/shard_map/ppermute | solution.py:626

commit v8 on v7

--- a/solution.py
+++ b/solution.py
@@ -676,18 +676,6 @@
     )
     returned = lax.all_to_all(outgoing, "dev", split_axis=0, concat_axis=0, tiled=True)
 
-    rel_part = call(operators_body, sds((relations, extra, width), full), (), [SMEM, VMEM])(
-        asked[:, 1, :blocks], d_op_here
-    )
-    core = me & 1
-    halves = rel_part.reshape(2, relations // 2, extra, width)
-    mine = lax.dynamic_index_in_dim(halves, core, 0, keepdims=False)
-    other = lax.dynamic_index_in_dim(halves, 1 - core, 0, keepdims=False)
-    chip = mine + neighbour(other, 1)
-    pair = (chip + neighbour(chip, 2)).astype(half)
-    near = lax.ppermute(pair, "dev", [(d, d ^ 1) for d in range(peers)])
-    low = (place_id & 1) == 0
-    planes = jnp.stack([jnp.where(low, pair, near), jnp.where(low, near, pair)])
     own_grad, visit_grad = call(
         sums_body,
         (sds((rows, width), full), sds((rows, width), full)),
@@ -696,9 +684,22 @@
         cost(2 * 3 * edges * rows * width, 7 * rows * width * 2),
     )(src_row, neg_src, neg_dst, d_src, d_neg_src, d_neg_dst)
 
-    returned, own_grad, visit_grad, planes = lax.optimization_barrier(
-        (returned, own_grad, visit_grad, planes)
-    )
+    rel_part = call(operators_body, sds((relations, extra, width), full), (), [SMEM, VMEM])(
+        asked[:, 1, :blocks], d_op_here
+    )
+    core = me & 1
+    halves = rel_part.reshape(2, relations // 2, extra, width)
+    mine = lax.dynamic_index_in_dim(halves, core, 0, keepdims=False)
+    other = lax.dynamic_index_in_dim(halves, 1 - core, 0, keepdims=False)
+    chip = mine + neighbour(other, 1)
+    chip_other, own_grad, visit_grad = lax.optimization_barrier(
+        (neighbour(chip, 2), own_grad, visit_grad)
+    )
+    pair = (chip + chip_other).astype(half)
+    near = lax.ppermute(pair, "dev", [(d, d ^ 1) for d in range(peers)])
+    low = (place_id & 1) == 0
+    planes = jnp.stack([jnp.where(low, pair, near), jnp.where(low, near, pair)])
+    returned, planes = lax.optimization_barrier((returned, planes))
 
     def home(parts, returned):
         return call(
@@ -709,8 +710,9 @@
             cost(0, 24 * MEBI),
         )(partner, group, visit_to, asked, returned, visit_grad)
 
-    home_cross_sibling, home_cross = home((3, 2), returned)
+    home_cross_sibling, home_cross, home_sibling = home((3, 2, 1), returned)
     chip_cross = (home_cross.astype(full) + neighbour(home_cross_sibling, 1).astype(full)).astype(half)
+    from_sibling = neighbour(home_sibling, 1)
     from_cross = neighbour(chip_cross, 2)
     gathered = lax.all_to_all(
         jnp.broadcast_to(planes[None], (peers // 2,) + planes.shape),
@@ -721,12 +723,11 @@
         tiled=True,
     ).reshape((peers,) + pair.shape)
 
-    home_sibling, home_own = home((1, 0), returned)
-    from_sibling = neighbour(home_sibling, 1)
-    gathered, from_cross = lax.optimization_barrier((gathered, from_cross))
+    (home_own,) = home((0,), returned)
     entity_new, acc_new = entity_update(
         own_grad, home_own, from_sibling, from_cross, entity, entity_acc
     )
+    gathered, entity_new, acc_new = lax.optimization_barrier((gathered, entity_new, acc_new))
     other_half = neighbour(gathered, 1)
     before = relation_update(core.reshape(1), gathered, relation, relation_acc)
     relation_new, relation_acc_new = relation_update(

time: 259 us -> 236 us (0.911)
  waiting for transfers between devices: 77.3 us -> 52.6 us
    ppermute x9, waiting for transfers between devices: 45.8 us -> 27.8 us  [neighbour(): return lax.ppermute(x, 'grp', [(g, g ^ flip) for g in range(4)])]
    all_to_all x1, waiting for transfers between devices: 8.6 us -> 0.01 us  [on_device(): lax.all_to_all(jnp.broadcast_to(planes[None], (peers // 2,) + planes.shap...]
  transfers between devices with their start and end apart: 15 -> 15, of which waited for: 8 -> 8; matrix products, arithmetic and copies ran while one was open for 3% -> 4% of each run, Pallas kernels for 26% -> 27%
where the time goes in v8:
time: 236 us; the launch traced here: 235 us
  Pallas kernels  111 us (47%)
  starting transfers between devices  55.4 us (23%)
  waiting for transfers between devices  52.6 us (22%)
  local copies, waits for them, and re-layouts  8.37 us (4%)
  other arithmetic  5.57 us (2%)
    ppermute x9, waiting for transfers between devices, neighbour(): return lax.ppermute(x, 'grp', [(g, g ^ flip) for g in range(4)])  27.8 us
    pallas_call x1, Pallas kernels, front(): call(front_body, (sds((edges, width), half), sds((blocks * negs, width),...  20.2 us
    pallas_call x1, Pallas kernels, model(): call(model_body, (sds((peers, blocks * (width // peers), width), half), s...  20 us
    pallas_call x2, Pallas kernels, home(): call(functools.partial(home_body, parts), tuple((sds((rows, width), half)...  16.3 us
    all_to_all x1, waiting for transfers between devices, on_device(): lax.all_to_all(wanted, 'dev', split_axis=0, concat_axis=0, tiled=True)  14.1 us
    ppermute x9, starting transfers between devices, neighbour(): return lax.ppermute(x, 'grp', [(g, g ^ flip) for g in range(4)])  13.2 us
    pallas_call x2, Pallas kernels, relation_update(): pl.pallas_call(relation_body, grid_spec=pltpu.PrefetchScalarGridSpec(num_...  11.8 us
    pallas_call x1, Pallas kernels, on_device(): call(sums_body, (sds((rows, width), full), sds((rows, width), full)), (),...  11.8 us
  transfers between devices with their start and end apart: 15, of which 8 were waited for; matrix products, arithmetic and copies ran while one was open for 4% of the time, Pallas kernels for 27%

profile of v8, /device:TPU:1, one launch (start us, length us, event | category | flops | bytes accessed | tf_op | source)
XLA Modules:
  0.0 235.0 jit_solution(1442735643389982708)
XLA Ops:
  4.5 3.0 %shard_map.147 = (s32[1,2048]{1,0:T(1,128)}, s32[32,2,128]{2,1,0:T(2,128)}) custom-call(s32[1,2]{1,0:T(1,128)} %rel_ref.5, s32[1,2048]{1,0:T(1,128)} %bitcast.28, s32[1,2048]{1,0:T(1,128)} %row_ref.1), custom_call_target="tpu_custom_call" | custom-call | tf_op jit(solution)/shard_map/pallas_call | solution.py:637
  7.6 10.2 %all-to-all-start = ((s32[32,2,128]{2,1,0:T(2,128)}), s32[32,2,128]{2,1,0:T(2,128)S(1)}, u32[]{:S(2)}, u32[]{:S(2)}) async-start(s32[32,2,128]{2,1,0:T(2,128)} %get-tuple-element.44), calls=%async_computation | async-start | bytes 65536 | tf_op jit(solution)/shard_map/all_to_all | solution.py:642
  19.1 14.1 %all-to-all-done.asked_ref = s32[32,2,128]{2,1,0:T(2,128)S(1)} async-done(((s32[32,2,128]{2,1,0:T(2,128)}), s32[32,2,128]{2,1,0:T(2,128)S(1)}, u32[]{:S(2)}, u32[]{:S(2)}) %all-to-all-start) | async-done | bytes 32800 | tf_op jit(solution)/shard_map/all_to_all | solution.py:642
  35.2 2.4 %collective-permute-done.2.refs_3_.cross_sibling_table = bf16[2048,256]{1,0:T(8,128)(2,1)} collective-permute-done((bf16[2048,256]{1,0:T(8,128)(2,1)S(1)}, bf16[2048,256]{1,0:T(8,128)(2,1)}, u32[]{:S(2)}, u32[]{:S(2)}) %collective-permute-start.2) | collective-permute-done | bytes 1048608 | tf_op jit(solution)/shard_map/ppermute | solution.py:626
  37.6 10.4 %shard_map.148 = bf16[32,128,256]{2,1,0:T(8,128)(2,1)} custom-call(s32[4,32]{1,0:T(4,128)} %partner_ref.5, s32[1]{0:T(128)} %bitcast.1.group_ref, s32[32,2,128]{2,1,0:T(2,128)} %copy-done.7, bf16[2048,256]{1,0:T(8,128)(2,1)} %copy-done.3, bf16[2048,256]{1,0:T(8,128)(2,1)} %copy-done.6, bf16[2048,256]{1,0:T(8,128)(2,1)} %copy-done.5, ...), custom_call_target="tpu_custom_call" | custom-call | tf_op jit(solution)/shard_map/pallas_call | solution.py:648
  48.0 5.6 %all-to-all-start.1 = ((bf16[32,128,256]{2,1,0:T(8,128)(2,1)}), bf16[32,128,256]{2,1,0:T(8,128)(2,1)S(1)}, u32[]{:S(2)}, u32[]{:S(2)}) async-start(bf16[32,128,256]{2,1,0:T(8,128)(2,1)} %shard_map.148), calls=%async_computation.1 | async-start | bytes 4194304 | tf_op jit(solution)/shard_map/all_to_all | solution.py:660
  56.2 20.2 %shard_map.149 = (bf16[2048,256]{1,0:T(8,128)(2,1)}, bf16[2048,256]{1,0:T(8,128)(2,1)}, bf16[2048,256]{1,0:T(8,128)(2,1)}, bf16[2048,1024]{1,0:T(8,128)(2,1)}, f32[2048,256]{1,0:T(8,128)}, /*index=5*/f32[2048,128]{1,0:T(8,128)}) custom-call(s32[1,2]{1,0:T(1,128)} %rel_ref.5, s32[1]{0:T(128)} %bitcast.5.visit_ref.visit_to_ref, s32[1,2048]{1,0:T(1,128)} %src_ref.3, ...), custom_call_target="tpu_custom_call" | custom-call | flops 8589934592 | bytes 12582912 | tf_op jit(solution)/shard_map/pallas_call | solution.py:372
  76.4 6.8 %all-to-all-done.1 = bf16[32,128,256]{2,1,0:T(8,128)(2,1)S(1)} async-done(((bf16[32,128,256]{2,1,0:T(8,128)(2,1)}), bf16[32,128,256]{2,1,0:T(8,128)(2,1)S(1)}, u32[]{:S(2)}, u32[]{:S(2)}) %all-to-all-start.1) | async-done | bytes 2097184 | tf_op jit(solution)/shard_map/all_to_all | solution.py:660
  84.5 20.0 %shard_map.150 = (bf16[32,16,256]{2,1,0:T(8,128)(2,1)}, bf16[2048,256]{1,0:T(8,128)(2,1)}, bf16[2048,256]{1,0:T(8,128)(2,1)}, bf16[2048,256]{1,0:T(8,128)(2,1)}, bf16[2048,256]{1,0:T(8,128)(2,1)}) custom-call(s32[1,2]{1,0:T(1,128)} %rel_ref.5, s32[1,1]{1,0:T(1,128)S(6)} %copy.21.count_ref, s32[1,2048]{1,0:T(1,128)} %get-tuple-element.43.slot_ref, ...), custom_call_target="tpu_custom_call" | custom-call | tf_op jit(solution)/shard_map/pallas_call | solution.py:402
  104.5 6.7 %all-to-all-start.2 = ((bf16[32,16,256]{2,1,0:T(8,128)(2,1)}), bf16[32,16,256]{2,1,0:T(8,128)(2,1)S(1)}, u32[]{:S(2)}, u32[]{:S(2)}) async-start(bf16[32,16,256]{2,1,0:T(8,128)(2,1)} %get-tuple-element.53), calls=%async_computation.2 | async-start | bytes 524288 | tf_op jit(solution)/shard_map/all_to_all | solution.py:666
  111.2 7.6 %shard_map.151 = bf16[32,128,256]{2,1,0:T(8,128)(2,1)} custom-call(s32[1,2048]{1,0:T(1,128)} %get-tuple-element.43.slot_ref, bf16[2048,256]{1,0:T(8,128)(2,1)} %get-tuple-element.54.d_dst), custom_call_target="tpu_custom_call" | custom-call | flops 4294967296 | bytes 4194304 | tf_op jit(solution)/shard_map/pallas_call | solution.py:667
  121.5 7.5 %all-to-all-start.3 = ((bf16[32,128,256]{2,1,0:T(8,128)(2,1)}), bf16[32,128,256]{2,1,0:T(8,128)(2,1)S(1)}, u32[]{:S(2)}, u32[]{:S(2)}) async-start(bf16[32,128,256]{2,1,0:T(8,128)(2,1)} %shard_map.151), calls=%async_computation.3 | async-start | bytes 4194304 | tf_op jit(solution)/shard_map/all_to_all | solution.py:677
  137.0 11.8 %shard_map.153 = (f32[2048,256]{1,0:T(8,128)}, f32[2048,256]{1,0:T(8,128)}) custom-call(s32[1,2048]{1,0:T(1,128)} %src_ref.3, s32[2,1024]{1,0:T(2,128)} %bitcast.30, s32[2,1024]{1,0:T(2,128)} %bitcast.32, bf16[2048,256]{1,0:T(8,128)(2,1)} %get-tuple-element.60.d_src, bf16[2048,256]{1,0:T(8,128)(2,1)} %get-tuple-element.61.d_neg_src, ...), custom_call_target="tpu_custom_call" | custom-call | flops 6442450944 | bytes 7340032 | tf_op jit(solution)/shard_map/pallas_call | solution.py:679
  148.8 6.0 %collective-permute-done.4 = f32[20,8,256]{2,1,0:T(8,128)S(1)} collective-permute-done((f32[20,8,256]{2,1,0:T(8,128)S(1)}, f32[20,8,256]{2,1,0:T(8,128)S(1)}, u32[]{:S(2)}, u32[]{:S(2)}) %collective-permute-start.4) | collective-permute-done | bytes 163872 | tf_op jit(solution)/shard_map/ppermute | solution.py:626
  154.8 5.6 %collective-permute-start.5 = (bf16[20,8,256]{2,1,0:T(8,128)(2,1)S(1)}, bf16[20,8,256]{2,1,0:T(8,128)(2,1)S(1)}, u32[]{:S(2)}, u32[]{:S(2)}) collective-permute-start(bf16[20,8,256]{2,1,0:T(8,128)(2,1)S(1)} %add_convert_fusion.1), channel_id=1, source_target_pairs={{0,1},{1,0},{2,3},{3,2},{4,5},{5,4},{6,7},{7,6},{8,9},{9,8},{10,11... | collective-permute-start | bytes 245768 | tf_op jit(solution)/shard_map/ppermute | solution.py:699
  163.6 10.2 %shard_map.155 = (bf16[2048,256]{1,0:T(8,128)(2,1)}, bf16[2048,256]{1,0:T(8,128)(2,1)}, bf16[2048,256]{1,0:T(8,128)(2,1)}) custom-call(s32[4,32]{1,0:T(4,128)} %partner_ref.5, s32[1]{0:T(128)} %bitcast.1.group_ref, s32[1]{0:T(128)} %bitcast.5.visit_ref.visit_to_ref, s32[32,2,128]{2,1,0:T(2,128)} %copy-done.7, bf16[32,128,256]{2,1,0:T(8,128)(2,1)} %copy-done, ...), custom_call_target="tpu_custom_call" | custom-call | bytes 25165824 | tf_op jit(solution)/shard_map/pallas_call | solution.py:705
  173.8 3.6 %collective-permute-start.7 = (bf16[2048,256]{1,0:T(8,128)(2,1)}, bf16[2048,256]{1,0:T(8,128)(2,1)}, u32[]{:S(2)}, u32[]{:S(2)}) collective-permute-start(bf16[2048,256]{1,0:T(8,128)(2,1)} %get-tuple-element.72), channel_id=1, source_target_pairs={{0,32},{32,0},{64,96},{96,64},{1,33},{33,1},{65,97},{97,65},{2,34}... | collective-permute-start | bytes 3145736 | tf_op jit(solution)/shard_map/ppermute | solution.py:626
  179.1 6.6 %all-to-all-start.4 = ((bf16[16,2,20,8,256]{4,3,2,1,0:T(8,128)(2,1)}), bf16[16,2,20,8,256]{4,3,2,1,0:T(8,128)(2,1)S(1)}, u32[]{:S(2)}, u32[]{:S(2)}) async-start(bf16[16,2,20,8,256]{4,3,2,1,0:T(8,128)(2,1)} %broadcast_in_dim.2), calls=%async_computation.4 | async-start | bytes 5242880 | tf_op jit(solution)/shard_map/all_to_all | solution.py:717
  186.1 2.9 %add_convert_fusion = bf16[2048,256]{1,0:T(8,128)(2,1)} fusion(bf16[2048,256]{1,0:T(8,128)(2,1)} %collective-permute-done.7, bf16[2048,256]{1,0:T(8,128)(2,1)} %get-tuple-element.71), kind=kLoop, calls=%fused_computation | loop fusion | flops 2097152 | bytes 3145728 | tf_op jit(solution)/shard_map/convert_element_type | solution.py:714
  189.3 6.1 %shard_map.154.home_ref = bf16[2048,256]{1,0:T(8,128)(2,1)} custom-call(s32[4,32]{1,0:T(4,128)} %partner_ref.5, s32[1]{0:T(128)} %bitcast.1.group_ref, s32[1]{0:T(128)} %bitcast.5.visit_ref.visit_to_ref, s32[32,2,128]{2,1,0:T(2,128)} %copy-done.7, bf16[32,128,256]{2,1,0:T(8,128)(2,1)} %copy-done, f32[2048,256]{1,0:T(8,128)} %get-tuple-element.69.visit_ref), custom_call_target="tpu_custom_call" | custom-call | bytes 25165824 | tf_op jit(solution)/shard_map/pallas_call | solution.py:705
  195.4 18.4 %collective-permute-done.8.cross_ref = bf16[2048,256]{1,0:T(8,128)(2,1)} collective-permute-done((bf16[2048,256]{1,0:T(8,128)(2,1)}, bf16[2048,256]{1,0:T(8,128)(2,1)}, u32[]{:S(2)}, u32[]{:S(2)}) %collective-permute-start.8) | collective-permute-done | bytes 1048608 | tf_op jit(solution)/shard_map/ppermute | solution.py:626
  213.8 7.9 %shard_map.156 = (f32[1,2048,256]{2,1,0:T(8,128)}, f32[1,2048]{1,0:T(1,128)}) custom-call(f32[2048,256]{1,0:T(8,128)} %get-tuple-element.67.grad_ref, bf16[2048,256]{1,0:T(8,128)(2,1)} %shard_map.154.home_ref, bf16[2048,256]{1,0:T(8,128)(2,1)} %collective-permute-done.6.sibling_ref, bf16[2048,256]{1,0:T(8,128)(2,1)} %collective-permute-done.8.cross_ref, ...), custom_call_target="tpu_custom_call" | custom-call | bytes 25165824 | tf_op jit(solution)/shard_map/pallas_call | solution.py:585
  223.2 5.9 %shard_map.157 = (f32[40,256,256]{2,1,0:T(8,128)}, f32[40,256]{1,0:T(8,128)}) custom-call(s32[1]{0:T(128)} %bitcast.16.part_ref, bf16[32,20,8,256]{3,2,1,0:T(8,128)(2,1)} %bitcast.23, f32[40,256,256]{2,1,0:T(8,128)} %relation_ref.7, f32[40,256]{1,0:T(8,128)} %acc_ref.5), custom_call_target="tpu_custom_call" | custom-call | bytes 25165824 | tf_op jit(solution)/shard_map/pallas_call | solution.py:555
  229.1 5.9 %shard_map.158 = (f32[40,256,256]{2,1,0:T(8,128)}, f32[40,256]{1,0:T(8,128)}) custom-call(s32[1]{0:T(128)} %bitcast.15.part_ref, bf16[32,20,8,256]{3,2,1,0:T(8,128)(2,1)} %collective-permute-done.9.grad_ref, f32[40,256,256]{2,1,0:T(8,128)} %relation_ref.7, f32[40,256]{1,0:T(8,128)} %acc_ref.5, ...), custom_call_target="tpu_custom_call", output_to_operand_aliasing={{0}: (4, {})} | custom-call | bytes 25165824 | tf_op jit(solution)/shard_map/pallas_call | solution.py:555
  (46 shorter events, 27.6 us)
Async XLA Ops:
  2.3 35.3 %copy-start.3 = (bf16[2048,256]{1,0:T(8,128)(2,1)}, bf16[2048,256]{1,0:T(8,128)(2,1)S(1)}, u32[]{:S(2)}) copy-start(bf16[2048,256]{1,0:T(8,128)(2,1)S(1)} %convert_bitcast_fusion.refs_0_.own_table) | copy-start | bytes 3145732
  2.3 30.9 %collective-permute-start = (bf16[2048,256]{1,0:T(8,128)(2,1)S(1)}, bf16[2048,256]{1,0:T(8,128)(2,1)S(1)}, u32[]{:S(2)}, u32[]{:S(2)}) collective-permute-start(bf16[2048,256]{1,0:T(8,128)(2,1)S(1)} %convert_bitcast_fusion.refs_0_.own_table), channel_id=1, source_target_pairs={{0,64},{32,96},{64,0},{96,32},{1,65},{33,97},{65,1},{97,33},{2,66}... | collective-permute-start | bytes 3145736 | tf_op jit(solution)/shard_map/ppermute | solution.py:626
  7.6 25.7 %all-to-all-start = ((s32[32,2,128]{2,1,0:T(2,128)}), s32[32,2,128]{2,1,0:T(2,128)S(1)}, u32[]{:S(2)}, u32[]{:S(2)}) async-start(s32[32,2,128]{2,1,0:T(2,128)} %get-tuple-element.44), calls=%async_computation | async-start | bytes 65536 | tf_op jit(solution)/shard_map/all_to_all | solution.py:642
  17.8 17.4 %collective-permute-start.1 = (bf16[2048,256]{1,0:T(8,128)(2,1)S(1)}, bf16[2048,256]{1,0:T(8,128)(2,1)S(1)}, u32[]{:S(2)}, u32[]{:S(2)}) collective-permute-start(bf16[2048,256]{1,0:T(8,128)(2,1)S(1)} %convert_bitcast_fusion.refs_0_.own_table), channel_id=1, source_target_pairs={{0,32},{32,0},{64,96},{96,64},{1,33},{33,1},{65,97},{97,65},{2,34}... | collective-permute-start | bytes 3145736 | tf_op jit(solution)/shard_map/ppermute | solution.py:626
  33.2 4.4 %copy-start.7 = (s32[32,2,128]{2,1,0:T(2,128)}, s32[32,2,128]{2,1,0:T(2,128)S(1)}, u32[]{:S(2)}) copy-start(s32[32,2,128]{2,1,0:T(2,128)S(1)} %all-to-all-done.asked_ref) | copy-start | bytes 98308
  33.2 4.4 %copy-start.5 = (bf16[2048,256]{1,0:T(8,128)(2,1)}, bf16[2048,256]{1,0:T(8,128)(2,1)S(1)}, u32[]{:S(2)}) copy-start(bf16[2048,256]{1,0:T(8,128)(2,1)S(1)} %collective-permute-done.refs_2_.cross_table) | copy-start | bytes 3145732
  33.2 4.3 %collective-permute-start.2 = (bf16[2048,256]{1,0:T(8,128)(2,1)S(1)}, bf16[2048,256]{1,0:T(8,128)(2,1)}, u32[]{:S(2)}, u32[]{:S(2)}) collective-permute-start(bf16[2048,256]{1,0:T(8,128)(2,1)S(1)} %collective-permute-done.refs_2_.cross_table), channel_id=1, source_target_pairs={{0,32},{32,0},{64,96},{96,64},{1,33},{33,1},{65,97},{97,65},{2,34}... | collective-permute-start | bytes 3145736 | tf_op jit(solution)/shard_map/ppermute | solution.py:626
  35.2 2.4 %copy-start.6 = (bf16[2048,256]{1,0:T(8,128)(2,1)}, bf16[2048,256]{1,0:T(8,128)(2,1)S(1)}, u32[]{:S(2)}) copy-start(bf16[2048,256]{1,0:T(8,128)(2,1)S(1)} %collective-permute-done.1.refs_1_.sibling_table) | copy-start | bytes 3145732
  48.0 35.2 %all-to-all-start.1 = ((bf16[32,128,256]{2,1,0:T(8,128)(2,1)}), bf16[32,128,256]{2,1,0:T(8,128)(2,1)S(1)}, u32[]{:S(2)}, u32[]{:S(2)}) async-start(bf16[32,128,256]{2,1,0:T(8,128)(2,1)} %shard_map.148), calls=%async_computation.1 | async-start | bytes 4194304 | tf_op jit(solution)/shard_map/all_to_all | solution.py:660
  83.2 1.3 copy-start.2
  104.5 16.3 %all-to-all-start.2 = ((bf16[32,16,256]{2,1,0:T(8,128)(2,1)}), bf16[32,16,256]{2,1,0:T(8,128)(2,1)S(1)}, u32[]{:S(2)}, u32[]{:S(2)}) async-start(bf16[32,16,256]{2,1,0:T(8,128)(2,1)} %get-tuple-element.53), calls=%async_computation.2 | async-start | bytes 524288 | tf_op jit(solution)/shard_map/all_to_all | solution.py:666
  120.8 0.7 copy-start.4
  120.8 8.2 %copy-start.8 = (s32[32,2,128]{2,1,0:T(2,128)S(1)}, s32[32,2,128]{2,1,0:T(2,128)}, u32[]{:S(2)}) copy-start(s32[32,2,128]{2,1,0:T(2,128)} %copy-done.7) | copy-start | bytes 98308
  121.5 40.7 %all-to-all-start.3 = ((bf16[32,128,256]{2,1,0:T(8,128)(2,1)}), bf16[32,128,256]{2,1,0:T(8,128)(2,1)S(1)}, u32[]{:S(2)}, u32[]{:S(2)}) async-start(bf16[32,128,256]{2,1,0:T(8,128)(2,1)} %shard_map.151), calls=%async_computation.3 | async-start | bytes 4194304 | tf_op jit(solution)/shard_map/all_to_all | solution.py:677
  132.6 2.5 %collective-permute-start.3 = (f32[20,8,256]{2,1,0:T(8,128)S(1)}, f32[20,8,256]{2,1,0:T(8,128)S(1)}, u32[]{:S(2)}, u32[]{:S(2)}) collective-permute-start(f32[20,8,256]{2,1,0:T(8,128)S(1)} %dynamic-slice_bitcast_fusion), channel_id=1, source_target_pairs={{0,32},{32,0},{64,96},{96,64},{1,33},{33,1},{65,97},{97,65},{2,34}... | collective-permute-start | bytes 491528 | tf_op jit(solution)/shard_map/ppermute | solution.py:626
  136.0 18.7 %collective-permute-start.4 = (f32[20,8,256]{2,1,0:T(8,128)S(1)}, f32[20,8,256]{2,1,0:T(8,128)S(1)}, u32[]{:S(2)}, u32[]{:S(2)}) collective-permute-start(f32[20,8,256]{2,1,0:T(8,128)S(1)} %bitcast_add_fusion), channel_id=1, source_target_pairs={{0,64},{32,96},{64,0},{96,32},{1,65},{33,97},{65,1},{97,33},{2,66}... | collective-permute-start | bytes 491528 | tf_op jit(solution)/shard_map/ppermute | solution.py:626
  154.8 7.4 %collective-permute-start.5 = (bf16[20,8,256]{2,1,0:T(8,128)(2,1)S(1)}, bf16[20,8,256]{2,1,0:T(8,128)(2,1)S(1)}, u32[]{:S(2)}, u32[]{:S(2)}) collective-permute-start(bf16[20,8,256]{2,1,0:T(8,128)(2,1)S(1)} %add_convert_fusion.1), channel_id=1, source_target_pairs={{0,1},{1,0},{2,3},{3,2},{4,5},{5,4},{6,7},{7,6},{8,9},{9,8},{10,11... | collective-permute-start | bytes 245768 | tf_op jit(solution)/shard_map/ppermute | solution.py:699
  162.2 1.3 copy-start
  173.8 12.3 %collective-permute-start.7 = (bf16[2048,256]{1,0:T(8,128)(2,1)}, bf16[2048,256]{1,0:T(8,128)(2,1)}, u32[]{:S(2)}, u32[]{:S(2)}) collective-permute-start(bf16[2048,256]{1,0:T(8,128)(2,1)} %get-tuple-element.72), channel_id=1, source_target_pairs={{0,32},{32,0},{64,96},{96,64},{1,33},{33,1},{65,97},{97,65},{2,34}... | collective-permute-start | bytes 3145736 | tf_op jit(solution)/shard_map/ppermute | solution.py:626
  179.1 42.6 %all-to-all-start.4 = ((bf16[16,2,20,8,256]{4,3,2,1,0:T(8,128)(2,1)}), bf16[16,2,20,8,256]{4,3,2,1,0:T(8,128)(2,1)S(1)}, u32[]{:S(2)}, u32[]{:S(2)}) async-start(bf16[16,2,20,8,256]{4,3,2,1,0:T(8,128)(2,1)} %broadcast_in_dim.2), calls=%async_computation.4 | async-start | bytes 5242880 | tf_op jit(solution)/shard_map/all_to_all | solution.py:717
  185.7 9.7 %collective-permute-start.6 = (bf16[2048,256]{1,0:T(8,128)(2,1)}, bf16[2048,256]{1,0:T(8,128)(2,1)}, u32[]{:S(2)}, u32[]{:S(2)}) collective-permute-start(bf16[2048,256]{1,0:T(8,128)(2,1)} %get-tuple-element.70), channel_id=1, source_target_pairs={{0,32},{32,0},{64,96},{96,64},{1,33},{33,1},{65,97},{97,65},{2,34}... | collective-permute-start | bytes 3145736 | tf_op jit(solution)/shard_map/ppermute | solution.py:626
  188.9 24.8 %collective-permute-start.8 = (bf16[2048,256]{1,0:T(8,128)(2,1)}, bf16[2048,256]{1,0:T(8,128)(2,1)}, u32[]{:S(2)}, u32[]{:S(2)}) collective-permute-start(bf16[2048,256]{1,0:T(8,128)(2,1)} %add_convert_fusion), channel_id=1, source_target_pairs={{0,64},{32,96},{64,0},{96,32},{1,65},{33,97},{65,1},{97,33},{2,66}... | collective-permute-start | bytes 3145736 | tf_op jit(solution)/shard_map/ppermute | solution.py:626
  221.7 1.5 copy-start.1
  221.7 7.4 %collective-permute-start.9 = (bf16[32,20,8,256]{3,2,1,0:T(8,128)(2,1)S(1)}, bf16[32,20,8,256]{3,2,1,0:T(8,128)(2,1)}, u32[]{:S(2)}, u32[]{:S(2)}) collective-permute-start(bf16[32,20,8,256]{3,2,1,0:T(8,128)(2,1)S(1)} %bitcast.22), channel_id=1, source_target_pairs={{0,32},{32,0},{64,96},{96,64},{1,33},{33,1},{65,97},{97,65},{2,34}... | collective-permute-start | bytes 7864328 | tf_op jit(solution)/shard_map/ppermute | solution.py:626

commit v9 on v8

--- a/solution.py
+++ b/solution.py
@@ -578,7 +578,7 @@
 
 def entity_update(grad, home, sibling, cross, entity, entity_acc):
     rows, width = grad.shape
-    step = 256
+    step = 1024 if rows % 1024 == 0 else 256
     part = pl.BlockSpec((step, width), lambda i: (i, 0))
     block = pl.BlockSpec((1, step, width), lambda i: (0, i, 0))
     line = pl.BlockSpec((1, step), lambda i: (0, i))

time: 236 us -> 235 us (level)
  Pallas kernels: 111 us -> 108 us
    pallas_call x1, Pallas kernels: 7.88 us -> 4.9 us  [entity_update(): pl.pallas_call(entity_body, grid=(rows // step,), in_specs=[part] * 4 + [...]
  transfers between devices with their start and end apart: 15 -> 15, of which waited for: 8 -> 9; matrix products, arithmetic and copies ran while one was open for 4% -> 4% of each run, Pallas kernels for 27% -> 26%
where the time goes in v9:
time: 235 us; the launch traced here: 234 us
  Pallas kernels  108 us (46%)
  starting transfers between devices  56.1 us (24%)
  waiting for transfers between devices  54 us (23%)
  local copies, waits for them, and re-layouts  7.96 us (3%)
  other arithmetic  5.57 us (2%)
    ppermute x9, waiting for transfers between devices, neighbour(): return lax.ppermute(x, 'grp', [(g, g ^ flip) for g in range(4)])  27.7 us
    pallas_call x1, Pallas kernels, front(): call(front_body, (sds((edges, width), half), sds((blocks * negs, width),...  20.2 us
    pallas_call x1, Pallas kernels, model(): call(model_body, (sds((peers, blocks * (width // peers), width), half), s...  20 us
    pallas_call x2, Pallas kernels, home(): call(functools.partial(home_body, parts), tuple((sds((rows, width), half)...  16.3 us
    all_to_all x1, waiting for transfers between devices, on_device(): lax.all_to_all(wanted, 'dev', split_axis=0, concat_axis=0, tiled=True)  14.1 us
    ppermute x9, starting transfers between devices, neighbour(): return lax.ppermute(x, 'grp', [(g, g ^ flip) for g in range(4)])  14 us
    pallas_call x2, Pallas kernels, relation_update(): pl.pallas_call(relation_body, grid_spec=pltpu.PrefetchScalarGridSpec(num_...  11.8 us
    pallas_call x1, Pallas kernels, on_device(): call(sums_body, (sds((rows, width), full), sds((rows, width), full)), (),...  11.8 us
  transfers between devices with their start and end apart: 15, of which 9 were waited for; matrix products, arithmetic and copies ran while one was open for 4% of the time, Pallas kernels for 26%

profile of v9, /device:TPU:1, one launch (start us, length us, event | category | flops | bytes accessed | tf_op | source)
XLA Modules:
  0.0 233.7 jit_solution(11511800188886536522)
XLA Ops:
  2.3 2.2 collective-permute-start
  4.5 3.0 %shard_map.147 = (s32[1,2048]{1,0:T(1,128)}, s32[32,2,128]{2,1,0:T(2,128)}) custom-call(s32[1,2]{1,0:T(1,128)} %rel_ref.5, s32[1,2048]{1,0:T(1,128)} %bitcast.28, s32[1,2048]{1,0:T(1,128)} %row_ref.1), custom_call_target="tpu_custom_call" | custom-call | tf_op jit(solution)/shard_map/pallas_call | solution.py:637
  7.6 10.2 %all-to-all-start = ((s32[32,2,128]{2,1,0:T(2,128)}), s32[32,2,128]{2,1,0:T(2,128)S(1)}, u32[]{:S(2)}, u32[]{:S(2)}) async-start(s32[32,2,128]{2,1,0:T(2,128)} %get-tuple-element.44), calls=%async_computation | async-start | bytes 65536 | tf_op jit(solution)/shard_map/all_to_all | solution.py:642
  19.1 14.1 %all-to-all-done.asked_ref = s32[32,2,128]{2,1,0:T(2,128)S(1)} async-done(((s32[32,2,128]{2,1,0:T(2,128)}), s32[32,2,128]{2,1,0:T(2,128)S(1)}, u32[]{:S(2)}, u32[]{:S(2)}) %all-to-all-start) | async-done | bytes 32800 | tf_op jit(solution)/shard_map/all_to_all | solution.py:642
  35.2 2.4 %collective-permute-done.2.refs_3_.cross_sibling_table = bf16[2048,256]{1,0:T(8,128)(2,1)} collective-permute-done((bf16[2048,256]{1,0:T(8,128)(2,1)S(1)}, bf16[2048,256]{1,0:T(8,128)(2,1)}, u32[]{:S(2)}, u32[]{:S(2)}) %collective-permute-start.2) | collective-permute-done | bytes 1048608 | tf_op jit(solution)/shard_map/ppermute | solution.py:626
  37.6 10.4 %shard_map.148 = bf16[32,128,256]{2,1,0:T(8,128)(2,1)} custom-call(s32[4,32]{1,0:T(4,128)} %partner_ref.5, s32[1]{0:T(128)} %bitcast.1.group_ref, s32[32,2,128]{2,1,0:T(2,128)} %copy-done.7, bf16[2048,256]{1,0:T(8,128)(2,1)} %copy-done.3, bf16[2048,256]{1,0:T(8,128)(2,1)} %copy-done.6, bf16[2048,256]{1,0:T(8,128)(2,1)} %copy-done.5, ...), custom_call_target="tpu_custom_call" | custom-call | tf_op jit(solution)/shard_map/pallas_call | solution.py:648
  48.0 5.6 %all-to-all-start.1 = ((bf16[32,128,256]{2,1,0:T(8,128)(2,1)}), bf16[32,128,256]{2,1,0:T(8,128)(2,1)S(1)}, u32[]{:S(2)}, u32[]{:S(2)}) async-start(bf16[32,128,256]{2,1,0:T(8,128)(2,1)} %shard_map.148), calls=%async_computation.1 | async-start | bytes 4194304 | tf_op jit(solution)/shard_map/all_to_all | solution.py:660
  56.2 20.2 %shard_map.149 = (bf16[2048,256]{1,0:T(8,128)(2,1)}, bf16[2048,256]{1,0:T(8,128)(2,1)}, bf16[2048,256]{1,0:T(8,128)(2,1)}, bf16[2048,1024]{1,0:T(8,128)(2,1)}, f32[2048,256]{1,0:T(8,128)}, /*index=5*/f32[2048,128]{1,0:T(8,128)}) custom-call(s32[1,2]{1,0:T(1,128)} %rel_ref.5, s32[1]{0:T(128)} %bitcast.5.visit_ref.visit_to_ref, s32[1,2048]{1,0:T(1,128)} %src_ref.3, ...), custom_call_target="tpu_custom_call" | custom-call | flops 8589934592 | bytes 12582912 | tf_op jit(solution)/shard_map/pallas_call | solution.py:372
  76.4 6.8 %all-to-all-done.1 = bf16[32,128,256]{2,1,0:T(8,128)(2,1)S(1)} async-done(((bf16[32,128,256]{2,1,0:T(8,128)(2,1)}), bf16[32,128,256]{2,1,0:T(8,128)(2,1)S(1)}, u32[]{:S(2)}, u32[]{:S(2)}) %all-to-all-start.1) | async-done | bytes 2097184 | tf_op jit(solution)/shard_map/all_to_all | solution.py:660
  84.5 20.0 %shard_map.150 = (bf16[32,16,256]{2,1,0:T(8,128)(2,1)}, bf16[2048,256]{1,0:T(8,128)(2,1)}, bf16[2048,256]{1,0:T(8,128)(2,1)}, bf16[2048,256]{1,0:T(8,128)(2,1)}, bf16[2048,256]{1,0:T(8,128)(2,1)}) custom-call(s32[1,2]{1,0:T(1,128)} %rel_ref.5, s32[1,1]{1,0:T(1,128)S(6)} %copy.21.count_ref, s32[1,2048]{1,0:T(1,128)} %get-tuple-element.43.slot_ref, ...), custom_call_target="tpu_custom_call" | custom-call | tf_op jit(solution)/shard_map/pallas_call | solution.py:402
  104.5 6.7 %all-to-all-start.2 = ((bf16[32,16,256]{2,1,0:T(8,128)(2,1)}), bf16[32,16,256]{2,1,0:T(8,128)(2,1)S(1)}, u32[]{:S(2)}, u32[]{:S(2)}) async-start(bf16[32,16,256]{2,1,0:T(8,128)(2,1)} %get-tuple-element.53), calls=%async_computation.2 | async-start | bytes 524288 | tf_op jit(solution)/shard_map/all_to_all | solution.py:666
  111.2 7.6 %shard_map.151 = bf16[32,128,256]{2,1,0:T(8,128)(2,1)} custom-call(s32[1,2048]{1,0:T(1,128)} %get-tuple-element.43.slot_ref, bf16[2048,256]{1,0:T(8,128)(2,1)} %get-tuple-element.54.d_dst), custom_call_target="tpu_custom_call" | custom-call | flops 4294967296 | bytes 4194304 | tf_op jit(solution)/shard_map/pallas_call | solution.py:667
  121.5 7.5 %all-to-all-start.3 = ((bf16[32,128,256]{2,1,0:T(8,128)(2,1)}), bf16[32,128,256]{2,1,0:T(8,128)(2,1)S(1)}, u32[]{:S(2)}, u32[]{:S(2)}) async-start(bf16[32,128,256]{2,1,0:T(8,128)(2,1)} %shard_map.151), calls=%async_computation.3 | async-start | bytes 4194304 | tf_op jit(solution)/shard_map/all_to_all | solution.py:677
  137.0 11.8 %shard_map.153 = (f32[2048,256]{1,0:T(8,128)}, f32[2048,256]{1,0:T(8,128)}) custom-call(s32[1,2048]{1,0:T(1,128)} %src_ref.3, s32[2,1024]{1,0:T(2,128)} %bitcast.30, s32[2,1024]{1,0:T(2,128)} %bitcast.32, bf16[2048,256]{1,0:T(8,128)(2,1)} %get-tuple-element.60.d_src, bf16[2048,256]{1,0:T(8,128)(2,1)} %get-tuple-element.61.d_neg_src, ...), custom_call_target="tpu_custom_call" | custom-call | flops 6442450944 | bytes 7340032 | tf_op jit(solution)/shard_map/pallas_call | solution.py:679
  148.8 6.0 %collective-permute-done.4 = f32[20,8,256]{2,1,0:T(8,128)S(1)} collective-permute-done((f32[20,8,256]{2,1,0:T(8,128)S(1)}, f32[20,8,256]{2,1,0:T(8,128)S(1)}, u32[]{:S(2)}, u32[]{:S(2)}) %collective-permute-start.4) | collective-permute-done | bytes 163872 | tf_op jit(solution)/shard_map/ppermute | solution.py:626
  154.8 5.6 %collective-permute-start.5 = (bf16[20,8,256]{2,1,0:T(8,128)(2,1)S(1)}, bf16[20,8,256]{2,1,0:T(8,128)(2,1)S(1)}, u32[]{:S(2)}, u32[]{:S(2)}) collective-permute-start(bf16[20,8,256]{2,1,0:T(8,128)(2,1)S(1)} %add_convert_fusion.1), channel_id=1, source_target_pairs={{0,1},{1,0},{2,3},{3,2},{4,5},{5,4},{6,7},{7,6},{8,9},{9,8},{10,11... | collective-permute-start | bytes 245768 | tf_op jit(solution)/shard_map/ppermute | solution.py:699
  163.6 10.9 %shard_map.155 = (bf16[2048,256]{1,0:T(8,128)(2,1)}, bf16[2048,256]{1,0:T(8,128)(2,1)}, bf16[2048,256]{1,0:T(8,128)(2,1)}) custom-call(s32[4,32]{1,0:T(4,128)} %partner_ref.5, s32[1]{0:T(128)} %bitcast.1.group_ref, s32[1]{0:T(128)} %bitcast.5.visit_ref.visit_to_ref, s32[32,2,128]{2,1,0:T(2,128)} %copy-done.7, bf16[32,128,256]{2,1,0:T(8,128)(2,1)} %copy-done, ...), custom_call_target="tpu_custom_call" | custom-call | bytes 25165824 | tf_op jit(solution)/shard_map/pallas_call | solution.py:705
  178.4 6.6 %all-to-all-start.4 = ((bf16[16,2,20,8,256]{4,3,2,1,0:T(8,128)(2,1)}), bf16[16,2,20,8,256]{4,3,2,1,0:T(8,128)(2,1)S(1)}, u32[]{:S(2)}, u32[]{:S(2)}) async-start(bf16[16,2,20,8,256]{4,3,2,1,0:T(8,128)(2,1)} %broadcast_in_dim.2), calls=%async_computation.4 | async-start | bytes 5242880 | tf_op jit(solution)/shard_map/all_to_all | solution.py:717
  185.3 2.9 %add_convert_fusion = bf16[2048,256]{1,0:T(8,128)(2,1)} fusion(bf16[2048,256]{1,0:T(8,128)(2,1)} %collective-permute-done.7, bf16[2048,256]{1,0:T(8,128)(2,1)} %get-tuple-element.71), kind=kLoop, calls=%fused_computation | loop fusion | flops 2097152 | bytes 3145728 | tf_op jit(solution)/shard_map/convert_element_type | solution.py:714
  190.0 5.4 %shard_map.154.home_ref = bf16[2048,256]{1,0:T(8,128)(2,1)} custom-call(s32[4,32]{1,0:T(4,128)} %partner_ref.5, s32[1]{0:T(128)} %bitcast.1.group_ref, s32[1]{0:T(128)} %bitcast.5.visit_ref.visit_to_ref, s32[32,2,128]{2,1,0:T(2,128)} %copy-done.7, bf16[32,128,256]{2,1,0:T(8,128)(2,1)} %copy-done, f32[2048,256]{1,0:T(8,128)} %get-tuple-element.69.visit_ref), custom_call_target="tpu_custom_call" | custom-call | bytes 25165824 | tf_op jit(solution)/shard_map/pallas_call | solution.py:705
  195.4 18.3 %collective-permute-done.8.cross_ref = bf16[2048,256]{1,0:T(8,128)(2,1)} collective-permute-done((bf16[2048,256]{1,0:T(8,128)(2,1)}, bf16[2048,256]{1,0:T(8,128)(2,1)}, u32[]{:S(2)}, u32[]{:S(2)}) %collective-permute-start.8) | collective-permute-done | bytes 1048608 | tf_op jit(solution)/shard_map/ppermute | solution.py:626
  213.7 4.9 %shard_map.156 = (f32[1,2048,256]{2,1,0:T(8,128)}, f32[1,2048]{1,0:T(1,128)}) custom-call(f32[2048,256]{1,0:T(8,128)} %get-tuple-element.67.grad_ref, bf16[2048,256]{1,0:T(8,128)(2,1)} %shard_map.154.home_ref, bf16[2048,256]{1,0:T(8,128)(2,1)} %collective-permute-done.6.sibling_ref, bf16[2048,256]{1,0:T(8,128)(2,1)} %collective-permute-done.8.cross_ref, ...), custom_call_target="tpu_custom_call" | custom-call | bytes 25165824 | tf_op jit(solution)/shard_map/pallas_call | solution.py:585
  221.9 5.9 %shard_map.157 = (f32[40,256,256]{2,1,0:T(8,128)}, f32[40,256]{1,0:T(8,128)}) custom-call(s32[1]{0:T(128)} %bitcast.16.part_ref, bf16[32,20,8,256]{3,2,1,0:T(8,128)(2,1)} %bitcast.23, f32[40,256,256]{2,1,0:T(8,128)} %relation_ref.7, f32[40,256]{1,0:T(8,128)} %acc_ref.5), custom_call_target="tpu_custom_call" | custom-call | bytes 25165824 | tf_op jit(solution)/shard_map/pallas_call | solution.py:555
  227.8 5.9 %shard_map.158 = (f32[40,256,256]{2,1,0:T(8,128)}, f32[40,256]{1,0:T(8,128)}) custom-call(s32[1]{0:T(128)} %bitcast.15.part_ref, bf16[32,20,8,256]{3,2,1,0:T(8,128)(2,1)} %collective-permute-done.9.grad_ref, f32[40,256,256]{2,1,0:T(8,128)} %relation_ref.7, f32[40,256]{1,0:T(8,128)} %acc_ref.5, ...), custom_call_target="tpu_custom_call", output_to_operand_aliasing={{0}: (4, {})} | custom-call | bytes 25165824 | tf_op jit(solution)/shard_map/pallas_call | solution.py:555
  (46 shorter events, 30.8 us)
Async XLA Ops:
  2.3 35.3 %copy-start.3 = (bf16[2048,256]{1,0:T(8,128)(2,1)}, bf16[2048,256]{1,0:T(8,128)(2,1)S(1)}, u32[]{:S(2)}) copy-start(bf16[2048,256]{1,0:T(8,128)(2,1)S(1)} %convert_bitcast_fusion.refs_0_.own_table) | copy-start | bytes 3145732
  2.3 30.9 %collective-permute-start = (bf16[2048,256]{1,0:T(8,128)(2,1)S(1)}, bf16[2048,256]{1,0:T(8,128)(2,1)S(1)}, u32[]{:S(2)}, u32[]{:S(2)}) collective-permute-start(bf16[2048,256]{1,0:T(8,128)(2,1)S(1)} %convert_bitcast_fusion.refs_0_.own_table), channel_id=1, source_target_pairs={{0,64},{32,96},{64,0},{96,32},{1,65},{33,97},{65,1},{97,33},{2,66}... | collective-permute-start | bytes 3145736 | tf_op jit(solution)/shard_map/ppermute | solution.py:626
  7.6 25.7 %all-to-all-start = ((s32[32,2,128]{2,1,0:T(2,128)}), s32[32,2,128]{2,1,0:T(2,128)S(1)}, u32[]{:S(2)}, u32[]{:S(2)}) async-start(s32[32,2,128]{2,1,0:T(2,128)} %get-tuple-element.44), calls=%async_computation | async-start | bytes 65536 | tf_op jit(solution)/shard_map/all_to_all | solution.py:642
  17.8 17.4 %collective-permute-start.1 = (bf16[2048,256]{1,0:T(8,128)(2,1)S(1)}, bf16[2048,256]{1,0:T(8,128)(2,1)S(1)}, u32[]{:S(2)}, u32[]{:S(2)}) collective-permute-start(bf16[2048,256]{1,0:T(8,128)(2,1)S(1)} %convert_bitcast_fusion.refs_0_.own_table), channel_id=1, source_target_pairs={{0,32},{32,0},{64,96},{96,64},{1,33},{33,1},{65,97},{97,65},{2,34}... | collective-permute-start | bytes 3145736 | tf_op jit(solution)/shard_map/ppermute | solution.py:626
  33.2 4.4 %copy-start.7 = (s32[32,2,128]{2,1,0:T(2,128)}, s32[32,2,128]{2,1,0:T(2,128)S(1)}, u32[]{:S(2)}) copy-start(s32[32,2,128]{2,1,0:T(2,128)S(1)} %all-to-all-done.asked_ref) | copy-start | bytes 98308
  33.2 4.4 %copy-start.5 = (bf16[2048,256]{1,0:T(8,128)(2,1)}, bf16[2048,256]{1,0:T(8,128)(2,1)S(1)}, u32[]{:S(2)}) copy-start(bf16[2048,256]{1,0:T(8,128)(2,1)S(1)} %collective-permute-done.refs_2_.cross_table) | copy-start | bytes 3145732
  33.2 4.3 %collective-permute-start.2 = (bf16[2048,256]{1,0:T(8,128)(2,1)S(1)}, bf16[2048,256]{1,0:T(8,128)(2,1)}, u32[]{:S(2)}, u32[]{:S(2)}) collective-permute-start(bf16[2048,256]{1,0:T(8,128)(2,1)S(1)} %collective-permute-done.refs_2_.cross_table), channel_id=1, source_target_pairs={{0,32},{32,0},{64,96},{96,64},{1,33},{33,1},{65,97},{97,65},{2,34}... | collective-permute-start | bytes 3145736 | tf_op jit(solution)/shard_map/ppermute | solution.py:626
  35.2 2.4 %copy-start.6 = (bf16[2048,256]{1,0:T(8,128)(2,1)}, bf16[2048,256]{1,0:T(8,128)(2,1)S(1)}, u32[]{:S(2)}) copy-start(bf16[2048,256]{1,0:T(8,128)(2,1)S(1)} %collective-permute-done.1.refs_1_.sibling_table) | copy-start | bytes 3145732
  48.0 35.2 %all-to-all-start.1 = ((bf16[32,128,256]{2,1,0:T(8,128)(2,1)}), bf16[32,128,256]{2,1,0:T(8,128)(2,1)S(1)}, u32[]{:S(2)}, u32[]{:S(2)}) async-start(bf16[32,128,256]{2,1,0:T(8,128)(2,1)} %shard_map.148), calls=%async_computation.1 | async-start | bytes 4194304 | tf_op jit(solution)/shard_map/all_to_all | solution.py:660
  83.2 1.3 copy-start.2
  104.5 16.3 %all-to-all-start.2 = ((bf16[32,16,256]{2,1,0:T(8,128)(2,1)}), bf16[32,16,256]{2,1,0:T(8,128)(2,1)S(1)}, u32[]{:S(2)}, u32[]{:S(2)}) async-start(bf16[32,16,256]{2,1,0:T(8,128)(2,1)} %get-tuple-element.53), calls=%async_computation.2 | async-start | bytes 524288 | tf_op jit(solution)/shard_map/all_to_all | solution.py:666
  120.8 0.7 copy-start.4
  120.8 8.2 %copy-start.8 = (s32[32,2,128]{2,1,0:T(2,128)S(1)}, s32[32,2,128]{2,1,0:T(2,128)}, u32[]{:S(2)}) copy-start(s32[32,2,128]{2,1,0:T(2,128)} %copy-done.7) | copy-start | bytes 98308
  121.5 40.7 %all-to-all-start.3 = ((bf16[32,128,256]{2,1,0:T(8,128)(2,1)}), bf16[32,128,256]{2,1,0:T(8,128)(2,1)S(1)}, u32[]{:S(2)}, u32[]{:S(2)}) async-start(bf16[32,128,256]{2,1,0:T(8,128)(2,1)} %shard_map.151), calls=%async_computation.3 | async-start | bytes 4194304 | tf_op jit(solution)/shard_map/all_to_all | solution.py:677
  132.6 2.5 %collective-permute-start.3 = (f32[20,8,256]{2,1,0:T(8,128)S(1)}, f32[20,8,256]{2,1,0:T(8,128)S(1)}, u32[]{:S(2)}, u32[]{:S(2)}) collective-permute-start(f32[20,8,256]{2,1,0:T(8,128)S(1)} %dynamic-slice_bitcast_fusion), channel_id=1, source_target_pairs={{0,32},{32,0},{64,96},{96,64},{1,33},{33,1},{65,97},{97,65},{2,34}... | collective-permute-start | bytes 491528 | tf_op jit(solution)/shard_map/ppermute | solution.py:626
  136.0 18.7 %collective-permute-start.4 = (f32[20,8,256]{2,1,0:T(8,128)S(1)}, f32[20,8,256]{2,1,0:T(8,128)S(1)}, u32[]{:S(2)}, u32[]{:S(2)}) collective-permute-start(f32[20,8,256]{2,1,0:T(8,128)S(1)} %bitcast_add_fusion), channel_id=1, source_target_pairs={{0,64},{32,96},{64,0},{96,32},{1,65},{33,97},{65,1},{97,33},{2,66}... | collective-permute-start | bytes 491528 | tf_op jit(solution)/shard_map/ppermute | solution.py:626
  154.8 7.4 %collective-permute-start.5 = (bf16[20,8,256]{2,1,0:T(8,128)(2,1)S(1)}, bf16[20,8,256]{2,1,0:T(8,128)(2,1)S(1)}, u32[]{:S(2)}, u32[]{:S(2)}) collective-permute-start(bf16[20,8,256]{2,1,0:T(8,128)(2,1)S(1)} %add_convert_fusion.1), channel_id=1, source_target_pairs={{0,1},{1,0},{2,3},{3,2},{4,5},{5,4},{6,7},{7,6},{8,9},{9,8},{10,11... | collective-permute-start | bytes 245768 | tf_op jit(solution)/shard_map/ppermute | solution.py:699
  162.2 1.3 copy-start
  174.5 10.9 %collective-permute-start.7 = (bf16[2048,256]{1,0:T(8,128)(2,1)}, bf16[2048,256]{1,0:T(8,128)(2,1)}, u32[]{:S(2)}, u32[]{:S(2)}) collective-permute-start(bf16[2048,256]{1,0:T(8,128)(2,1)} %get-tuple-element.72), channel_id=1, source_target_pairs={{0,32},{32,0},{64,96},{96,64},{1,33},{33,1},{65,97},{97,65},{2,34}... | collective-permute-start | bytes 3145736 | tf_op jit(solution)/shard_map/ppermute | solution.py:626
  178.4 41.6 %all-to-all-start.4 = ((bf16[16,2,20,8,256]{4,3,2,1,0:T(8,128)(2,1)}), bf16[16,2,20,8,256]{4,3,2,1,0:T(8,128)(2,1)S(1)}, u32[]{:S(2)}, u32[]{:S(2)}) async-start(bf16[16,2,20,8,256]{4,3,2,1,0:T(8,128)(2,1)} %broadcast_in_dim.2), calls=%async_computation.4 | async-start | bytes 5242880 | tf_op jit(solution)/shard_map/all_to_all | solution.py:717
  185.0 10.4 %collective-permute-start.6 = (bf16[2048,256]{1,0:T(8,128)(2,1)}, bf16[2048,256]{1,0:T(8,128)(2,1)}, u32[]{:S(2)}, u32[]{:S(2)}) collective-permute-start(bf16[2048,256]{1,0:T(8,128)(2,1)} %get-tuple-element.70), channel_id=1, source_target_pairs={{0,32},{32,0},{64,96},{96,64},{1,33},{33,1},{65,97},{97,65},{2,34}... | collective-permute-start | bytes 3145736 | tf_op jit(solution)/shard_map/ppermute | solution.py:626
  188.2 25.5 %collective-permute-start.8 = (bf16[2048,256]{1,0:T(8,128)(2,1)}, bf16[2048,256]{1,0:T(8,128)(2,1)}, u32[]{:S(2)}, u32[]{:S(2)}) collective-permute-start(bf16[2048,256]{1,0:T(8,128)(2,1)} %add_convert_fusion), channel_id=1, source_target_pairs={{0,64},{32,96},{64,0},{96,32},{1,65},{33,97},{65,1},{97,33},{2,66}... | collective-permute-start | bytes 3145736 | tf_op jit(solution)/shard_map/ppermute | solution.py:626
  220.0 1.9 copy-start.1
  220.0 7.8 %collective-permute-start.9 = (bf16[32,20,8,256]{3,2,1,0:T(8,128)(2,1)S(1)}, bf16[32,20,8,256]{3,2,1,0:T(8,128)(2,1)}, u32[]{:S(2)}, u32[]{:S(2)}) collective-permute-start(bf16[32,20,8,256]{3,2,1,0:T(8,128)(2,1)S(1)} %bitcast.22), channel_id=1, source_target_pairs={{0,32},{32,0},{64,96},{96,64},{1,33},{33,1},{65,97},{97,65},{2,34}... | collective-permute-start | bytes 7864328 | tf_op jit(solution)/shard_map/ppermute | solution.py:626
